TPU v7x, 128 devices: a whole 4x4x4 slice. The times are simulated.
128 devices in a mesh: samp: 16 (over z_hi, x, core), blk: 8 (over z_lo, y).
Axes of the slice: x: 4, y: 4, z: 4 (z_hi: 2, z_lo: 2; z = z_hi * 2 + z_lo), core: 2. Of those that a mesh axis runs over, the one named last changes fastest.
Arguments:
- genotypes: int32 [32768, 12288], P('samp', 'blk'), may hold values from 0 to 2
- phenotype: float32 [32768], P('samp'), may hold values from -15 to 15
- fold_ids: int32 [32768], P('samp'), may hold values from 0 to 4, as said below
Outputs:
- coeff_all: float32 [12288, 400], P('blk')
- fold_scores: float32 [2, 400], replicated
Inputs may be any that keep to these rules, and one draw needn't show every extreme that they name: `fold_ids`: every fold holds 6553 or 6554 people.
All inputs are finite; a program needn't handle non-finite values.
Results may differ from a plain program's by a relative error of at most 0.0003.
Values sent between devices are 32-bit elements; how exact they have to be, the bound alone decides.
No kernel may reach another device: no remote copies, remote signals or barrier semaphores. Data moves between devices by JAX's collectives and lax.ppermute only.
A program may use at most 128 MiB of HBM per device.

v0:
```python
import math

import jax
import jax.numpy as jnp
from jax import lax
from jax.sharding import PartitionSpec as P

FOLDS = 5
LAMBDAS = 20
SWEEPS = 3
GRID = 400


step_size = 0.6
epsilon = 1e-05
lambda_base = 0.1
lambda_ratio = 1.2
shrink_unit = 0.2
highest = lax.Precision.HIGHEST


def grid_tables():
    column = jnp.arange(GRID)
    fold_of = column % FOLDS
    levels = column // FOLDS % LAMBDAS
    penalty = lambda_base * jnp.exp(levels.astype(jnp.float32) * math.log(lambda_ratio))
    shrink = shrink_unit * (column // (FOLDS * LAMBDAS) + 1).astype(jnp.float32)
    return (fold_of, penalty, shrink)


def soft_threshold(values, cutoff):
    return values - jnp.clip(values, -cutoff, cutoff)


def local(genotypes, phenotype, fold_ids):
    num_rows, block_width = genotypes.shape
    sample_count = num_rows * lax.axis_size("samp")
    snp_total = block_width * lax.axis_size("blk")
    dosage_bf = genotypes.astype(jnp.bfloat16)
    onehot = fold_ids[:, None] == jnp.arange(FOLDS)[None, :]
    pheno_split = jnp.where(onehot, phenotype[:, None], 0.0)
    local_sum = jnp.sum(genotypes, axis=0).astype(jnp.float32)
    local_sq = jnp.sum(genotypes * genotypes, axis=0).astype(jnp.float32)
    local_geno_pheno = jnp.dot(pheno_split.T, genotypes.astype(jnp.float32), precision=highest)
    local_pheno_sum = jnp.sum(pheno_split, axis=0)
    local_count = jnp.sum(onehot.astype(jnp.int32), axis=0).astype(jnp.float32)
    fold_of, penalty, shrink = grid_tables()
    column_fold = fold_of[None, :] == jnp.arange(FOLDS)[:, None]
    gram_local = jnp.dot(dosage_bf.T, dosage_bf, preferred_element_type=jnp.float32)
    gram_sum, geno_sum, geno_sq, geno_pheno, fold_pheno_sum, fold_count = lax.psum(
        (gram_local, local_sum, local_sq, local_geno_pheno, local_pheno_sum, local_count), "samp"
    )
    snp_mean = geno_sum / sample_count
    scales = jnp.sqrt(geno_sq / sample_count - snp_mean * snp_mean + epsilon)
    train_geno = jnp.sum(geno_pheno, axis=0)[None, :] - geno_pheno
    train_pheno = jnp.sum(fold_pheno_sum) - fold_pheno_sum
    zscore = (train_geno - train_pheno[:, None] * snp_mean[None, :]) / (
        scales[None, :] * jnp.sqrt(sample_count - fold_count)[:, None]
    )
    snp_mean, scales, zscore = (snp_mean, scales, zscore)
    ld_block = (gram_sum / sample_count - snp_mean[:, None] * snp_mean[None, :]) / (
        scales[:, None] * scales[None, :]
    )
    col_share = GRID // lax.axis_size("samp")
    first_col = lax.axis_index("samp") * col_share
    target = lax.dynamic_slice_in_dim(
        jnp.sum(jnp.where(column_fold[None, :, :], zscore.T[:, :, None], 0.0), axis=1),
        first_col,
        col_share,
        1,
    )
    penalty_mine = lax.dynamic_slice_in_dim(penalty, first_col, col_share, 0)
    shrink_mine = lax.dynamic_slice_in_dim(shrink, first_col, col_share, 0)
    coeffs = soft_threshold(step_size * target, step_size * penalty_mine)
    for sweep_idx in range(SWEEPS - 1):
        gradient = (
            (1.0 - shrink_mine) * jnp.dot(ld_block, coeffs, precision=highest)
            + shrink_mine * coeffs
            - target
        )
        coeffs = soft_threshold(coeffs - step_size * gradient, step_size * penalty_mine)
    coeff_all = lax.all_gather(coeffs, "samp", axis=1, tiled=True)
    weighted = (coeff_all / scales[:, None]).astype(jnp.bfloat16)
    offset = jnp.dot(snp_mean[None, :], weighted.astype(jnp.float32), precision=highest)
    partial_value = jnp.dot(dosage_bf, weighted, preferred_element_type=jnp.float32) - offset
    root_snps = math.sqrt(snp_total)
    predicted = lax.psum(partial_value, "blk") / root_snps
    chosen = fold_ids[:, None] == fold_of[None, :]
    numerator = jnp.sum(jnp.where(chosen, predicted * phenotype[:, None], 0.0), axis=0)
    denominator = jnp.sum(jnp.where(chosen, predicted * predicted, 0.0), axis=0)
    numerator, denominator = lax.psum((numerator, denominator), "samp")
    counts = jnp.sum(jnp.where(column_fold, fold_count[:, None], 0.0), axis=0)
    fold_scores = jnp.stack([numerator / counts, denominator / counts])
    return (coeff_all, fold_scores)


def solution(mesh):
    return jax.shard_map(
        local,
        mesh=mesh,
        in_specs=(P("samp", "blk"), P("samp"), P("samp")),
        out_specs=(P("blk", None), P()),
        check_vma=False,
    )
```

profile of v0, /device:TPU:0, one launch (start us, length us, event | category | flops | bytes accessed | tf_op | source)
XLA Modules:
  0.0 422.9 jit_solution(10892874406251603030)
XLA Ops:
  7.2 0.0 all-reduce.5.cloned.1.call-start
  7.2 19.0 %fusion.6 = f32[1536,1536]{1,0:T(8,128)} fusion(s32[2048,1536]{1,0:T(8,128)} %param.3), kind=kOutput, calls=%fused_computation.12 | convolution fusion | flops 9666822144 | bytes 22020096 | tf_op jit(solution)/shard_map/dot_general | solution.py:49
  26.2 0.0 all-reduce.5.cloned.1.call-update
  26.2 0.2 all-gather.3.cloned.1.call-start
  26.5 6.1 %fusion.52 = (s32[1536]{0:T(1024)S(1)}, s32[1536]{0:T(1024)S(1)}) fusion(s32[2048,1536]{1,0:T(8,128)} %param.3), kind=kLoop, calls=%fused_computation.83 | loop fusion | flops 9434112 | bytes 12595200 | tf_op jit(solution)/shard_map/reduce_sum | solution.py:42
  32.6 0.1 convert_reduce_fusion
  32.7 0.1 select_reduce_fusion.1
  32.9 1.8 copy-done
  34.6 6.2 %fusion = f32[5,1536]{1,0:T(8,128)S(1)} fusion(s32[2048,1536]{1,0:T(8,128)S(1)} %copy-done, f32[2048]{0:T(1024)S(1)} %copy-done.3, s32[2048]{0:T(1024)S(1)} %copy-done.2), kind=kOutput, calls=%fused_computation.1 | convolution fusion | flops 191909888 | bytes 12630016 | tf_op jit(solution)/shard_map/dot_general | solution.py:44
  40.9 71.7 %all-reduce.1 = (f32[1536]{0:T(1024)S(1)}, f32[1536]{0:T(1024)S(1)}, f32[5,1536]{1,0:T(8,128)S(1)}, f32[5]{0:T(128)S(1)}, f32[5]{0:T(128)S(1)}) all-reduce(f32[1536]{0:T(1024)S(1)} %convert_element_type.30, f32[1536]{0:T(1024)S(1)} %convert_element_type.29, f32[5,1536]{1,0:T(8,128)S(1)} %fusion, ...), channel_id=1, replica_groups=mesh['samp'=16,'blk'=8] {'samp'}, use_global_device_ids=true, to_apply=%region_8.9 | all-reduce | flops 10762 | bytes 86096 | tf_op jit(solution)/shard_map/psum | solution.py:50
  112.6 0.6 reduce_sum.92
  113.3 0.1 broadcast_subtract_fusion
  113.4 0.7 subtract_sqrt_fusion
  114.0 0.1 divide_bitcast_fusion
  114.1 0.9 select_reduce_fusion
  115.1 81.5 %all-reduce.5.cloned.1.call-done = f32[1536,1536]{1,0:T(8,128)} async-done(((f32[1536,1536]{1,0:T(8,128)}), f32[1536,1536]{1,0:T(8,128)}) %all-reduce.5.cloned.1.call-update) | async-done | bytes 9437200 | tf_op jit(solution)/shard_map/psum | solution.py:50
  196.6 5.4 %multiply_divide_fusion = f32[1536,1536]{1,0:T(8,128)S(1)} fusion(f32[1536,1536]{1,0:T(8,128)} %all-reduce.5.cloned.1.call-done, f32[1536]{0:T(1024)S(1)} %get-tuple-element.18, f32[1536]{0:T(1024)S(1)} %get-tuple-element.17), kind=kLoop, calls=%fused_computation.4 | loop fusion | flops 11796480 | bytes 18886656 | tf_op jit(solution)/shard_map/div | solution.py:61
  202.0 8.8 %fusion.15 = f32[1536,25]{0,1:T(8,128)S(1)} fusion(f32[1536,1536]{1,0:T(8,128)S(1)} %multiply_divide_fusion, f32[1536,400]{0,1:T(8,128)S(1)} %select_reduce_fusion, s32[]{:T(128)S(6)} %select_n.54, f32[25]{0:T(128)S(1)} %get-tuple-element.16, f32[25]{0:T(128)S(1)} %get-tuple-element.15, f32[25]{0:T(128)S(1)} %get-tuple-element.23, f32[25]{0:T(128)S(1)} %get-tuple-element.24), kind=kOutput, calls=%fused_computation.22 | convolution fusion | flops 708326400 | bytes 9988096 | tf_op jit(solution)/shard_map/dot_general | solution.py:77
  210.9 9.8 %subtract_bitcast_fusion.1 = f32[1,25,1536]{2,1,0:T(8,128)} fusion(f32[1536,1536]{1,0:T(8,128)S(1)} %multiply_divide_fusion, f32[1536,25]{0,1:T(8,128)S(1)} %fusion.15, f32[1536,400]{0,1:T(8,128)S(1)} %select_reduce_fusion, s32[]{:T(128)S(6)} %select_n.54, f32[25]{0:T(128)S(1)} %get-tuple-element.16, f32[25]{0:T(128)S(1)} %get-tuple-element.15, ...), kind=kOutput, calls=%fused_computation.25 | convolution fusion | flops 708364800 | bytes 10183684 | tf_op jit(solution)/shard_map/dot_general | solution.py:77
  220.7 0.0 all-gather.3.cloned.1.call-update
  220.7 0.0 all-reduce.7.cloned.1.call-start
  220.8 52.5 %all-gather.3.cloned.1.call-done = f32[16,25,1536]{2,1,0:T(8,128)} async-done(((f32[1,25,1536]{2,1,0:T(8,128)}), f32[16,25,1536]{2,1,0:T(8,128)}) %all-gather.3.cloned.1.call-update) | async-done | bytes 2457616 | tf_op jit(solution)/shard_map/all_gather | solution.py:82
  273.3 2.1 reshape.53
  275.4 0.2 divide_convert_fusion
  275.7 1.0 fusion.55
  276.7 9.1 %subtract_bitcast_fusion = f32[2048,400]{0,1:T(8,128)} fusion(bf16[1536,400]{0,1:T(8,128)(2,1)S(1)} %divide_convert_fusion, s32[2048,1536]{1,0:T(8,128)} %param.3, f32[400]{0:T(512)S(1)} %bitcast.21), kind=kOutput, calls=%fused_computation.9 | convolution fusion | flops 2520547328 | bytes 17090112 | tf_op jit(solution)/shard_map/dot_general | solution.py:85
  285.8 0.0 all-reduce.7.cloned.1.call-update
  285.8 0.1 select_reduce_fusion.2
  285.9 90.3 %all-reduce.7.cloned.1.call-done = f32[2048,400]{0,1:T(8,128)} async-done(((f32[2048,400]{0,1:T(8,128)}), f32[2048,400]{0,1:T(8,128)}) %all-reduce.7.cloned.1.call-update) | async-done | bytes 3276816 | tf_op jit(solution)/shard_map/psum | solution.py:87
  376.1 3.0 fusion.2
  379.1 36.6 %all-reduce = (f32[400]{0:T(512)S(1)}, f32[400]{0:T(512)S(1)}) all-reduce(f32[400]{0:T(512)S(1)} %get-tuple-element.5, f32[400]{0:T(512)S(1)} %get-tuple-element.4), channel_id=1, replica_groups=mesh['samp'=16,'blk'=8] {'samp'}, use_global_device_ids=true, to_apply=%region_18.19 | all-reduce | flops 800 | bytes 6400 | tf_op jit(solution)/shard_map/psum | solution.py:91
  415.8 0.6 pad_maximum_fusion
  (19 shorter events, 0.1 us)
Async XLA Ops:
  7.2 189.4 %all-reduce.5.cloned.1.call-start = ((), (), s32[]{:S(2)}) async-start(), calls=%async_computation | async-start | bytes 18874368 | tf_op jit(solution)/shard_map/psum | solution.py:50
  26.2 247.1 %all-gather.3.cloned.1.call-start = ((), (), s32[]{:S(2)}) async-start(), calls=%async_computation.2 | async-start | bytes 3342336 | tf_op jit(solution)/shard_map/all_gather | solution.py:82
  26.5 6.1 %copy-start.2 = (s32[2048]{0:T(1024)S(1)}, s32[2048]{0:T(1024)}, u32[]{:S(2)}) copy-start(s32[2048]{0:T(1024)} %param.5) | copy-start | bytes 24580
  26.5 6.3 %copy-start.3 = (f32[2048]{0:T(1024)S(1)}, f32[2048]{0:T(1024)}, u32[]{:S(2)}) copy-start(f32[2048]{0:T(1024)} %param.4) | copy-start | bytes 24580
  26.5 8.2 %copy-start = (s32[2048,1536]{1,0:T(8,128)S(1)}, s32[2048,1536]{1,0:T(8,128)}, u32[]{:S(2)}) copy-start(s32[2048,1536]{1,0:T(8,128)} %param.3) | copy-start | bytes 37748740
  220.7 155.4 %all-reduce.7.cloned.1.call-start = ((), (), s32[]{:S(2)}) async-start(), calls=%async_computation.1 | async-start | bytes 6553600 | tf_op jit(solution)/shard_map/psum | solution.py:87
  275.4 10.4 %copy-start.1 = (f32[400,1536]{1,0:T(8,128)}, f32[400,1536]{1,0:T(8,128)S(1)}, u32[]{:S(2)}) copy-start(f32[400,1536]{1,0:T(8,128)S(1)} %reshape.53) | copy-start | bytes 7372804
Sparse Core Ops, SparseCore 0:
  26.3 170.1 all-reduce.4
  220.8 52.4 all-gather.2
  285.9 90.1 all-reduce.6
where the time goes:
time: 423 us
  waiting for transfers between devices  224 us (53%)
  blocking collectives  108 us (26%)
  matrix products  54 us (13%)
  other arithmetic  18.2 us (4%)
  between operations  13.9 us (3%)
    psum x1, waiting for transfers between devices, local(): predicted = lax.psum(partial_value, 'blk') / root_snps  90.3 us
    psum x1, waiting for transfers between devices, local(): lax.psum((gram_local, local_sum, local_sq, local_geno_pheno, local_pheno_...  81.5 us
    psum x1, blocking collectives, local(): lax.psum((gram_local, local_sum, local_sq, local_geno_pheno, local_pheno_...  71.7 us
    all_gather x1, waiting for transfers between devices, local(): coeff_all = lax.all_gather(coeffs, 'samp', axis=1, tiled=True)  52.5 us
    psum x1, blocking collectives, local(): numerator, denominator = lax.psum((numerator, denominator), 'samp')  36.6 us
    dot_general x1, matrix products, local(): jnp.dot(dosage_bf.T, dosage_bf, preferred_element_type=jnp.float32)  19 us
    dot_general x2, matrix products, local(): jnp.dot(ld_block, coeffs, precision=highest)  18.7 us
    dot_general x1, matrix products, local(): jnp.dot(dosage_bf, weighted, preferred_element_type=jnp.float32) - offset  9.06 us
  transfers between devices with their start and end apart: 3, of which 3 were waited for; matrix products, arithmetic and copies ran while one was open for 4% of the time, Pallas kernels for 0%

commit v1 on v0

v1 whole, which is shorter than its diff:
```python
import math

import jax
import jax.numpy as jnp
from jax import lax
from jax.sharding import PartitionSpec as P

FOLDS = 5
LAMBDAS = 20
GRID = 400
BASE = FOLDS * LAMBDAS
SHRINKS = GRID // BASE

step_size = 0.6
epsilon = 1e-05
lambda_base = 0.1
lambda_ratio = 1.2
shrink_unit = 0.2


def soft_threshold(values, cutoff):
    return values - jnp.clip(values, -cutoff, cutoff)


def swap(values, axis, bit):
    size = lax.axis_size(axis)
    return lax.ppermute(values, axis, [(i, i ^ bit) for i in range(size)])


def rounded(values):
    return lax.reduce_precision(values, 8, 7)


def split2(values):
    high = rounded(values)
    return high.astype(jnp.bfloat16), (values - high).astype(jnp.bfloat16)


def split3(values):
    high = rounded(values)
    return (high.astype(jnp.bfloat16),) + split2(values - high)


def order4(parts, place):
    low, high = (place & 1) == 1, (place & 2) == 2
    a, b, c, d = parts
    a, b, c, d = (jnp.where(low, b, a), jnp.where(low, a, b), jnp.where(low, d, c), jnp.where(low, c, d))
    return jnp.where(high, c, a), jnp.where(high, d, b), jnp.where(high, a, c), jnp.where(high, b, d)


def reduce_scatter(values, core, place):
    half = values.shape[0] // 2
    width = values.shape[1] // 4
    kept = lax.dynamic_slice_in_dim(values, core * half, half, 0)
    sent = lax.dynamic_slice_in_dim(values, (1 - core) * half, half, 0)
    kept = kept + swap(sent, "samp", 1)
    kept = kept + swap(kept, "samp", 8)
    got = [
        swap(lax.dynamic_slice_in_dim(kept, (place ^ k) * width, width, 1), "samp", 2 * k) for k in (1, 2, 3)
    ]
    mine = lax.dynamic_slice_in_dim(kept, place * width, width, 1)
    return mine + got[0] + got[1] + got[2]


def gather(piece, core, place):
    parts = [piece] + [swap(piece, "samp", 2 * k) for k in (1, 2, 3)]
    half = jnp.concatenate(order4(parts, place), axis=1)
    other = swap(half, "samp", 1)
    first = core == 0
    return jnp.concatenate([jnp.where(first, half, other), jnp.where(first, other, half)], axis=0)


def all_sum(values, bits):
    for axis, group in bits:
        got = [swap(values, axis, bit) for bit in group]
        values = values + got[0] if len(got) == 1 else (values + got[0]) + (got[1] + got[2])
    return values


SAMP_BITS = (("samp", (1,)), ("samp", (8,)), ("samp", (2, 4, 6)))


def by_fold(table, rows):
    fold_of = lax.broadcasted_iota(jnp.int32, (rows, 1), 0) % FOLDS
    out = jnp.zeros((rows, table.shape[1]), table.dtype)
    for fold in range(FOLDS):
        out = jnp.where(fold_of == fold, table[fold : fold + 1], out)
    return out


def people_times(coeff, dosage, offset):
    rows = coeff.shape[0]
    both = jnp.concatenate(split2(coeff), axis=0)
    out = lax.dot_general(both, dosage, (((1,), (1,)), ((), ())), preferred_element_type=jnp.float32)
    return out[:rows] + out[rows:] - offset


def snps_times(scores, dosage):
    rows = scores.shape[0]
    both = jnp.concatenate(split2(scores), axis=0)
    out = lax.dot_general(both, dosage, (((1,), (0,)), ((), ())), preferred_element_type=jnp.float32)
    return out[:rows] + out[rows:]


def local(genotypes, phenotype, fold_ids):
    num_rows, block_width = genotypes.shape
    sample_count = num_rows * lax.axis_size("samp")
    snp_total = block_width * lax.axis_size("blk")
    samp = lax.axis_index("samp")
    core, place = samp % 2, samp // 2 % 4
    dosage = genotypes.astype(jnp.bfloat16)

    onehot = fold_ids[None, :] == jnp.arange(FOLDS)[:, None]
    pheno_split = jnp.where(onehot, phenotype[None, :], 0.0)
    left = jnp.concatenate(split3(pheno_split), axis=0)
    parts = lax.dot_general(left, dosage, (((1,), (0,)), ((), ())), preferred_element_type=jnp.float32)
    geno_pheno = parts[:5] + parts[5:10] + parts[10:15]
    geno_sum = jnp.sum(genotypes, axis=0).astype(jnp.float32)
    geno_sq = jnp.sum(genotypes * genotypes, axis=0).astype(jnp.float32)
    counts = jnp.sum(onehot.astype(jnp.float32), axis=1)
    fold_sum = jnp.sum(pheno_split, axis=1)
    extra = jnp.concatenate([counts, fold_sum, jnp.zeros((block_width - 10,), jnp.float32)])
    stats = jnp.concatenate([geno_pheno, geno_sum[None], geno_sq[None], extra[None]], axis=0)
    stats = all_sum(stats, SAMP_BITS)
    geno_pheno = stats[:5]
    fold_count = stats[7, :5][:, None]
    fold_pheno_sum = stats[7, 5:10][:, None]
    snp_mean = stats[5:6] / sample_count
    scales = jnp.sqrt(stats[6:7] / sample_count - snp_mean * snp_mean + epsilon)
    train_geno = jnp.sum(geno_pheno, axis=0, keepdims=True) - geno_pheno
    train_pheno = jnp.sum(fold_pheno_sum) - fold_pheno_sum
    zscore = (train_geno - train_pheno * snp_mean) / (scales * jnp.sqrt(sample_count - fold_count))
    inverse = 1.0 / scales

    level = (lax.broadcasted_iota(jnp.int32, (BASE, 1), 0) // FOLDS).astype(jnp.float32)
    cutoff = step_size * (lambda_base * jnp.exp(level * math.log(lambda_ratio)))
    target = by_fold(zscore, BASE)
    coeff0 = soft_threshold(step_size * target, cutoff)

    def centred(coeff):
        scaled = coeff * inverse
        offset = jnp.sum(scaled * snp_mean, axis=1, keepdims=True)
        return scaled, offset

    scaled, offset = centred(coeff0)
    scores = people_times(scaled, dosage, offset)
    product = reduce_scatter(snps_times(scores, dosage), core, place)
    product = gather(product, core, place) * (inverse / sample_count)

    def sweep(coeff, product, target, shrink, cutoff):
        gradient = (1.0 - shrink) * product + shrink * coeff - target
        return soft_threshold(coeff - step_size * gradient, cutoff)

    shrinks = [shrink_unit * (group + 1) for group in range(SHRINKS)]
    coeff1 = jnp.concatenate([sweep(coeff0, product, target, shrink, cutoff) for shrink in shrinks], axis=0)
    scaled, offset = centred(coeff1)
    scores = people_times(scaled, dosage, offset)
    piece = reduce_scatter(snps_times(scores, dosage), core, place)

    half, width = GRID // 2, block_width // 4
    here = lambda a: lax.dynamic_slice_in_dim(a, place * width, width, 1)
    column = core * half + lax.broadcasted_iota(jnp.int32, (half, 1), 0)
    shrink = shrink_unit * (column // BASE + 1).astype(jnp.float32)
    level = (column // FOLDS % LAMBDAS).astype(jnp.float32)
    cutoff2 = step_size * (lambda_base * jnp.exp(level * math.log(lambda_ratio)))
    coeff_piece = lax.dynamic_slice(coeff1, (core * half, place * width), (half, width))
    target_piece = by_fold(here(zscore), half)
    piece = sweep(coeff_piece, piece * (here(inverse) / sample_count), target_piece, shrink, cutoff2)
    coeff_all = gather(piece, core, place)

    wide = rounded(coeff_all / scales)
    weighted = wide.astype(jnp.bfloat16)
    offset = jnp.sum(wide * snp_mean, axis=1)
    centred_pheno = geno_pheno - snp_mean * fold_pheno_sum
    numerator = jnp.sum(wide * by_fold(centred_pheno, GRID), axis=1)
    grouped = weighted.reshape(GRID // FOLDS, FOLDS, block_width).transpose(1, 0, 2).reshape(GRID, block_width)
    offset = offset.reshape(GRID // FOLDS, FOLDS).T.reshape(GRID, 1)
    predicted = lax.dot_general(grouped, dosage, (((1,), (1,)), ((), ())), preferred_element_type=jnp.float32) - offset
    predicted = predicted.reshape(FOLDS, GRID // FOLDS, num_rows)
    predicted = jnp.sum(jnp.where(onehot[:, None, :], predicted, 0.0), axis=0)

    blk = lax.axis_index("blk")
    along = blk % 4
    width = num_rows // 4
    mine = lax.dynamic_slice_in_dim(predicted, along * width, width, 1)
    for k in (1, 2, 3):
        mine = mine + swap(lax.dynamic_slice_in_dim(predicted, (along ^ k) * width, width, 1), "blk", k)
    mine = mine + swap(mine, "blk", 4)
    numerator = numerator + swap(numerator, "blk", 4)
    folds_here = lax.dynamic_slice_in_dim(fold_ids, along * width, width, 0)
    square = mine * mine
    denominator = jnp.stack(
        [jnp.sum(jnp.where((folds_here == fold)[None, :], square, 0.0), axis=1) for fold in range(FOLDS)], axis=1
    ).reshape(GRID)
    sums = jnp.stack([numerator / lax.axis_size("samp"), denominator])
    sums = all_sum(sums, SAMP_BITS + (("blk", (1, 2, 3)),))
    count_of = by_fold(fold_count, GRID)[:, 0]
    fold_scores = jnp.stack([sums[0] / math.sqrt(snp_total), sums[1] / snp_total]) / count_of[None, :]
    return (coeff_all.T, fold_scores)


def solution(mesh):
    return jax.shard_map(
        local,
        mesh=mesh,
        in_specs=(P("samp", "blk"), P("samp"), P("samp")),
        out_specs=(P("blk", None), P()),
        check_vma=False,
    )
```

time: 423 us -> 225 us (0.53)
  waiting for transfers between devices: 224 us -> 102 us
  blocking collectives: 108 us -> 0 us
  starting transfers between devices: 0.3 us -> 52 us
  matrix products: 54 us -> 20.8 us
  other arithmetic: 18.2 us -> 36.5 us
  between operations: 13.9 us -> 1.2 us
  local copies, waits for them, and re-layouts: 3.91 us -> 11.4 us
    psum x2 -> x0, waiting for transfers between devices: 172 us -> none  [the longest x1 90.3 us: local(): predicted = lax.psum(partial_value, 'blk') / root_snps]
    psum x2 -> x0, blocking collectives: 108 us -> none  [the longest x1 71.7 us: local(): lax.psum((gram_local, local_sum, local_sq, local_geno_pheno, local_pheno_...]
    ppermute x0 -> x36, waiting for transfers between devices: none -> 102 us  [swap(): return lax.ppermute(values, axis, [(i, i ^ bit) for i in range(size)])]
    all_gather x1 -> x0, waiting for transfers between devices: 52.5 us -> none  [local(): coeff_all = lax.all_gather(coeffs, 'samp', axis=1, tiled=True)]
    ppermute x0 -> x36, starting transfers between devices: none -> 52 us  [swap(): return lax.ppermute(values, axis, [(i, i ^ bit) for i in range(size)])]
    dot_general x6, matrix products: 54 us -> 20.8 us  [the longest x2 10.4 us: people_times(): lax.dot_general(both, dosage, (((1,), (1,)), ((), ())), preferred_element...]
    add x0 -> x16, other arithmetic: none -> 5.42 us  [the longest x2 2.94 us: reduce_scatter(): kept = kept + swap(sent, 'samp', 1)]
    div x3 -> x5, other arithmetic: 5.46 us -> 0.72 us  [the longest x1 0.61 us: local(): jnp.stack([sums[0] / math.sqrt(snp_total), sums[1] / snp_total])]
  transfers between devices with their start and end apart: 3 -> 36, of which waited for: 3 -> 29; matrix products, arithmetic and copies ran while one was open for 4% -> 2% of each run, Pallas kernels for 0% -> 0%
where the time goes in v1:
time: 225 us; the launch traced here: 224 us
  waiting for transfers between devices  102 us (45%)
  starting transfers between devices  52 us (23%)
  other arithmetic  36.5 us (16%)
  matrix products  20.8 us (9%)
  local copies, waits for them, and re-layouts  11.4 us (5%)
    ppermute x36, waiting for transfers between devices, swap(): return lax.ppermute(values, axis, [(i, i ^ bit) for i in range(size)])  102 us
    ppermute x36, starting transfers between devices, swap(): return lax.ppermute(values, axis, [(i, i ^ bit) for i in range(size)])  52 us
    dot_general x2, matrix products, people_times(): lax.dot_general(both, dosage, (((1,), (1,)), ((), ())), preferred_element...  10.4 us
    reduce_sum x1, other arithmetic, local(): geno_sum = jnp.sum(genotypes, axis=0).astype(jnp.float32)  9.58 us
    dot_general x2, matrix products, snps_times(): lax.dot_general(both, dosage, (((1,), (0,)), ((), ())), preferred_element...  6.71 us
  transfers between devices with their start and end apart: 36, of which 29 were waited for; matrix products, arithmetic and copies ran while one was open for 2% of the time, Pallas kernels for 0%

profile of v1, /device:TPU:0, one launch (start us, length us, event | category | flops | bytes accessed | tf_op | source)
XLA Modules:
  0.0 224.2 jit_solution(17555399139901806886)
XLA Ops:
  1.6 9.6 %fusion.65 = (s32[1536]{0:T(1024)S(1)}, s32[1536]{0:T(1024)S(1)}, bf16[2048,1536]{1,0:T(8,128)(2,1)S(1)}) fusion(s32[2048,1536]{1,0:T(8,128)} %param.3), kind=kLoop, calls=%fused_computation.215 | loop fusion | flops 12579840 | bytes 18886656 | tf_op jit(solution)/shard_map/reduce_sum | solution.py:118
  15.3 4.0 %collective-permute-start.1 = (f32[8,1536]{1,0:T(8,128)S(1)}, f32[8,1536]{1,0:T(8,128)S(1)}, u32[]{:S(2)}, u32[]{:S(2)}) collective-permute-start(f32[8,1536]{1,0:T(8,128)S(1)} %fusion.76), channel_id=1, source_target_pairs={{0,64},{8,72},{16,80},{24,88},{32,96},{40,104},{48,112},{56,120},{... | collective-permute-start | bytes 147464 | tf_op jit(solution)/shard_map/ppermute | solution.py:27
  21.4 2.8 %collective-permute-start.4 = (f32[8,1536]{1,0:T(8,128)S(1)}, f32[8,1536]{1,0:T(8,128)S(1)}, u32[]{:S(2)}, u32[]{:S(2)}) collective-permute-start(f32[8,1536]{1,0:T(8,128)S(1)} %add.365), channel_id=1, source_target_pairs={{0,48},{8,56},{16,32},{24,40},{32,16},{40,24},{48,0},{56,8},{64,11... | collective-permute-start | bytes 147464 | tf_op jit(solution)/shard_map/ppermute | solution.py:27
  26.8 3.1 %collective-permute-done.3 = f32[8,1536]{1,0:T(8,128)S(1)} collective-permute-done((f32[8,1536]{1,0:T(8,128)S(1)}, f32[8,1536]{1,0:T(8,128)S(1)}, u32[]{:S(2)}, u32[]{:S(2)}) %collective-permute-start.3) | collective-permute-done | bytes 49184 | tf_op jit(solution)/shard_map/ppermute | solution.py:27
  32.1 5.1 %fusion.20 = f32[200,2048]{1,0:T(8,128)S(1)} fusion(bf16[2048,1536]{1,0:T(8,128)(2,1)} %copy-done, bf16[100,1536]{1,0:T(8,128)(2,1)S(1)} %get-tuple-element.71, bf16[100,1536]{1,0:T(8,128)(2,1)S(1)} %get-tuple-element.69), kind=kOutput, calls=%fused_computation.52 | convolution fusion | flops 1259520000 | bytes 8544256 | tf_op jit(solution)/shard_map/dot_general | solution.py:94
  41.0 3.6 %collective-permute-start.6 = (f32[50,1536]{1,0:T(8,128)S(1)}, f32[50,1536]{1,0:T(8,128)S(1)}, u32[]{:S(2)}, u32[]{:S(2)}) collective-permute-start(f32[50,1536]{1,0:T(8,128)S(1)} %dynamic-slice_add_fusion.1), channel_id=1, source_target_pairs={{0,64},{8,72},{16,80},{24,88},{32,96},{40,104},{48,112},{56,120},{... | collective-permute-start | bytes 921608 | tf_op jit(solution)/shard_map/ppermute | solution.py:27
  44.6 8.4 %collective-permute-done.6 = f32[50,1536]{1,0:T(8,128)S(1)} collective-permute-done((f32[50,1536]{1,0:T(8,128)S(1)}, f32[50,1536]{1,0:T(8,128)S(1)}, u32[]{:S(2)}, u32[]{:S(2)}) %collective-permute-start.6) | collective-permute-done | bytes 307232 | tf_op jit(solution)/shard_map/ppermute | solution.py:27
  53.3 2.4 %collective-permute-start.9 = (f32[50,384]{1,0:T(8,128)S(1)}, f32[50,384]{1,0:T(8,128)S(1)}, u32[]{:S(2)}, u32[]{:S(2)}) collective-permute-start(f32[50,384]{1,0:T(8,128)S(1)} %get-tuple-element.65), channel_id=1, source_target_pairs={{0,48},{8,56},{16,32},{24,40},{32,16},{40,24},{48,0},{56,8},{64,11... | collective-permute-start | bytes 230408 | tf_op jit(solution)/shard_map/ppermute | solution.py:27
  62.0 2.5 %collective-permute-start.11 = (f32[50,384]{1,0:T(8,128)S(1)}, f32[50,384]{1,0:T(8,128)S(1)}, u32[]{:S(2)}, u32[]{:S(2)}) collective-permute-start(f32[50,384]{1,0:T(8,128)S(1)} %add_add_fusion.1), channel_id=1, source_target_pairs={{0,32},{8,40},{16,48},{24,56},{32,0},{40,8},{48,16},{56,24},{64,96... | collective-permute-start | bytes 230408 | tf_op jit(solution)/shard_map/ppermute | solution.py:27
  77.1 5.3 %fusion.7 = f32[800,2048]{1,0:T(8,128)S(1)} fusion(bf16[2048,1536]{1,0:T(8,128)(2,1)S(1)} %bitcast.34, bf16[400,1536]{1,0:T(8,128)(2,1)S(1)} %get-tuple-element.37, bf16[400,1536]{1,0:T(8,128)(2,1)S(1)} %get-tuple-element.30), kind=kOutput, calls=%fused_computation.18 | convolution fusion | flops 5038080000 | bytes 15302656 | tf_op jit(solution)/shard_map/dot_general | solution.py:94
  83.4 5.2 %fusion.2 = f32[800,1536]{1,0:T(8,128)S(1)} fusion(bf16[2048,1536]{1,0:T(8,128)(2,1)S(1)} %bitcast.34, bf16[400,2048]{1,0:T(8,128)(2,1)S(1)} %get-tuple-element.36, bf16[400,2048]{1,0:T(8,128)(2,1)S(1)} %get-tuple-element.35), kind=kOutput, calls=%fused_computation.9 | convolution fusion | flops 5039718400 | bytes 14483456 | tf_op jit(solution)/shard_map/dot_general | solution.py:101
  91.8 3.1 %collective-permute-done.14 = f32[200,1536]{1,0:T(8,128)} collective-permute-done((f32[200,1536]{1,0:T(8,128)}, f32[200,1536]{1,0:T(8,128)}, u32[]{:S(2)}, u32[]{:S(2)}) %collective-permute-start.14) | collective-permute-done | bytes 1228832 | tf_op jit(solution)/shard_map/ppermute | solution.py:27
  94.9 2.9 %dynamic-slice_add_fusion = f32[200,1536]{1,0:T(8,128)} fusion(f32[200,1536]{1,0:T(8,128)} %collective-permute-done.14, f32[400,1536]{1,0:T(8,128)} %copy-done.1, s32[]{:T(128)S(6)} %select_n.492), kind=kLoop, calls=%fused_computation.29 | loop fusion | flops 307200 | bytes 3686404 | tf_op jit(solution)/shard_map/add | solution.py:56
  97.8 3.1 %collective-permute-start.15 = (f32[200,1536]{1,0:T(8,128)}, f32[200,1536]{1,0:T(8,128)}, u32[]{:S(2)}, u32[]{:S(2)}) collective-permute-start(f32[200,1536]{1,0:T(8,128)} %dynamic-slice_add_fusion), channel_id=1, source_target_pairs={{0,64},{8,72},{16,80},{24,88},{32,96},{40,104},{48,112},{56,120},{... | collective-permute-start | bytes 3686408 | tf_op jit(solution)/shard_map/ppermute | solution.py:27
  101.0 27.7 %collective-permute-done.15 = f32[200,1536]{1,0:T(8,128)} collective-permute-done((f32[200,1536]{1,0:T(8,128)}, f32[200,1536]{1,0:T(8,128)}, u32[]{:S(2)}, u32[]{:S(2)}) %collective-permute-start.15) | collective-permute-done | bytes 1228832 | tf_op jit(solution)/shard_map/ppermute | solution.py:27
  135.0 5.9 %collective-permute-done.16 = f32[200,384]{1,0:T(8,128)S(1)} collective-permute-done((f32[200,384]{1,0:T(8,128)S(1)}, f32[200,384]{1,0:T(8,128)S(1)}, u32[]{:S(2)}, u32[]{:S(2)}) %collective-permute-start.16) | collective-permute-done | bytes 307232 | tf_op jit(solution)/shard_map/ppermute | solution.py:27
  140.9 4.5 %collective-permute-done.18 = f32[200,384]{1,0:T(8,128)S(1)} collective-permute-done((f32[200,384]{1,0:T(8,128)S(1)}, f32[200,384]{1,0:T(8,128)S(1)}, u32[]{:S(2)}, u32[]{:S(2)}) %collective-permute-start.18) | collective-permute-done | bytes 307232 | tf_op jit(solution)/shard_map/ppermute | solution.py:27
  147.9 3.0 %collective-permute-start.20 = (f32[200,384]{1,0:T(8,128)S(1)}, f32[200,384]{1,0:T(8,128)S(1)}, u32[]{:S(2)}, u32[]{:S(2)}) collective-permute-start(f32[200,384]{1,0:T(8,128)S(1)} %minimum_subtract_fusion.5), channel_id=1, source_target_pairs={{0,32},{8,40},{16,48},{24,56},{32,0},{40,8},{48,16},{56,24},{64,96... | collective-permute-start | bytes 921608 | tf_op jit(solution)/shard_map/ppermute | solution.py:27
  152.3 5.5 %collective-permute-done.21 = f32[200,384]{1,0:T(8,128)S(1)} collective-permute-done((f32[200,384]{1,0:T(8,128)S(1)}, f32[200,384]{1,0:T(8,128)S(1)}, u32[]{:S(2)}, u32[]{:S(2)}) %collective-permute-start.21) | collective-permute-done | bytes 307232 | tf_op jit(solution)/shard_map/ppermute | solution.py:27
  157.8 4.8 %collective-permute-done.20 = f32[200,384]{1,0:T(8,128)S(1)} collective-permute-done((f32[200,384]{1,0:T(8,128)S(1)}, f32[200,384]{1,0:T(8,128)S(1)}, u32[]{:S(2)}, u32[]{:S(2)}) %collective-permute-start.20) | collective-permute-done | bytes 307232 | tf_op jit(solution)/shard_map/ppermute | solution.py:27
  162.6 2.6 %collective-permute-done.19 = f32[200,384]{1,0:T(8,128)S(1)} collective-permute-done((f32[200,384]{1,0:T(8,128)S(1)}, f32[200,384]{1,0:T(8,128)S(1)}, u32[]{:S(2)}, u32[]{:S(2)}) %collective-permute-start.19) | collective-permute-done | bytes 307232 | tf_op jit(solution)/shard_map/ppermute | solution.py:27
  166.6 3.0 %collective-permute-done.22 = f32[200,1536]{1,0:T(8,128)S(1)} collective-permute-done((f32[200,1536]{1,0:T(8,128)}, f32[200,1536]{1,0:T(8,128)S(1)}, u32[]{:S(2)}, u32[]{:S(2)}) %collective-permute-start.22) | collective-permute-done | bytes 1228832 | tf_op jit(solution)/shard_map/ppermute | solution.py:27
  169.9 3.6 %multiply_reduce_fusion.2 = (f32[400]{0:T(512)S(1)}, f32[400]{0:T(512)S(1)}, f32[1536,400]{0,1:T(8,128)}, f32[400,1536]{1,0:T(8,128)}) fusion(f32[1536]{0:T(1024)S(1)} %get-tuple-element.12, f32[1536]{0:T(1024)S(1)} %get-tuple-element.13, f32[1536]{0:T(1024)S(1)} %get-tuple-element.14, f32[1536]{0:T(1024)S(1)} %get-tuple-element.15, ...), kind=kLoop, calls=%fused_computation.24 | loop fusion | flops 7372000 | bytes 7421008 | tf_op jit(solution)/shard_map/reduce_sum | solution.py:175
  173.8 3.9 %concatenate.50 = f32[80,5,1536]{2,1,0:T(8,128)} reshape(f32[400,1536]{1,0:T(8,128)} %get-tuple-element.40) | data formatting | bytes 4915200 | tf_op jit(solution)/shard_map/concatenate | solution.py:70
  177.7 2.7 %fusion.11 = bf16[5,80,1536]{2,0,1:T(8,128)(2,1)S(1)} fusion(f32[80,5,1536]{2,1,0:T(8,128)} %concatenate.50, f32[1536]{0:T(1024)S(1)} %reduce.2), kind=kLoop, calls=%fused_computation.27 | loop fusion | flops 1843200 | bytes 3692544 | tf_op jit(solution)/shard_map/transpose | solution.py:176
  181.1 2.7 %convolution_subtract_fusion = f32[400,2048]{1,0:T(8,128)S(1)} fusion(bf16[400,1536]{1,0:T(8,128)(2,1)S(1)} %bitcast.38, bf16[2048,1536]{1,0:T(8,128)(2,1)S(1)} %bitcast.36, f32[400]{0:T(512)S(1)} %sub.223), kind=kOutput, calls=%fused_computation.14 | convolution fusion | flops 2517401600 | bytes 10798656 | tf_op jit(solution)/shard_map/dot_general | solution.py:178
  190.9 4.1 %collective-permute-done.26 = f32[80,512]{1,0:T(8,128)S(1)} collective-permute-done((f32[80,512]{1,0:T(8,128)S(1)}, f32[80,512]{1,0:T(8,128)S(1)}, u32[]{:S(2)}, u32[]{:S(2)}) %collective-permute-start.26) | collective-permute-done | bytes 163872 | tf_op jit(solution)/shard_map/ppermute | solution.py:27
  197.9 4.2 %collective-permute-done.27 = f32[80,512]{1,0:T(8,128)S(1)} collective-permute-done((f32[80,512]{1,0:T(8,128)S(1)}, f32[80,512]{1,0:T(8,128)S(1)}, u32[]{:S(2)}, u32[]{:S(2)}) %collective-permute-start.27) | collective-permute-done | bytes 163872 | tf_op jit(solution)/shard_map/ppermute | solution.py:27
  203.8 3.2 %collective-permute-start.29 = (f32[2,400]{1,0:T(2,128)S(1)}, f32[2,400]{1,0:T(2,128)S(1)}, u32[]{:S(2)}, u32[]{:S(2)}) collective-permute-start(f32[2,400]{1,0:T(2,128)S(1)} %fusion.63), channel_id=1, source_target_pairs={{0,64},{8,72},{16,80},{24,88},{32,96},{40,104},{48,112},{56,120},{... | collective-permute-start | bytes 9608 | tf_op jit(solution)/shard_map/ppermute | solution.py:27
  213.9 2.2 %collective-permute-done.31 = f32[2,400]{1,0:T(2,128)S(1)} collective-permute-done((f32[2,400]{1,0:T(2,128)S(1)}, f32[2,400]{1,0:T(2,128)S(1)}, u32[]{:S(2)}, u32[]{:S(2)}) %collective-permute-start.31) | collective-permute-done | bytes 3232 | tf_op jit(solution)/shard_map/ppermute | solution.py:27
  216.2 2.2 collective-permute-start.35
  220.4 3.2 %select_select_fusion.1 = f32[400]{0:T(512)S(1)} fusion(f32[]{:T(128)} %bitcast.17, f32[]{:T(128)} %bitcast.16, f32[]{:T(128)} %bitcast.15, f32[]{:T(128)} %bitcast.14, f32[]{:T(128)} %bitcast.13), kind=kLoop, calls=%fused_computation.145 | loop fusion | flops 6400 | bytes 1620 | tf_op jit(solution)/shard_map/jit(_where)/select_n | solution.py:87
  (154 shorter events, 72.9 us)
Async XLA Ops:
  15.3 6.1 %collective-permute-start.1 = (f32[8,1536]{1,0:T(8,128)S(1)}, f32[8,1536]{1,0:T(8,128)S(1)}, u32[]{:S(2)}, u32[]{:S(2)}) collective-permute-start(f32[8,1536]{1,0:T(8,128)S(1)} %fusion.76), channel_id=1, source_target_pairs={{0,64},{8,72},{16,80},{24,88},{32,96},{40,104},{48,112},{56,120},{... | collective-permute-start | bytes 147464 | tf_op jit(solution)/shard_map/ppermute | solution.py:27
  21.4 5.4 %collective-permute-start.4 = (f32[8,1536]{1,0:T(8,128)S(1)}, f32[8,1536]{1,0:T(8,128)S(1)}, u32[]{:S(2)}, u32[]{:S(2)}) collective-permute-start(f32[8,1536]{1,0:T(8,128)S(1)} %add.365), channel_id=1, source_target_pairs={{0,48},{8,56},{16,32},{24,40},{32,16},{40,24},{48,0},{56,8},{64,11... | collective-permute-start | bytes 147464 | tf_op jit(solution)/shard_map/ppermute | solution.py:27
  24.3 5.6 %collective-permute-start.3 = (f32[8,1536]{1,0:T(8,128)S(1)}, f32[8,1536]{1,0:T(8,128)S(1)}, u32[]{:S(2)}, u32[]{:S(2)}) collective-permute-start(f32[8,1536]{1,0:T(8,128)S(1)} %add.365), channel_id=1, source_target_pairs={{0,32},{8,40},{16,48},{24,56},{32,0},{40,8},{48,16},{56,24},{64,96... | collective-permute-start | bytes 147464 | tf_op jit(solution)/shard_map/ppermute | solution.py:27
  25.1 4.8 %collective-permute-start.2 = (f32[8,1536]{1,0:T(8,128)S(1)}, f32[8,1536]{1,0:T(8,128)S(1)}, u32[]{:S(2)}, u32[]{:S(2)}) collective-permute-start(f32[8,1536]{1,0:T(8,128)S(1)} %add.365), channel_id=1, source_target_pairs={{0,16},{8,24},{16,0},{24,8},{32,48},{40,56},{48,32},{56,40},{64,80... | collective-permute-start | bytes 147464 | tf_op jit(solution)/shard_map/ppermute | solution.py:27
  41.0 12.0 %collective-permute-start.6 = (f32[50,1536]{1,0:T(8,128)S(1)}, f32[50,1536]{1,0:T(8,128)S(1)}, u32[]{:S(2)}, u32[]{:S(2)}) collective-permute-start(f32[50,1536]{1,0:T(8,128)S(1)} %dynamic-slice_add_fusion.1), channel_id=1, source_target_pairs={{0,64},{8,72},{16,80},{24,88},{32,96},{40,104},{48,112},{56,120},{... | collective-permute-start | bytes 921608 | tf_op jit(solution)/shard_map/ppermute | solution.py:27
  53.0 5.0 %collective-permute-start.7 = (f32[50,384]{1,0:T(8,128)S(1)}, f32[50,384]{1,0:T(8,128)S(1)}, u32[]{:S(2)}, u32[]{:S(2)}) collective-permute-start(f32[50,384]{1,0:T(8,128)S(1)} %get-tuple-element.64), channel_id=1, source_target_pairs={{0,16},{8,24},{16,0},{24,8},{32,48},{40,56},{48,32},{56,40},{64,80... | collective-permute-start | bytes 230408 | tf_op jit(solution)/shard_map/ppermute | solution.py:27
  53.3 6.6 %collective-permute-start.9 = (f32[50,384]{1,0:T(8,128)S(1)}, f32[50,384]{1,0:T(8,128)S(1)}, u32[]{:S(2)}, u32[]{:S(2)}) collective-permute-start(f32[50,384]{1,0:T(8,128)S(1)} %get-tuple-element.65), channel_id=1, source_target_pairs={{0,48},{8,56},{16,32},{24,40},{32,16},{40,24},{48,0},{56,8},{64,11... | collective-permute-start | bytes 230408 | tf_op jit(solution)/shard_map/ppermute | solution.py:27
  55.7 6.0 %collective-permute-start.8 = (f32[50,384]{1,0:T(8,128)S(1)}, f32[50,384]{1,0:T(8,128)S(1)}, u32[]{:S(2)}, u32[]{:S(2)}) collective-permute-start(f32[50,384]{1,0:T(8,128)S(1)} %get-tuple-element.66), channel_id=1, source_target_pairs={{0,32},{8,40},{16,48},{24,56},{32,0},{40,8},{48,16},{56,24},{64,96... | collective-permute-start | bytes 230408 | tf_op jit(solution)/shard_map/ppermute | solution.py:27
  61.7 4.8 %collective-permute-start.12 = (f32[50,384]{1,0:T(8,128)S(1)}, f32[50,384]{1,0:T(8,128)S(1)}, u32[]{:S(2)}, u32[]{:S(2)}) collective-permute-start(f32[50,384]{1,0:T(8,128)S(1)} %add_add_fusion.1), channel_id=1, source_target_pairs={{0,16},{8,24},{16,0},{24,8},{32,48},{40,56},{48,32},{56,40},{64,80... | collective-permute-start | bytes 230408 | tf_op jit(solution)/shard_map/ppermute | solution.py:27
  62.0 6.0 %collective-permute-start.11 = (f32[50,384]{1,0:T(8,128)S(1)}, f32[50,384]{1,0:T(8,128)S(1)}, u32[]{:S(2)}, u32[]{:S(2)}) collective-permute-start(f32[50,384]{1,0:T(8,128)S(1)} %add_add_fusion.1), channel_id=1, source_target_pairs={{0,32},{8,40},{16,48},{24,56},{32,0},{40,8},{48,16},{56,24},{64,96... | collective-permute-start | bytes 230408 | tf_op jit(solution)/shard_map/ppermute | solution.py:27
  64.5 5.7 %collective-permute-start.10 = (f32[50,384]{1,0:T(8,128)S(1)}, f32[50,384]{1,0:T(8,128)S(1)}, u32[]{:S(2)}, u32[]{:S(2)}) collective-permute-start(f32[50,384]{1,0:T(8,128)S(1)} %add_add_fusion.1), channel_id=1, source_target_pairs={{0,48},{8,56},{16,32},{24,40},{32,16},{40,24},{48,0},{56,8},{64,11... | collective-permute-start | bytes 230408 | tf_op jit(solution)/shard_map/ppermute | solution.py:27
  91.7 3.3 %collective-permute-start.14 = (f32[200,1536]{1,0:T(8,128)}, f32[200,1536]{1,0:T(8,128)}, u32[]{:S(2)}, u32[]{:S(2)}) collective-permute-start(f32[200,1536]{1,0:T(8,128)} %constant_dynamic-slice_fusion.8), channel_id=1, source_target_pairs={{0,8},{8,0},{16,24},{24,16},{32,40},{40,32},{48,56},{56,48},{64,72... | collective-permute-start | bytes 3686408 | tf_op jit(solution)/shard_map/ppermute | solution.py:27
  97.8 30.9 %collective-permute-start.15 = (f32[200,1536]{1,0:T(8,128)}, f32[200,1536]{1,0:T(8,128)}, u32[]{:S(2)}, u32[]{:S(2)}) collective-permute-start(f32[200,1536]{1,0:T(8,128)} %dynamic-slice_add_fusion), channel_id=1, source_target_pairs={{0,64},{8,72},{16,80},{24,88},{32,96},{40,104},{48,112},{56,120},{... | collective-permute-start | bytes 3686408 | tf_op jit(solution)/shard_map/ppermute | solution.py:27
  130.6 10.3 %collective-permute-start.16 = (f32[200,384]{1,0:T(8,128)S(1)}, f32[200,384]{1,0:T(8,128)S(1)}, u32[]{:S(2)}, u32[]{:S(2)}) collective-permute-start(f32[200,384]{1,0:T(8,128)S(1)} %get-tuple-element.49), channel_id=1, source_target_pairs={{0,16},{8,24},{16,0},{24,8},{32,48},{40,56},{48,32},{56,40},{64,80... | collective-permute-start | bytes 921608 | tf_op jit(solution)/shard_map/ppermute | solution.py:27
  130.7 14.7 %collective-permute-start.18 = (f32[200,384]{1,0:T(8,128)S(1)}, f32[200,384]{1,0:T(8,128)S(1)}, u32[]{:S(2)}, u32[]{:S(2)}) collective-permute-start(f32[200,384]{1,0:T(8,128)S(1)} %get-tuple-element.50), channel_id=1, source_target_pairs={{0,48},{8,56},{16,32},{24,40},{32,16},{40,24},{48,0},{56,8},{64,11... | collective-permute-start | bytes 921608 | tf_op jit(solution)/shard_map/ppermute | solution.py:27
  132.8 14.4 %collective-permute-start.17 = (f32[200,384]{1,0:T(8,128)S(1)}, f32[200,384]{1,0:T(8,128)S(1)}, u32[]{:S(2)}, u32[]{:S(2)}) collective-permute-start(f32[200,384]{1,0:T(8,128)S(1)} %get-tuple-element.51), channel_id=1, source_target_pairs={{0,32},{8,40},{16,48},{24,56},{32,0},{40,8},{48,16},{56,24},{64,96... | collective-permute-start | bytes 921608 | tf_op jit(solution)/shard_map/ppermute | solution.py:27
  147.5 10.3 %collective-permute-start.21 = (f32[200,384]{1,0:T(8,128)S(1)}, f32[200,384]{1,0:T(8,128)S(1)}, u32[]{:S(2)}, u32[]{:S(2)}) collective-permute-start(f32[200,384]{1,0:T(8,128)S(1)} %minimum_subtract_fusion.5), channel_id=1, source_target_pairs={{0,16},{8,24},{16,0},{24,8},{32,48},{40,56},{48,32},{56,40},{64,80... | collective-permute-start | bytes 921608 | tf_op jit(solution)/shard_map/ppermute | solution.py:27
  147.9 14.7 %collective-permute-start.20 = (f32[200,384]{1,0:T(8,128)S(1)}, f32[200,384]{1,0:T(8,128)S(1)}, u32[]{:S(2)}, u32[]{:S(2)}) collective-permute-start(f32[200,384]{1,0:T(8,128)S(1)} %minimum_subtract_fusion.5), channel_id=1, source_target_pairs={{0,32},{8,40},{16,48},{24,56},{32,0},{40,8},{48,16},{56,24},{64,96... | collective-permute-start | bytes 921608 | tf_op jit(solution)/shard_map/ppermute | solution.py:27
  151.0 14.2 %collective-permute-start.19 = (f32[200,384]{1,0:T(8,128)S(1)}, f32[200,384]{1,0:T(8,128)S(1)}, u32[]{:S(2)}, u32[]{:S(2)}) collective-permute-start(f32[200,384]{1,0:T(8,128)S(1)} %minimum_subtract_fusion.5), channel_id=1, source_target_pairs={{0,48},{8,56},{16,32},{24,40},{32,16},{40,24},{48,0},{56,8},{64,11... | collective-permute-start | bytes 921608 | tf_op jit(solution)/shard_map/ppermute | solution.py:27
  166.5 3.1 %collective-permute-start.22 = (f32[200,1536]{1,0:T(8,128)}, f32[200,1536]{1,0:T(8,128)S(1)}, u32[]{:S(2)}, u32[]{:S(2)}) collective-permute-start(f32[200,1536]{1,0:T(8,128)} %pad_maximum_fusion.2), channel_id=1, source_target_pairs={{0,8},{8,0},{16,24},{24,16},{32,40},{40,32},{48,56},{56,48},{64,72... | collective-permute-start | bytes 3686408 | tf_op jit(solution)/shard_map/ppermute | solution.py:27
  184.2 6.7 %collective-permute-start.24 = (f32[80,512]{1,0:T(8,128)S(1)}, f32[80,512]{1,0:T(8,128)S(1)}, u32[]{:S(2)}, u32[]{:S(2)}) collective-permute-start(f32[80,512]{1,0:T(8,128)S(1)} %get-tuple-element.57), channel_id=1, source_target_pairs={{0,1},{1,0},{2,3},{3,2},{4,5},{5,4},{6,7},{7,6},{8,9},{9,8},{10,11... | collective-permute-start | bytes 491528 | tf_op jit(solution)/shard_map/ppermute | solution.py:27
  185.9 9.2 %collective-permute-start.26 = (f32[80,512]{1,0:T(8,128)S(1)}, f32[80,512]{1,0:T(8,128)S(1)}, u32[]{:S(2)}, u32[]{:S(2)}) collective-permute-start(f32[80,512]{1,0:T(8,128)S(1)} %get-tuple-element.58), channel_id=1, source_target_pairs={{0,3},{1,2},{2,1},{3,0},{4,7},{5,6},{6,5},{7,4},{8,11},{9,10},{10,... | collective-permute-start | bytes 491528 | tf_op jit(solution)/shard_map/ppermute | solution.py:27
  188.1 8.5 %collective-permute-start.25 = (f32[80,512]{1,0:T(8,128)S(1)}, f32[80,512]{1,0:T(8,128)S(1)}, u32[]{:S(2)}, u32[]{:S(2)}) collective-permute-start(f32[80,512]{1,0:T(8,128)S(1)} %get-tuple-element.59), channel_id=1, source_target_pairs={{0,2},{1,3},{2,0},{3,1},{4,6},{5,7},{6,4},{7,5},{8,10},{9,11},{10,... | collective-permute-start | bytes 491528 | tf_op jit(solution)/shard_map/ppermute | solution.py:27
  188.9 9.0 %collective-permute-start.23 = (f32[400]{0:T(512)S(1)}, f32[400]{0:T(512)S(1)}, u32[]{:S(2)}, u32[]{:S(2)}) collective-permute-start(f32[400]{0:T(512)S(1)} %get-tuple-element.4), channel_id=1, source_target_pairs={{0,4},{1,5},{2,6},{3,7},{4,0},{5,1},{6,2},{7,3},{8,12},{9,13},{10,... | collective-permute-start | bytes 4808 | tf_op jit(solution)/shard_map/ppermute | solution.py:27
  196.6 5.4 %collective-permute-start.27 = (f32[80,512]{1,0:T(8,128)S(1)}, f32[80,512]{1,0:T(8,128)S(1)}, u32[]{:S(2)}, u32[]{:S(2)}) collective-permute-start(f32[80,512]{1,0:T(8,128)S(1)} %add_add_fusion), channel_id=1, source_target_pairs={{0,4},{1,5},{2,6},{3,7},{4,0},{5,1},{6,2},{7,3},{8,12},{9,13},{10,... | collective-permute-start | bytes 491528 | tf_op jit(solution)/shard_map/ppermute | solution.py:27
  203.8 5.2 %collective-permute-start.29 = (f32[2,400]{1,0:T(2,128)S(1)}, f32[2,400]{1,0:T(2,128)S(1)}, u32[]{:S(2)}, u32[]{:S(2)}) collective-permute-start(f32[2,400]{1,0:T(2,128)S(1)} %fusion.63), channel_id=1, source_target_pairs={{0,64},{8,72},{16,80},{24,88},{32,96},{40,104},{48,112},{56,120},{... | collective-permute-start | bytes 9608 | tf_op jit(solution)/shard_map/ppermute | solution.py:27
  209.0 4.9 %collective-permute-start.32 = (f32[2,400]{1,0:T(2,128)S(1)}, f32[2,400]{1,0:T(2,128)S(1)}, u32[]{:S(2)}, u32[]{:S(2)}) collective-permute-start(f32[2,400]{1,0:T(2,128)S(1)} %fusion.75), channel_id=1, source_target_pairs={{0,48},{8,56},{16,32},{24,40},{32,16},{40,24},{48,0},{56,8},{64,11... | collective-permute-start | bytes 9608 | tf_op jit(solution)/shard_map/ppermute | solution.py:27
  211.1 5.1 %collective-permute-start.31 = (f32[2,400]{1,0:T(2,128)S(1)}, f32[2,400]{1,0:T(2,128)S(1)}, u32[]{:S(2)}, u32[]{:S(2)}) collective-permute-start(f32[2,400]{1,0:T(2,128)S(1)} %fusion.75), channel_id=1, source_target_pairs={{0,32},{8,40},{16,48},{24,56},{32,0},{40,8},{48,16},{56,24},{64,96... | collective-permute-start | bytes 9608 | tf_op jit(solution)/shard_map/ppermute | solution.py:27
  211.1 5.1 %collective-permute-start.30 = (f32[2,400]{1,0:T(2,128)S(1)}, f32[2,400]{1,0:T(2,128)S(1)}, u32[]{:S(2)}, u32[]{:S(2)}) collective-permute-start(f32[2,400]{1,0:T(2,128)S(1)} %fusion.75), channel_id=1, source_target_pairs={{0,16},{8,24},{16,0},{24,8},{32,48},{40,56},{48,32},{56,40},{64,80... | collective-permute-start | bytes 9608 | tf_op jit(solution)/shard_map/ppermute | solution.py:27
  216.2 7.3 %collective-permute-start.35 = (f32[2,400]{1,0:T(2,128)S(1)}, f32[2,400]{1,0:T(2,128)S(1)}, u32[]{:S(2)}, u32[]{:S(2)}) collective-permute-start(f32[2,400]{1,0:T(2,128)S(1)} %add_add_fusion.4), channel_id=1, source_target_pairs={{0,3},{1,2},{2,1},{3,0},{4,7},{5,6},{6,5},{7,4},{8,11},{9,10},{10,... | collective-permute-start | bytes 9608 | tf_op jit(solution)/shard_map/ppermute | solution.py:27
  218.4 5.1 %collective-permute-start.34 = (f32[2,400]{1,0:T(2,128)S(1)}, f32[2,400]{1,0:T(2,128)S(1)}, u32[]{:S(2)}, u32[]{:S(2)}) collective-permute-start(f32[2,400]{1,0:T(2,128)S(1)} %add_add_fusion.4), channel_id=1, source_target_pairs={{0,2},{1,3},{2,0},{3,1},{4,6},{5,7},{6,4},{7,5},{8,10},{9,11},{10,... | collective-permute-start | bytes 9608 | tf_op jit(solution)/shard_map/ppermute | solution.py:27
  218.6 5.0 %collective-permute-start.33 = (f32[2,400]{1,0:T(2,128)S(1)}, f32[2,400]{1,0:T(2,128)S(1)}, u32[]{:S(2)}, u32[]{:S(2)}) collective-permute-start(f32[2,400]{1,0:T(2,128)S(1)} %add_add_fusion.4), channel_id=1, source_target_pairs={{0,1},{1,0},{2,3},{3,2},{4,5},{5,4},{6,7},{7,6},{8,9},{9,8},{10,11... | collective-permute-start | bytes 9608 | tf_op jit(solution)/shard_map/ppermute | solution.py:27
  (13 other events, 55.8 us)

commit v2 on v0

v2 whole, which is shorter than its diff:
```python
import functools
import math

import jax
import jax.numpy as jnp
from jax import lax
from jax.experimental import pallas as pl
from jax.experimental.pallas import tpu as pltpu
from jax.sharding import PartitionSpec as P

FOLDS = 5
LAMBDAS = 20
GRID = 400
BASE = FOLDS * LAMBDAS
SHRINKS = GRID // BASE
LEVELS = GRID // FOLDS
ROWS0 = 112
ROWS1 = 104
PEOPLE = 32768
SNPS = 12288
VMEM = 56 * 1024 * 1024

step_size = 0.6
epsilon = 1e-05
lambda_base = 0.1
lambda_ratio = 1.2
shrink_unit = 0.2

NT = (((1,), (1,)), ((), ()))
NN = (((1,), (0,)), ((), ()))
TN = (((0,), (0,)), ((), ()))


def matmul(left, right, dims):
    return lax.dot_general(left, right, dims, preferred_element_type=jnp.float32)


def soft_threshold(values, cutoff):
    return values - jnp.clip(values, -cutoff, cutoff)


def swap(values, axis, bit):
    size = lax.axis_size(axis)
    return lax.ppermute(values, axis, [(i, i ^ bit) for i in range(size)])


def rounded(values):
    return lax.reduce_precision(values, 8, 7)


def split2(values):
    high = values.astype(jnp.bfloat16)
    return high, (values - high.astype(jnp.float32)).astype(jnp.bfloat16)


def order4(parts, place):
    low, high = (place & 1) == 1, (place & 2) == 2
    a, b, c, d = parts
    a, b, c, d = (jnp.where(low, b, a), jnp.where(low, a, b), jnp.where(low, d, c), jnp.where(low, c, d))
    return jnp.where(high, c, a), jnp.where(high, d, b), jnp.where(high, a, c), jnp.where(high, b, d)


def all_sum(values, bits):
    for axis, group in bits:
        got = [swap(values, axis, bit) for bit in group]
        values = values + got[0] if len(got) == 1 else (values + got[0]) + (got[1] + got[2])
    return values


SAMP_BITS = (("samp", (1,)), ("samp", (8,)), ("samp", (2, 4, 6)))


def scatter_chips(kept, place):
    width = kept.shape[1] // 4
    got = [
        swap(lax.dynamic_slice_in_dim(kept, (place ^ k) * width, width, 1), "samp", 2 * k) for k in (1, 2, 3)
    ]
    mine = lax.dynamic_slice_in_dim(kept, place * width, width, 1)
    mine = (mine + got[0]) + (got[1] + got[2])
    return mine + swap(mine, "samp", 8)


def gather_chips(piece, place):
    parts = [piece] + [swap(piece, "samp", 2 * k) for k in (1, 2, 3)]
    return jnp.concatenate(order4(parts, place), axis=1)


def prepare_kernel(left_ref, geno_ref, dose_ref, sums_ref, squares_ref):
    @pl.when(pl.program_id(0) == 0)
    def _():
        sums_ref[...] = jnp.zeros_like(sums_ref)
        squares_ref[...] = jnp.zeros_like(squares_ref)

    values = geno_ref[...].astype(jnp.float32)
    dose = values.astype(jnp.bfloat16)
    dose_ref[...] = dose
    sums_ref[...] += matmul(left_ref[...], dose, NN)
    squares_ref[...] += jnp.sum((values * values).reshape(-1, 8, values.shape[1]), axis=0)


def prepare(left, genotypes, tile=256):
    people, width = genotypes.shape
    return pl.pallas_call(
        prepare_kernel,
        grid=(people // tile,),
        in_specs=[pl.BlockSpec((16, tile), lambda i: (0, i)), pl.BlockSpec((tile, width), lambda i: (i, 0))],
        out_specs=[
            pl.BlockSpec((tile, width), lambda i: (i, 0)),
            pl.BlockSpec((16, width), lambda i: (0, 0)),
            pl.BlockSpec((8, width), lambda i: (0, 0)),
        ],
        out_shape=[
            jax.ShapeDtypeStruct((people, width), jnp.bfloat16),
            jax.ShapeDtypeStruct((16, width), jnp.float32),
            jax.ShapeDtypeStruct((8, width), jnp.float32),
        ],
        compiler_params=pltpu.CompilerParams(vmem_limit_bytes=VMEM),
    )(left, genotypes)


def base_rows(rows):
    row = lax.broadcasted_iota(jnp.int32, (rows, 1), 0)
    cutoff = step_size * (lambda_base * jnp.exp((row // FOLDS).astype(jnp.float32) * math.log(lambda_ratio)))
    return row, row % FOLDS, cutoff


def spread(table, fold_of):
    out = jnp.broadcast_to(table[FOLDS - 1 : FOLDS], (fold_of.shape[0], table.shape[1]))
    for fold in range(FOLDS - 1):
        out = jnp.where(fold_of == fold, table[fold : fold + 1], out)
    return out


def next_coeff(coeff, product, target, shrink, cutoff):
    gradient = (1.0 - shrink) * product + shrink * coeff - target
    return soft_threshold(coeff - step_size * gradient, cutoff)


def first_kernel(table_ref, dose_ref, out_ref, both_ref, offset_ref, total_ref):
    @pl.when(pl.program_id(0) == 0)
    def _():
        table = table_ref[...]
        row, fold_of, cutoff = base_rows(ROWS0)
        coeff = soft_threshold(step_size * spread(table[:FOLDS], fold_of), cutoff)
        scaled = jnp.where(row < BASE, coeff * table[7:8], 0.0)
        high, low = split2(scaled)
        both_ref[...] = jnp.zeros_like(both_ref)
        both_ref[0:ROWS0] = high
        both_ref[128 : 128 + ROWS0] = low
        mean_high, mean_rest = split2(table[5:6])
        rest = table[5:6] - mean_high.astype(jnp.float32)
        mean_mid, mean_low = split2(rest)
        line = lax.broadcasted_iota(jnp.int32, (16, 1), 0)
        means = jnp.where(
            line == 0,
            mean_high.astype(jnp.float32),
            jnp.where(
                line == 1,
                mean_mid.astype(jnp.float32),
                jnp.where(line == 2, mean_low.astype(jnp.float32), 0.0),
            ),
        ).astype(jnp.bfloat16)
        offset = jnp.sum(matmul(means, both_ref[...], NT), axis=0, keepdims=True)
        offset_ref[...] = jnp.broadcast_to(offset[:, :128] + offset[:, 128:], offset_ref.shape)
        total_ref[...] = jnp.zeros_like(total_ref)

    dose = dose_ref[...]
    scores = matmul(dose, both_ref[...], NT)
    scores = scores[:, :128] + scores[:, 128:] - offset_ref[0:1]
    pair = jnp.concatenate(split2(scores), axis=1)
    total_ref[...] += matmul(pair, dose, TN)

    @pl.when(pl.program_id(0) == pl.num_programs(0) - 1)
    def _():
        out_ref[...] = total_ref[0:ROWS0] + total_ref[128 : 128 + ROWS0]


def first_product(table, dose, tile=512):
    people, width = dose.shape
    return pl.pallas_call(
        first_kernel,
        grid=(people // tile,),
        in_specs=[pl.BlockSpec((8, width), lambda i: (0, 0)), pl.BlockSpec((tile, width), lambda i: (i, 0))],
        out_specs=pl.BlockSpec((ROWS0, width), lambda i: (0, 0)),
        out_shape=jax.ShapeDtypeStruct((ROWS0, width), jnp.float32),
        scratch_shapes=[
            pltpu.VMEM((256, width), jnp.bfloat16),
            pltpu.VMEM((8, 128), jnp.float32),
            pltpu.VMEM((256, width), jnp.float32),
        ],
        compiler_params=pltpu.CompilerParams(vmem_limit_bytes=VMEM),
    )(table, dose)


def second_kernel(half_ref, table_ref, product_ref, dose_ref, out_ref, coeff_ref, both_ref, offset_ref):
    rows = 2 * ROWS1

    @pl.when(pl.program_id(0) == 0)
    def _():
        table = table_ref[...]
        row, fold_of, cutoff = base_rows(ROWS1)
        target = spread(table[:FOLDS], fold_of)
        coeff = soft_threshold(step_size * target, cutoff)
        product = product_ref[0:ROWS1] * (table[7:8] / PEOPLE)
        for group in range(2):
            shrink = shrink_unit * (2 * half_ref[0] + group + 1).astype(jnp.float32)
            new = next_coeff(coeff, product, target, shrink, cutoff)
            coeff_ref[group * ROWS1 : (group + 1) * ROWS1] = jnp.where(row < BASE, new, 0.0)
        scaled = coeff_ref[...] * table[7:8]
        offset_ref[...] = jnp.sum(scaled * table[5:6], axis=1, keepdims=True)
        high, low = split2(scaled)
        both_ref[0:rows] = high
        both_ref[rows:] = low
        out_ref[...] = jnp.zeros_like(out_ref)

    dose = dose_ref[...]
    scores = matmul(both_ref[...], dose, NT)
    scores = scores[:rows] + scores[rows:] - offset_ref[...]
    pair = jnp.concatenate(split2(scores), axis=0)
    sums = matmul(pair, dose, NN)
    out_ref[...] += sums[:rows] + sums[rows:]


def second_product(half, table, product, dose, tile=512):
    people, width = dose.shape
    rows = 2 * ROWS1
    return pl.pallas_call(
        second_kernel,
        grid=(people // tile,),
        in_specs=[
            pl.BlockSpec(memory_space=pltpu.SMEM),
            pl.BlockSpec((8, width), lambda i: (0, 0)),
            pl.BlockSpec((ROWS0, width), lambda i: (0, 0)),
            pl.BlockSpec((tile, width), lambda i: (i, 0)),
        ],
        out_specs=pl.BlockSpec((rows, width), lambda i: (0, 0)),
        out_shape=jax.ShapeDtypeStruct((rows, width), jnp.float32),
        scratch_shapes=[
            pltpu.VMEM((rows, width), jnp.float32),
            pltpu.VMEM((2 * rows, width), jnp.bfloat16),
            pltpu.VMEM((rows, 1), jnp.float32),
        ],
        compiler_params=pltpu.CompilerParams(vmem_limit_bytes=VMEM),
        cost_estimate=pl.CostEstimate(
            flops=8 * people * width * rows, bytes_accessed=2 * people * width, transcendentals=0
        ),
    )(half, table, product, dose)


def predict_kernel(
    core_ref, own_ref, other_ref, table_ref, pheno_ref, fold_ref, dose_ref,
    coeff_out, number_out, score_out, coeff_ref, wide_ref, weight_ref, offset_ref,
):
    half, width = own_ref.shape

    @pl.when(pl.program_id(0) == 0)
    def _():
        def place(first_ref, second_ref):
            for lane in range(width // 128):
                lanes = slice(lane * 128, (lane + 1) * 128)
                coeff_ref[lane, 0:half] = first_ref[:, lanes]
                coeff_ref[lane, half:] = second_ref[:, lanes]
            for group in range(SHRINKS):
                ref = first_ref if group < 2 else second_ref
                start = group % 2 * ROWS1
                coeff_out[group * BASE : (group + 1) * BASE] = ref[start : start + BASE]

        @pl.when(core_ref[0] == 0)
        def _():
            place(own_ref, other_ref)

        @pl.when(core_ref[0] != 0)
        def _():
            place(other_ref, own_ref)

        for lane in range(width // 128):
            lanes = slice(lane * 128, (lane + 1) * 128)
            for fold in range(FOLDS):
                for group in range(SHRINKS):
                    first = fold * LEVELS + group * LAMBDAS
                    rows = pl.ds(group * ROWS1 + fold, LAMBDAS, FOLDS)
                    wide_ref[first : first + LAMBDAS, lanes] = coeff_ref[lane, rows]
        table = table_ref[...]
        for fold in range(FOLDS):
            span = slice(fold * LEVELS, (fold + 1) * LEVELS)
            weighted = (wide_ref[span] / table[6:7]).astype(jnp.bfloat16)
            weight_ref[span] = weighted
            wide = weighted.astype(jnp.float32)
            offset_ref[span] = jnp.sum(wide * table[5:6], axis=1, keepdims=True)
            number_out[span] = jnp.sum(wide * pheno_ref[fold : fold + 1], axis=1, keepdims=True)

    scores = matmul(weight_ref[...], dose_ref[...], NT) - offset_ref[...]
    folds = fold_ref[...]
    out = scores[0:LEVELS]
    for fold in range(1, FOLDS):
        out = jnp.where(folds == fold, scores[fold * LEVELS : (fold + 1) * LEVELS], out)
    score_out[0] = out


def predict(core, own, other, table, pheno, fold_ids, dose, parts):
    people, width = dose.shape
    half = own.shape[0]
    tile = people // parts
    whole = lambda rows: pl.BlockSpec((rows, width), lambda i: (0, 0))
    return pl.pallas_call(
        predict_kernel,
        grid=(parts,),
        in_specs=[
            pl.BlockSpec(memory_space=pltpu.SMEM),
            whole(half),
            whole(half),
            whole(8),
            whole(FOLDS),
            pl.BlockSpec((1, tile), lambda i: (0, i)),
            pl.BlockSpec((tile, width), lambda i: (i, 0)),
        ],
        out_specs=[
            whole(GRID),
            pl.BlockSpec((GRID, 1), lambda i: (0, 0)),
            pl.BlockSpec((1, LEVELS, tile), lambda i: (i, 0, 0)),
        ],
        out_shape=[
            jax.ShapeDtypeStruct((GRID, width), jnp.float32),
            jax.ShapeDtypeStruct((GRID, 1), jnp.float32),
            jax.ShapeDtypeStruct((parts, LEVELS, tile), jnp.float32),
        ],
        scratch_shapes=[
            pltpu.VMEM((width // 128, 2 * half, 128), jnp.float32),
            pltpu.VMEM((GRID, width), jnp.float32),
            pltpu.VMEM((GRID, width), jnp.bfloat16),
            pltpu.VMEM((GRID, 1), jnp.float32),
        ],
        compiler_params=pltpu.CompilerParams(vmem_limit_bytes=VMEM),
    )(core, own, other, table, pheno, fold_ids.reshape(1, people), dose)


def local(genotypes, phenotype, fold_ids):
    num_rows, block_width = genotypes.shape
    samp, blk = lax.axis_index("samp"), lax.axis_index("blk")
    core, place = samp & 1, (samp >> 1) & 3

    onehot = fold_ids[None, :] == jnp.arange(FOLDS)[:, None]
    pheno_split = jnp.where(onehot, phenotype[None, :], 0.0)
    high = rounded(pheno_split)
    mid = rounded(pheno_split - high)
    low = pheno_split - high - mid
    ones = jnp.ones((1, num_rows), jnp.float32)
    left = jnp.concatenate([high, mid, low, ones], axis=0).astype(jnp.bfloat16)
    dose, parts, squares = prepare(left, genotypes)
    counts = jnp.sum(onehot.astype(jnp.float32), axis=1)
    fold_sum = jnp.sum(pheno_split, axis=1)
    extra = jnp.concatenate([counts, fold_sum, jnp.zeros((block_width - 2 * FOLDS,), jnp.float32)])
    stats = jnp.concatenate(
        [
            parts[:5] + parts[5:10] + parts[10:15],
            parts[15:16],
            jnp.sum(squares, axis=0, keepdims=True),
            extra[None],
        ],
        axis=0,
    )
    stats = all_sum(stats, SAMP_BITS)
    geno_pheno = stats[:FOLDS]
    fold_count = stats[7, :FOLDS][:, None]
    fold_pheno_sum = stats[7, FOLDS : 2 * FOLDS][:, None]
    snp_mean = stats[5:6] / PEOPLE
    scales = jnp.sqrt(stats[6:7] / PEOPLE - snp_mean * snp_mean + epsilon)
    train_geno = jnp.sum(geno_pheno, axis=0, keepdims=True) - geno_pheno
    train_pheno = jnp.sum(fold_pheno_sum) - fold_pheno_sum
    zscore = (train_geno - train_pheno * snp_mean) / (scales * jnp.sqrt(PEOPLE - fold_count))
    table = jnp.concatenate([zscore, snp_mean, scales, 1.0 / scales], axis=0)

    part = first_product(table, dose)
    rows = ROWS0 // 2
    kept = lax.dynamic_slice_in_dim(part, core * rows, rows, 0)
    sent = lax.dynamic_slice_in_dim(part, (1 - core) * rows, rows, 0)
    piece = scatter_chips(kept + swap(sent, "samp", 1), place)
    own = gather_chips(piece, place)
    other = swap(own, "samp", 1)
    first = core == 0
    product = jnp.concatenate([jnp.where(first, own, other), jnp.where(first, other, own)], axis=0)

    sent = second_product((1 - core)[None], table, product, dose)
    sent = swap(sent, "samp", 1)
    kept = second_product(core[None], table, product, dose)
    piece = scatter_chips(kept + sent, place)
    width = block_width // 4
    here = lambda a: lax.dynamic_slice_in_dim(a, place * width, width, 1)
    row, fold_of, cutoff = base_rows(ROWS1)
    table_here = here(table)
    target = spread(table_here[:FOLDS], fold_of)
    coeff = soft_threshold(step_size * target, cutoff)
    scale_here = table_here[7:8] / PEOPLE
    old = here(product[:ROWS1]) * scale_here
    final = []
    for group in range(2):
        shrink = shrink_unit * (2 * core + group + 1).astype(jnp.float32)
        new = next_coeff(coeff, old, target, shrink, cutoff)
        latest = piece[group * ROWS1 : (group + 1) * ROWS1] * scale_here
        final.append(next_coeff(new, latest, target, shrink, cutoff))
    own = gather_chips(jnp.concatenate(final, axis=0), place)
    other = swap(own, "samp", 1)

    centred_pheno = geno_pheno - snp_mean * fold_pheno_sum
    blocks = lax.axis_size("blk")
    coeff_all, numerator, scores = predict(core[None], own, other, table, centred_pheno, fold_ids, dose, blocks)
    scores = jnp.sum(lax.all_to_all(scores, "blk", 0, 0, tiled=True), axis=0)
    people = num_rows // blocks
    folds_here = lax.dynamic_slice_in_dim(fold_ids, blk * people, people, 0)
    square = scores * scores
    denominator = jnp.stack(
        [jnp.sum(jnp.where((folds_here == fold)[None, :], square, 0.0), axis=1) for fold in range(FOLDS)]
    )
    sums = jnp.stack([numerator.reshape(FOLDS, LEVELS) / lax.axis_size("samp"), denominator])
    sums = all_sum(sums, SAMP_BITS + (("blk", (4,)), ("blk", (1, 2, 3))))
    sums = sums * jnp.array([1.0 / math.sqrt(SNPS), 1.0 / SNPS], jnp.float32)[:, None, None] / fold_count[None]
    fold_scores = sums.transpose(0, 2, 1).reshape(2, GRID)
    return (coeff_all.T, fold_scores)


def solution(mesh):
    return jax.shard_map(
        local,
        mesh=mesh,
        in_specs=(P("samp", "blk"), P("samp"), P("samp")),
        out_specs=(P("blk", None), P()),
        check_vma=False,
    )
```

time: 423 us -> 205 us (0.48)
  waiting for transfers between devices: 224 us -> 80.5 us
  blocking collectives: 108 us -> 0 us
  matrix products: 54 us -> 0 us
  starting transfers between devices: 0.3 us -> 53.2 us
  Pallas kernels: 0 us -> 51.8 us
  between operations: 13.9 us -> 0.94 us
  other arithmetic: 18.2 us -> 13.1 us
    psum x2 -> x0, waiting for transfers between devices: 172 us -> none  [the longest x1 90.3 us: local(): predicted = lax.psum(partial_value, 'blk') / root_snps]
    psum x2 -> x0, blocking collectives: 108 us -> none  [the longest x1 71.7 us: local(): lax.psum((gram_local, local_sum, local_sq, local_geno_pheno, local_pheno_...]
    ppermute x0 -> x32, waiting for transfers between devices: none -> 69.7 us  [swap(): return lax.ppermute(values, axis, [(i, i ^ bit) for i in range(size)])]
    dot_general x6 -> x0, matrix products: 54 us -> none  [the longest x1 19 us: local(): jnp.dot(dosage_bf.T, dosage_bf, preferred_element_type=jnp.float32)]
    all_gather x1 -> x0, waiting for transfers between devices: 52.5 us -> none  [local(): coeff_all = lax.all_gather(coeffs, 'samp', axis=1, tiled=True)]
    pallas_call x0 -> x5, Pallas kernels: none -> 51.8 us  [the longest x2 20.7 us: second_product(): pl.pallas_call(second_kernel, grid=(people // tile,), in_specs=[pl.BlockS...]
    ppermute x0 -> x32, starting transfers between devices: none -> 48.2 us  [swap(): return lax.ppermute(values, axis, [(i, i ^ bit) for i in range(size)])]
    all_to_all x0 -> x1, waiting for transfers between devices: none -> 10.8 us  [local(): scores = jnp.sum(lax.all_to_all(scores, 'blk', 0, 0, tiled=True), axis=0)]
  transfers between devices with their start and end apart: 3 -> 33, of which waited for: 3 -> 27; matrix products, arithmetic and copies ran while one was open for 4% -> 1% of each run, Pallas kernels for 0% -> 5%
where the time goes in v2:
time: 205 us; the launch traced here: 204 us
  waiting for transfers between devices  80.5 us (39%)
  starting transfers between devices  53.2 us (26%)
  Pallas kernels  51.8 us (25%)
  other arithmetic  13.1 us (6%)
  local copies, waits for them, and re-layouts  4.36 us (2%)
    ppermute x32, waiting for transfers between devices, swap(): return lax.ppermute(values, axis, [(i, i ^ bit) for i in range(size)])  69.7 us
    ppermute x32, starting transfers between devices, swap(): return lax.ppermute(values, axis, [(i, i ^ bit) for i in range(size)])  48.2 us
    pallas_call x2, Pallas kernels, second_product(): pl.pallas_call(second_kernel, grid=(people // tile,), in_specs=[pl.BlockS...  20.7 us
    all_to_all x1, waiting for transfers between devices, local(): scores = jnp.sum(lax.all_to_all(scores, 'blk', 0, 0, tiled=True), axis=0)  10.8 us
    pallas_call x1, Pallas kernels, predict(): pl.pallas_call(predict_kernel, grid=(parts,), in_specs=[pl.BlockSpec(memo...  10.6 us
    pallas_call x1, Pallas kernels, first_product(): pl.pallas_call(first_kernel, grid=(people // tile,), in_specs=[pl.BlockSp...  10.6 us
    pallas_call x1, Pallas kernels, prepare(): pl.pallas_call(prepare_kernel, grid=(people // tile,), in_specs=[pl.Block...  9.86 us
    all_to_all x1, starting transfers between devices, local(): scores = jnp.sum(lax.all_to_all(scores, 'blk', 0, 0, tiled=True), axis=0)  5.02 us
  transfers between devices with their start and end apart: 33, of which 27 were waited for; matrix products, arithmetic and copies ran while one was open for 1% of the time, Pallas kernels for 5%

profile of v2, /device:TPU:0, one launch (start us, length us, event | category | flops | bytes accessed | tf_op | source)
XLA Modules:
  0.0 203.9 jit_solution(9218015804013458607)
XLA Ops:
  2.3 9.9 %shard_map.59 = (bf16[2048,1536]{1,0:T(8,128)(2,1)}, f32[16,1536]{1,0:T(8,128)}, f32[8,1536]{1,0:T(8,128)}) custom-call(bf16[16,2048]{1,0:T(8,128)(2,1)} %maximum_maximum_fusion.left_ref, s32[2048,1536]{1,0:T(8,128)} %geno_ref.1), custom_call_target="tpu_custom_call" | custom-call | tf_op jit(solution)/shard_map/pallas_call | solution.py:103
  16.2 4.0 %collective-permute-start.1 = (f32[8,1536]{1,0:T(8,128)S(1)}, f32[8,1536]{1,0:T(8,128)S(1)}, u32[]{:S(2)}, u32[]{:S(2)}) collective-permute-start(f32[8,1536]{1,0:T(8,128)S(1)} %fusion.25), channel_id=1, source_target_pairs={{0,64},{8,72},{16,80},{24,88},{32,96},{40,104},{48,112},{56,120},{... | collective-permute-start | bytes 147464 | tf_op jit(solution)/shard_map/ppermute | solution.py:44
  20.2 2.1 %collective-permute-done.1 = f32[8,1536]{1,0:T(8,128)S(1)} collective-permute-done((f32[8,1536]{1,0:T(8,128)S(1)}, f32[8,1536]{1,0:T(8,128)S(1)}, u32[]{:S(2)}, u32[]{:S(2)}) %collective-permute-start.1) | collective-permute-done | bytes 49184 | tf_op jit(solution)/shard_map/ppermute | solution.py:44
  23.9 2.7 %collective-permute-start.3 = (f32[8,1536]{1,0:T(8,128)S(1)}, f32[8,1536]{1,0:T(8,128)S(1)}, u32[]{:S(2)}, u32[]{:S(2)}) collective-permute-start(f32[8,1536]{1,0:T(8,128)S(1)} %add.171), channel_id=1, source_target_pairs={{0,32},{8,40},{16,48},{24,56},{32,0},{40,8},{48,16},{56,24},{64,96... | collective-permute-start | bytes 147464 | tf_op jit(solution)/shard_map/ppermute | solution.py:44
  27.1 2.4 %collective-permute-done.3 = f32[8,1536]{1,0:T(8,128)S(1)} collective-permute-done((f32[8,1536]{1,0:T(8,128)S(1)}, f32[8,1536]{1,0:T(8,128)S(1)}, u32[]{:S(2)}, u32[]{:S(2)}) %collective-permute-start.3) | collective-permute-done | bytes 49184 | tf_op jit(solution)/shard_map/ppermute | solution.py:44
  29.5 2.4 %collective-permute-done.4 = f32[8,1536]{1,0:T(8,128)S(1)} collective-permute-done((f32[8,1536]{1,0:T(8,128)S(1)}, f32[8,1536]{1,0:T(8,128)S(1)}, u32[]{:S(2)}, u32[]{:S(2)}) %collective-permute-start.4) | collective-permute-done | bytes 49184 | tf_op jit(solution)/shard_map/ppermute | solution.py:44
  34.7 10.6 %shard_map.60 = f32[112,1536]{1,0:T(8,128)} custom-call(f32[8,1536]{1,0:T(8,128)} %pad_maximum_fusion.5.table_ref, bf16[2048,1536]{1,0:T(8,128)(2,1)} %get-tuple-element.10.dose_ref), custom_call_target="tpu_custom_call" | custom-call | tf_op jit(solution)/shard_map/pallas_call | solution.py:180
  51.2 2.8 %collective-permute-start.8 = (f32[56,384]{1,0:T(8,128)S(1)}, f32[56,384]{1,0:T(8,128)S(1)}, u32[]{:S(2)}, u32[]{:S(2)}) collective-permute-start(f32[56,384]{1,0:T(8,128)S(1)} %get-tuple-element.43), channel_id=1, source_target_pairs={{0,48},{8,56},{16,32},{24,40},{32,16},{40,24},{48,0},{56,8},{64,11... | collective-permute-start | bytes 258056 | tf_op jit(solution)/shard_map/ppermute | solution.py:44
  57.4 3.6 %collective-permute-start.9 = (f32[56,384]{1,0:T(8,128)S(1)}, f32[56,384]{1,0:T(8,128)S(1)}, u32[]{:S(2)}, u32[]{:S(2)}) collective-permute-start(f32[56,384]{1,0:T(8,128)S(1)} %add_add_fusion.1), channel_id=1, source_target_pairs={{0,64},{8,72},{16,80},{24,88},{32,96},{40,104},{48,112},{56,120},{... | collective-permute-start | bytes 258056 | tf_op jit(solution)/shard_map/ppermute | solution.py:44
  61.0 2.5 %collective-permute-done.9 = f32[56,384]{1,0:T(8,128)S(1)} collective-permute-done((f32[56,384]{1,0:T(8,128)S(1)}, f32[56,384]{1,0:T(8,128)S(1)}, u32[]{:S(2)}, u32[]{:S(2)}) %collective-permute-start.9) | collective-permute-done | bytes 86048 | tf_op jit(solution)/shard_map/ppermute | solution.py:44
  63.5 2.8 %collective-permute-start.10 = (f32[56,384]{1,0:T(8,128)S(1)}, f32[56,384]{1,0:T(8,128)S(1)}, u32[]{:S(2)}, u32[]{:S(2)}) collective-permute-start(f32[56,384]{1,0:T(8,128)S(1)} %add.188), channel_id=1, source_target_pairs={{0,48},{8,56},{16,32},{24,40},{32,16},{40,24},{48,0},{56,8},{64,11... | collective-permute-start | bytes 258056 | tf_op jit(solution)/shard_map/ppermute | solution.py:44
  67.7 2.5 %collective-permute-done.10 = f32[56,384]{1,0:T(8,128)S(1)} collective-permute-done((f32[56,384]{1,0:T(8,128)S(1)}, f32[56,384]{1,0:T(8,128)S(1)}, u32[]{:S(2)}, u32[]{:S(2)}) %collective-permute-start.10) | collective-permute-done | bytes 86048 | tf_op jit(solution)/shard_map/ppermute | solution.py:44
  70.2 2.1 %collective-permute-done.11 = f32[56,384]{1,0:T(8,128)S(1)} collective-permute-done((f32[56,384]{1,0:T(8,128)S(1)}, f32[56,384]{1,0:T(8,128)S(1)}, u32[]{:S(2)}, u32[]{:S(2)}) %collective-permute-start.11) | collective-permute-done | bytes 86048 | tf_op jit(solution)/shard_map/ppermute | solution.py:44
  75.1 10.4 %shard_map.62 = f32[208,1536]{1,0:T(8,128)} custom-call(s32[1]{0:T(128)} %bitcast.3.half_ref, f32[8,1536]{1,0:T(8,128)} %pad_maximum_fusion.5.table_ref, f32[112,1536]{1,0:T(8,128)} %pad_maximum_fusion.1.product_ref, bf16[2048,1536]{1,0:T(8,128)(2,1)} %get-tuple-element.10.dose_ref), custom_call_target="tpu_custom_call" | custom-call | flops 5234491392 | bytes 6291456 | tf_op jit(solution)/shard_map/pallas_call | solution.py:227
  85.6 10.4 %shard_map.61 = f32[208,1536]{1,0:T(8,128)} custom-call(s32[1]{0:T(128)} %bitcast.half_ref.core_ref, f32[8,1536]{1,0:T(8,128)} %pad_maximum_fusion.5.table_ref, f32[112,1536]{1,0:T(8,128)} %pad_maximum_fusion.1.product_ref, bf16[2048,1536]{1,0:T(8,128)(2,1)} %get-tuple-element.10.dose_ref), custom_call_target="tpu_custom_call" | custom-call | flops 5234491392 | bytes 6291456 | tf_op jit(solution)/shard_map/pallas_call | solution.py:227
  97.9 2.9 %collective-permute-start.16 = (f32[208,384]{1,0:T(8,128)S(1)}, f32[208,384]{1,0:T(8,128)S(1)}, u32[]{:S(2)}, u32[]{:S(2)}) collective-permute-start(f32[208,384]{1,0:T(8,128)S(1)} %get-tuple-element.35), channel_id=1, source_target_pairs={{0,32},{8,40},{16,48},{24,56},{32,0},{40,8},{48,16},{56,24},{64,96... | collective-permute-start | bytes 958472 | tf_op jit(solution)/shard_map/ppermute | solution.py:44
  102.6 5.6 %collective-permute-done.15 = f32[208,384]{1,0:T(8,128)S(1)} collective-permute-done((f32[208,384]{1,0:T(8,128)S(1)}, f32[208,384]{1,0:T(8,128)S(1)}, u32[]{:S(2)}, u32[]{:S(2)}) %collective-permute-start.15) | collective-permute-done | bytes 319520 | tf_op jit(solution)/shard_map/ppermute | solution.py:44
  108.2 7.3 %collective-permute-done.16 = f32[208,384]{1,0:T(8,128)S(1)} collective-permute-done((f32[208,384]{1,0:T(8,128)S(1)}, f32[208,384]{1,0:T(8,128)S(1)}, u32[]{:S(2)}, u32[]{:S(2)}) %collective-permute-start.16) | collective-permute-done | bytes 319520 | tf_op jit(solution)/shard_map/ppermute | solution.py:44
  115.6 2.6 %collective-permute-done.17 = f32[208,384]{1,0:T(8,128)S(1)} collective-permute-done((f32[208,384]{1,0:T(8,128)S(1)}, f32[208,384]{1,0:T(8,128)S(1)}, u32[]{:S(2)}, u32[]{:S(2)}) %collective-permute-start.17) | collective-permute-done | bytes 319520 | tf_op jit(solution)/shard_map/ppermute | solution.py:44
  118.2 3.6 %collective-permute-start.18 = (f32[208,384]{1,0:T(8,128)S(1)}, f32[208,384]{1,0:T(8,128)S(1)}, u32[]{:S(2)}, u32[]{:S(2)}) collective-permute-start(f32[208,384]{1,0:T(8,128)S(1)} %add_add_fusion), channel_id=1, source_target_pairs={{0,64},{8,72},{16,80},{24,88},{32,96},{40,104},{48,112},{56,120},{... | collective-permute-start | bytes 958472 | tf_op jit(solution)/shard_map/ppermute | solution.py:44
  123.0 5.4 %collective-permute-done.18 = f32[208,384]{1,0:T(8,128)S(1)} collective-permute-done((f32[208,384]{1,0:T(8,128)S(1)}, f32[208,384]{1,0:T(8,128)S(1)}, u32[]{:S(2)}, u32[]{:S(2)}) %collective-permute-start.18) | collective-permute-done | bytes 319520 | tf_op jit(solution)/shard_map/ppermute | solution.py:44
  130.9 2.3 %collective-permute-start.21 = (f32[208,384]{1,0:T(8,128)S(1)}, f32[208,384]{1,0:T(8,128)S(1)}, u32[]{:S(2)}, u32[]{:S(2)}) collective-permute-start(f32[208,384]{1,0:T(8,128)S(1)} %pad_maximum_fusion.3), channel_id=1, source_target_pairs={{0,16},{8,24},{16,0},{24,8},{32,48},{40,56},{48,32},{56,40},{64,80... | collective-permute-start | bytes 958472 | tf_op jit(solution)/shard_map/ppermute | solution.py:44
  133.2 11.7 %collective-permute-done.19 = f32[208,384]{1,0:T(8,128)S(1)} collective-permute-done((f32[208,384]{1,0:T(8,128)S(1)}, f32[208,384]{1,0:T(8,128)S(1)}, u32[]{:S(2)}, u32[]{:S(2)}) %collective-permute-start.19) | collective-permute-done | bytes 319520 | tf_op jit(solution)/shard_map/ppermute | solution.py:44
  145.9 3.0 %collective-permute-done.22.other_ref = f32[208,1536]{1,0:T(8,128)S(1)} collective-permute-done((f32[208,1536]{1,0:T(8,128)S(1)}, f32[208,1536]{1,0:T(8,128)S(1)}, u32[]{:S(2)}, u32[]{:S(2)}) %collective-permute-start.22) | collective-permute-done | bytes 1277984 | tf_op jit(solution)/shard_map/ppermute | solution.py:44
  150.0 10.6 %shard_map.63 = (f32[400,1536]{1,0:T(8,128)}, f32[400,1]{1,0:T(8,128)}, f32[8,80,256]{2,1,0:T(8,128)}) custom-call(s32[1]{0:T(128)} %bitcast.half_ref.core_ref, f32[208,1536]{1,0:T(8,128)} %copy-done, f32[208,1536]{1,0:T(8,128)} %copy-done.1, f32[8,1536]{1,0:T(8,128)} %pad_maximum_fusion.5.table_ref, f32[5,1536]{1,0:T(8,128)} %get-tuple-element.45.pheno_ref, ...), custom_call_target="tpu_custom_call" | custom-call | tf_op jit(solution)/shard_map/pallas_call | solution.py:305
  160.6 5.0 %all-to-all-start = ((f32[8,80,256]{2,1,0:T(8,128)}), f32[8,80,256]{2,1,0:T(8,128)S(1)}, u32[]{:S(2)}, u32[]{:S(2)}) async-start(f32[8,80,256]{2,1,0:T(8,128)} %get-tuple-element.13), calls=%async_computation | async-start | bytes 1310720 | tf_op jit(solution)/shard_map/all_to_all | solution.py:407
  166.7 10.8 %all-to-all-done = f32[8,80,256]{2,1,0:T(8,128)S(1)} async-done(((f32[8,80,256]{2,1,0:T(8,128)}), f32[8,80,256]{2,1,0:T(8,128)S(1)}, u32[]{:S(2)}, u32[]{:S(2)}) %all-to-all-start) | async-done | bytes 655392 | tf_op jit(solution)/shard_map/all_to_all | solution.py:407
  179.0 3.6 %collective-permute-start.24 = (f32[2,5,80]{2,1,0:T(8,128)S(1)}, f32[2,5,80]{2,1,0:T(8,128)S(1)}, u32[]{:S(2)}, u32[]{:S(2)}) collective-permute-start(f32[2,5,80]{2,1,0:T(8,128)S(1)} %fusion.21), channel_id=1, source_target_pairs={{0,64},{8,72},{16,80},{24,88},{32,96},{40,104},{48,112},{56,120},{... | collective-permute-start | bytes 9608 | tf_op jit(solution)/shard_map/ppermute | solution.py:44
  184.2 3.2 %collective-permute-start.26 = (f32[2,5,80]{2,1,0:T(8,128)S(1)}, f32[2,5,80]{2,1,0:T(8,128)S(1)}, u32[]{:S(2)}, u32[]{:S(2)}) collective-permute-start(f32[2,5,80]{2,1,0:T(8,128)S(1)} %fusion.24), channel_id=1, source_target_pairs={{0,32},{8,40},{16,48},{24,56},{32,0},{40,8},{48,16},{56,24},{64,96... | collective-permute-start | bytes 9608 | tf_op jit(solution)/shard_map/ppermute | solution.py:44
  189.5 2.9 %collective-permute-done.27 = f32[2,5,80]{2,1,0:T(8,128)S(1)} collective-permute-done((f32[2,5,80]{2,1,0:T(8,128)S(1)}, f32[2,5,80]{2,1,0:T(8,128)S(1)}, u32[]{:S(2)}, u32[]{:S(2)}) %collective-permute-start.27) | collective-permute-done | bytes 3232 | tf_op jit(solution)/shard_map/ppermute | solution.py:44
  192.8 3.1 %collective-permute-done.28 = f32[2,5,80]{2,1,0:T(8,128)S(1)} collective-permute-done((f32[2,5,80]{2,1,0:T(8,128)S(1)}, f32[2,5,80]{2,1,0:T(8,128)S(1)}, u32[]{:S(2)}, u32[]{:S(2)}) %collective-permute-start.28) | collective-permute-done | bytes 3232 | tf_op jit(solution)/shard_map/ppermute | solution.py:44
  198.0 2.7 %collective-permute-start.31 = (f32[2,5,80]{2,1,0:T(8,128)S(1)}, f32[2,5,80]{2,1,0:T(8,128)S(1)}, u32[]{:S(2)}, u32[]{:S(2)}) collective-permute-start(f32[2,5,80]{2,1,0:T(8,128)S(1)} %add.205), channel_id=1, source_target_pairs={{0,3},{1,2},{2,1},{3,0},{4,7},{5,6},{6,5},{7,4},{8,11},{9,10},{10,... | collective-permute-start | bytes 9608 | tf_op jit(solution)/shard_map/ppermute | solution.py:44
  (105 shorter events, 45.4 us)
Async XLA Ops:
  14.8 1.3 collective-permute-start
  16.2 6.1 %collective-permute-start.1 = (f32[8,1536]{1,0:T(8,128)S(1)}, f32[8,1536]{1,0:T(8,128)S(1)}, u32[]{:S(2)}, u32[]{:S(2)}) collective-permute-start(f32[8,1536]{1,0:T(8,128)S(1)} %fusion.25), channel_id=1, source_target_pairs={{0,64},{8,72},{16,80},{24,88},{32,96},{40,104},{48,112},{56,120},{... | collective-permute-start | bytes 147464 | tf_op jit(solution)/shard_map/ppermute | solution.py:44
  22.3 4.8 %collective-permute-start.2 = (f32[8,1536]{1,0:T(8,128)S(1)}, f32[8,1536]{1,0:T(8,128)S(1)}, u32[]{:S(2)}, u32[]{:S(2)}) collective-permute-start(f32[8,1536]{1,0:T(8,128)S(1)} %add.171), channel_id=1, source_target_pairs={{0,16},{8,24},{16,0},{24,8},{32,48},{40,56},{48,32},{56,40},{64,80... | collective-permute-start | bytes 147464 | tf_op jit(solution)/shard_map/ppermute | solution.py:44
  23.9 5.6 %collective-permute-start.3 = (f32[8,1536]{1,0:T(8,128)S(1)}, f32[8,1536]{1,0:T(8,128)S(1)}, u32[]{:S(2)}, u32[]{:S(2)}) collective-permute-start(f32[8,1536]{1,0:T(8,128)S(1)} %add.171), channel_id=1, source_target_pairs={{0,32},{8,40},{16,48},{24,56},{32,0},{40,8},{48,16},{56,24},{64,96... | collective-permute-start | bytes 147464 | tf_op jit(solution)/shard_map/ppermute | solution.py:44
  26.6 5.3 %collective-permute-start.4 = (f32[8,1536]{1,0:T(8,128)S(1)}, f32[8,1536]{1,0:T(8,128)S(1)}, u32[]{:S(2)}, u32[]{:S(2)}) collective-permute-start(f32[8,1536]{1,0:T(8,128)S(1)} %add.171), channel_id=1, source_target_pairs={{0,48},{8,56},{16,32},{24,40},{32,16},{40,24},{48,0},{56,8},{64,11... | collective-permute-start | bytes 147464 | tf_op jit(solution)/shard_map/ppermute | solution.py:44
  46.3 1.7 collective-permute-start.5
  49.1 5.5 %collective-permute-start.6 = (f32[56,384]{1,0:T(8,128)S(1)}, f32[56,384]{1,0:T(8,128)S(1)}, u32[]{:S(2)}, u32[]{:S(2)}) collective-permute-start(f32[56,384]{1,0:T(8,128)S(1)} %get-tuple-element.42), channel_id=1, source_target_pairs={{0,16},{8,24},{16,0},{24,8},{32,48},{40,56},{48,32},{56,40},{64,80... | collective-permute-start | bytes 258056 | tf_op jit(solution)/shard_map/ppermute | solution.py:44
  49.2 6.4 %collective-permute-start.7 = (f32[56,384]{1,0:T(8,128)S(1)}, f32[56,384]{1,0:T(8,128)S(1)}, u32[]{:S(2)}, u32[]{:S(2)}) collective-permute-start(f32[56,384]{1,0:T(8,128)S(1)} %get-tuple-element.44), channel_id=1, source_target_pairs={{0,32},{8,40},{16,48},{24,56},{32,0},{40,8},{48,16},{56,24},{64,96... | collective-permute-start | bytes 258056 | tf_op jit(solution)/shard_map/ppermute | solution.py:44
  51.2 6.2 %collective-permute-start.8 = (f32[56,384]{1,0:T(8,128)S(1)}, f32[56,384]{1,0:T(8,128)S(1)}, u32[]{:S(2)}, u32[]{:S(2)}) collective-permute-start(f32[56,384]{1,0:T(8,128)S(1)} %get-tuple-element.43), channel_id=1, source_target_pairs={{0,48},{8,56},{16,32},{24,40},{32,16},{40,24},{48,0},{56,8},{64,11... | collective-permute-start | bytes 258056 | tf_op jit(solution)/shard_map/ppermute | solution.py:44
  57.4 6.1 %collective-permute-start.9 = (f32[56,384]{1,0:T(8,128)S(1)}, f32[56,384]{1,0:T(8,128)S(1)}, u32[]{:S(2)}, u32[]{:S(2)}) collective-permute-start(f32[56,384]{1,0:T(8,128)S(1)} %add_add_fusion.1), channel_id=1, source_target_pairs={{0,64},{8,72},{16,80},{24,88},{32,96},{40,104},{48,112},{56,120},{... | collective-permute-start | bytes 258056 | tf_op jit(solution)/shard_map/ppermute | solution.py:44
  63.5 6.7 %collective-permute-start.10 = (f32[56,384]{1,0:T(8,128)S(1)}, f32[56,384]{1,0:T(8,128)S(1)}, u32[]{:S(2)}, u32[]{:S(2)}) collective-permute-start(f32[56,384]{1,0:T(8,128)S(1)} %add.188), channel_id=1, source_target_pairs={{0,48},{8,56},{16,32},{24,40},{32,16},{40,24},{48,0},{56,8},{64,11... | collective-permute-start | bytes 258056 | tf_op jit(solution)/shard_map/ppermute | solution.py:44
  66.3 6.0 %collective-permute-start.11 = (f32[56,384]{1,0:T(8,128)S(1)}, f32[56,384]{1,0:T(8,128)S(1)}, u32[]{:S(2)}, u32[]{:S(2)}) collective-permute-start(f32[56,384]{1,0:T(8,128)S(1)} %add.188), channel_id=1, source_target_pairs={{0,32},{8,40},{16,48},{24,56},{32,0},{40,8},{48,16},{56,24},{64,96... | collective-permute-start | bytes 258056 | tf_op jit(solution)/shard_map/ppermute | solution.py:44
  66.3 6.0 %collective-permute-start.12 = (f32[56,384]{1,0:T(8,128)S(1)}, f32[56,384]{1,0:T(8,128)S(1)}, u32[]{:S(2)}, u32[]{:S(2)}) collective-permute-start(f32[56,384]{1,0:T(8,128)S(1)} %add.188), channel_id=1, source_target_pairs={{0,16},{8,24},{16,0},{24,8},{32,48},{40,56},{48,32},{56,40},{64,80... | collective-permute-start | bytes 258056 | tf_op jit(solution)/shard_map/ppermute | solution.py:44
  72.4 1.7 collective-permute-start.13
  85.5 10.5 %collective-permute-start.14 = (f32[208,1536]{1,0:T(8,128)}, f32[208,1536]{1,0:T(8,128)S(1)}, u32[]{:S(2)}, u32[]{:S(2)}) collective-permute-start(f32[208,1536]{1,0:T(8,128)} %shard_map.62), channel_id=1, source_target_pairs={{0,8},{8,0},{16,24},{24,16},{32,40},{40,32},{48,56},{56,48},{64,72... | collective-permute-start | bytes 3833864 | tf_op jit(solution)/shard_map/ppermute | solution.py:44
  97.6 10.6 %collective-permute-start.15 = (f32[208,384]{1,0:T(8,128)S(1)}, f32[208,384]{1,0:T(8,128)S(1)}, u32[]{:S(2)}, u32[]{:S(2)}) collective-permute-start(f32[208,384]{1,0:T(8,128)S(1)} %get-tuple-element.33), channel_id=1, source_target_pairs={{0,16},{8,24},{16,0},{24,8},{32,48},{40,56},{48,32},{56,40},{64,80... | collective-permute-start | bytes 958472 | tf_op jit(solution)/shard_map/ppermute | solution.py:44
  97.9 17.7 %collective-permute-start.16 = (f32[208,384]{1,0:T(8,128)S(1)}, f32[208,384]{1,0:T(8,128)S(1)}, u32[]{:S(2)}, u32[]{:S(2)}) collective-permute-start(f32[208,384]{1,0:T(8,128)S(1)} %get-tuple-element.35), channel_id=1, source_target_pairs={{0,32},{8,40},{16,48},{24,56},{32,0},{40,8},{48,16},{56,24},{64,96... | collective-permute-start | bytes 958472 | tf_op jit(solution)/shard_map/ppermute | solution.py:44
  100.8 17.3 %collective-permute-start.17 = (f32[208,384]{1,0:T(8,128)S(1)}, f32[208,384]{1,0:T(8,128)S(1)}, u32[]{:S(2)}, u32[]{:S(2)}) collective-permute-start(f32[208,384]{1,0:T(8,128)S(1)} %get-tuple-element.34), channel_id=1, source_target_pairs={{0,48},{8,56},{16,32},{24,40},{32,16},{40,24},{48,0},{56,8},{64,11... | collective-permute-start | bytes 958472 | tf_op jit(solution)/shard_map/ppermute | solution.py:44
  118.2 10.2 %collective-permute-start.18 = (f32[208,384]{1,0:T(8,128)S(1)}, f32[208,384]{1,0:T(8,128)S(1)}, u32[]{:S(2)}, u32[]{:S(2)}) collective-permute-start(f32[208,384]{1,0:T(8,128)S(1)} %add_add_fusion), channel_id=1, source_target_pairs={{0,64},{8,72},{16,80},{24,88},{32,96},{40,104},{48,112},{56,120},{... | collective-permute-start | bytes 958472 | tf_op jit(solution)/shard_map/ppermute | solution.py:44
  129.0 15.8 %collective-permute-start.19 = (f32[208,384]{1,0:T(8,128)S(1)}, f32[208,384]{1,0:T(8,128)S(1)}, u32[]{:S(2)}, u32[]{:S(2)}) collective-permute-start(f32[208,384]{1,0:T(8,128)S(1)} %pad_maximum_fusion.3), channel_id=1, source_target_pairs={{0,48},{8,56},{16,32},{24,40},{32,16},{40,24},{48,0},{56,8},{64,11... | collective-permute-start | bytes 958472 | tf_op jit(solution)/shard_map/ppermute | solution.py:44
  130.9 14.0 %collective-permute-start.20 = (f32[208,384]{1,0:T(8,128)S(1)}, f32[208,384]{1,0:T(8,128)S(1)}, u32[]{:S(2)}, u32[]{:S(2)}) collective-permute-start(f32[208,384]{1,0:T(8,128)S(1)} %pad_maximum_fusion.3), channel_id=1, source_target_pairs={{0,32},{8,40},{16,48},{24,56},{32,0},{40,8},{48,16},{56,24},{64,96... | collective-permute-start | bytes 958472 | tf_op jit(solution)/shard_map/ppermute | solution.py:44
  130.9 14.6 %collective-permute-start.21 = (f32[208,384]{1,0:T(8,128)S(1)}, f32[208,384]{1,0:T(8,128)S(1)}, u32[]{:S(2)}, u32[]{:S(2)}) collective-permute-start(f32[208,384]{1,0:T(8,128)S(1)} %pad_maximum_fusion.3), channel_id=1, source_target_pairs={{0,16},{8,24},{16,0},{24,8},{32,48},{40,56},{48,32},{56,40},{64,80... | collective-permute-start | bytes 958472 | tf_op jit(solution)/shard_map/ppermute | solution.py:44
  145.8 3.1 %collective-permute-start.22 = (f32[208,1536]{1,0:T(8,128)S(1)}, f32[208,1536]{1,0:T(8,128)S(1)}, u32[]{:S(2)}, u32[]{:S(2)}) collective-permute-start(f32[208,1536]{1,0:T(8,128)S(1)} %pad_maximum_fusion.own_ref), channel_id=1, source_target_pairs={{0,8},{8,0},{16,24},{24,16},{32,40},{40,32},{48,56},{56,48},{64,72... | collective-permute-start | bytes 3833864 | tf_op jit(solution)/shard_map/ppermute | solution.py:44
  160.6 16.8 %all-to-all-start = ((f32[8,80,256]{2,1,0:T(8,128)}), f32[8,80,256]{2,1,0:T(8,128)S(1)}, u32[]{:S(2)}, u32[]{:S(2)}) async-start(f32[8,80,256]{2,1,0:T(8,128)} %get-tuple-element.13), calls=%async_computation | async-start | bytes 1310720 | tf_op jit(solution)/shard_map/all_to_all | solution.py:407
  179.0 5.2 %collective-permute-start.24 = (f32[2,5,80]{2,1,0:T(8,128)S(1)}, f32[2,5,80]{2,1,0:T(8,128)S(1)}, u32[]{:S(2)}, u32[]{:S(2)}) collective-permute-start(f32[2,5,80]{2,1,0:T(8,128)S(1)} %fusion.21), channel_id=1, source_target_pairs={{0,64},{8,72},{16,80},{24,88},{32,96},{40,104},{48,112},{56,120},{... | collective-permute-start | bytes 9608 | tf_op jit(solution)/shard_map/ppermute | solution.py:44
  184.2 4.7 %collective-permute-start.25 = (f32[2,5,80]{2,1,0:T(8,128)S(1)}, f32[2,5,80]{2,1,0:T(8,128)S(1)}, u32[]{:S(2)}, u32[]{:S(2)}) collective-permute-start(f32[2,5,80]{2,1,0:T(8,128)S(1)} %fusion.24), channel_id=1, source_target_pairs={{0,16},{8,24},{16,0},{24,8},{32,48},{40,56},{48,32},{56,40},{64,80... | collective-permute-start | bytes 9608 | tf_op jit(solution)/shard_map/ppermute | solution.py:44
  184.2 5.2 %collective-permute-start.26 = (f32[2,5,80]{2,1,0:T(8,128)S(1)}, f32[2,5,80]{2,1,0:T(8,128)S(1)}, u32[]{:S(2)}, u32[]{:S(2)}) collective-permute-start(f32[2,5,80]{2,1,0:T(8,128)S(1)} %fusion.24), channel_id=1, source_target_pairs={{0,32},{8,40},{16,48},{24,56},{32,0},{40,8},{48,16},{56,24},{64,96... | collective-permute-start | bytes 9608 | tf_op jit(solution)/shard_map/ppermute | solution.py:44
  187.5 4.9 %collective-permute-start.27 = (f32[2,5,80]{2,1,0:T(8,128)S(1)}, f32[2,5,80]{2,1,0:T(8,128)S(1)}, u32[]{:S(2)}, u32[]{:S(2)}) collective-permute-start(f32[2,5,80]{2,1,0:T(8,128)S(1)} %fusion.24), channel_id=1, source_target_pairs={{0,48},{8,56},{16,32},{24,40},{32,16},{40,24},{48,0},{56,8},{64,11... | collective-permute-start | bytes 9608 | tf_op jit(solution)/shard_map/ppermute | solution.py:44
  192.3 3.7 %collective-permute-start.28 = (f32[2,5,80]{2,1,0:T(8,128)S(1)}, f32[2,5,80]{2,1,0:T(8,128)S(1)}, u32[]{:S(2)}, u32[]{:S(2)}) collective-permute-start(f32[2,5,80]{2,1,0:T(8,128)S(1)} %add_add_fusion.3), channel_id=1, source_target_pairs={{0,4},{1,5},{2,6},{3,7},{4,0},{5,1},{6,2},{7,3},{8,12},{9,13},{10,... | collective-permute-start | bytes 9608 | tf_op jit(solution)/shard_map/ppermute | solution.py:44
  196.0 4.7 %collective-permute-start.29 = (f32[2,5,80]{2,1,0:T(8,128)S(1)}, f32[2,5,80]{2,1,0:T(8,128)S(1)}, u32[]{:S(2)}, u32[]{:S(2)}) collective-permute-start(f32[2,5,80]{2,1,0:T(8,128)S(1)} %add.205), channel_id=1, source_target_pairs={{0,1},{1,0},{2,3},{3,2},{4,5},{5,4},{6,7},{7,6},{8,9},{9,8},{10,11... | collective-permute-start | bytes 9608 | tf_op jit(solution)/shard_map/ppermute | solution.py:44
  196.8 5.2 %collective-permute-start.30 = (f32[2,5,80]{2,1,0:T(8,128)S(1)}, f32[2,5,80]{2,1,0:T(8,128)S(1)}, u32[]{:S(2)}, u32[]{:S(2)}) collective-permute-start(f32[2,5,80]{2,1,0:T(8,128)S(1)} %add.205), channel_id=1, source_target_pairs={{0,2},{1,3},{2,0},{3,1},{4,6},{5,7},{6,4},{7,5},{8,10},{9,11},{10,... | collective-permute-start | bytes 9608 | tf_op jit(solution)/shard_map/ppermute | solution.py:44
  198.0 4.9 %collective-permute-start.31 = (f32[2,5,80]{2,1,0:T(8,128)S(1)}, f32[2,5,80]{2,1,0:T(8,128)S(1)}, u32[]{:S(2)}, u32[]{:S(2)}) collective-permute-start(f32[2,5,80]{2,1,0:T(8,128)S(1)} %add.205), channel_id=1, source_target_pairs={{0,3},{1,2},{2,1},{3,0},{4,7},{5,6},{6,5},{7,4},{8,11},{9,10},{10,... | collective-permute-start | bytes 9608 | tf_op jit(solution)/shard_map/ppermute | solution.py:44
  (5 other events, 53.6 us)

commit v3 on v0

v3 whole, which is shorter than its diff:
```python
import functools
import math

import jax
import jax.numpy as jnp
from jax import lax
from jax.experimental import pallas as pl
from jax.experimental.pallas import tpu as pltpu
from jax.sharding import PartitionSpec as P

FOLDS = 5
LAMBDAS = 20
GRID = 400
BASE = FOLDS * LAMBDAS
SHRINKS = GRID // BASE
LEVELS = GRID // FOLDS
ROWS0 = 112
ROWS1 = 104
PEOPLE = 32768
SNPS = 12288
VMEM = 36 * 1024 * 1024
TILE = 512

step_size = 0.6
epsilon = 1e-05
lambda_base = 0.1
lambda_ratio = 1.2
shrink_unit = 0.2

NT = (((1,), (1,)), ((), ()))
NN = (((1,), (0,)), ((), ()))
TN = (((0,), (0,)), ((), ()))


def matmul(left, right, dims):
    return lax.dot_general(left, right, dims, preferred_element_type=jnp.float32)


def soft_threshold(values, cutoff):
    return values - jnp.clip(values, -cutoff, cutoff)


def swap(values, axis, bit):
    size = lax.axis_size(axis)
    return lax.ppermute(values, axis, [(i, i ^ bit) for i in range(size)])


def split2(values):
    high = values.astype(jnp.bfloat16)
    return high, (values - high.astype(jnp.float32)).astype(jnp.bfloat16)


def order4(parts, place):
    low, high = (place & 1) == 1, (place & 2) == 2
    a, b, c, d = parts
    a, b, c, d = (jnp.where(low, b, a), jnp.where(low, a, b), jnp.where(low, d, c), jnp.where(low, c, d))
    return jnp.where(high, c, a), jnp.where(high, d, b), jnp.where(high, a, c), jnp.where(high, b, d)


def all_sum(values, bits):
    for axis, group in bits:
        got = [swap(values, axis, bit) for bit in group]
        values = values + got[0] if len(got) == 1 else (values + got[0]) + (got[1] + got[2])
    return values


BOTH = ("samp", "blk")
SAMP_BITS = (("samp", (1,)), ("samp", (8,)), ("samp", (2, 4, 6)))
ALL_BITS = (("samp", (1,)), ("samp", (2, 4, 6)), ("blk", (1, 2, 3)), (BOTH, (4, 64, 68)))


def scatter_chips(kept, place):
    width = kept.shape[1] // 4
    got = [
        swap(lax.dynamic_slice_in_dim(kept, (place ^ k) * width, width, 1), "samp", 2 * k) for k in (1, 2, 3)
    ]
    mine = lax.dynamic_slice_in_dim(kept, place * width, width, 1)
    mine = (mine + got[0]) + (got[1] + got[2])
    return mine + swap(mine, "samp", 8)


def gather_chips(piece, place):
    parts = [piece] + [swap(piece, "samp", 2 * k) for k in (1, 2, 3)]
    return jnp.concatenate(order4(parts, place), axis=1)


def whole(count):
    return [pl.BlockSpec(memory_space=pltpu.VMEM)] * count


def params():
    return pltpu.CompilerParams(vmem_limit_bytes=VMEM)


def parts3(values):
    high, rest = split2(values)
    rest = values - high.astype(jnp.float32)
    mid, low = split2(rest)
    return [part.astype(jnp.float32) for part in (high, mid, low)]


def prepare_kernel(pheno_ref, fold_ref, geno_ref, dose_ref, stats_ref, buffer_ref, left_ref, sums_ref, sems):
    people, width = dose_ref.shape
    parts = sems.shape[0]
    tile = people // parts
    copies = [
        pltpu.make_async_copy(
            geno_ref.at[pl.ds(part * tile, tile)], buffer_ref.at[pl.ds(part * tile, tile)], sems.at[part]
        )
        for part in range(parts)
    ]
    for copy in copies:
        copy.start()
    line = lax.broadcasted_iota(jnp.int32, (8, people), 0)
    chosen = line == fold_ref[...]
    split = jnp.where(chosen, pheno_ref[...], 0.0)
    high, mid, low = parts3(split)
    high = jnp.where(line == FOLDS, 1.0, high)
    left_ref[...] = jnp.concatenate([high, mid, low, jnp.zeros_like(low)], axis=0).astype(jnp.bfloat16)
    counts = jnp.sum(chosen.astype(jnp.float32), axis=1, keepdims=True)
    sums = jnp.sum(split, axis=1, keepdims=True)
    lane = lax.broadcasted_iota(jnp.int32, (1, width), 1)
    extra = jnp.zeros((1, width), jnp.float32)
    for fold in range(FOLDS):
        extra = jnp.where(lane == fold, counts[fold : fold + 1], extra)
        extra = jnp.where(lane == FOLDS + fold, sums[fold : fold + 1], extra)
    squares = jnp.zeros((8, width), jnp.float32)
    for part in range(parts):
        copies[part].wait()
        span = slice(part * tile, (part + 1) * tile)
        values = buffer_ref[span].astype(jnp.float32)
        dose = values.astype(jnp.bfloat16)
        dose_ref[span] = dose
        product = matmul(left_ref[:, span], dose, NN)
        sums_ref[...] = product if part == 0 else sums_ref[...] + product
        squares += jnp.sum((values * values).reshape(-1, 8, width), axis=0)
    stats_ref[0:8] = sums_ref[0:8] + sums_ref[8:16] + sums_ref[16:24]
    stats_ref[6:7] = jnp.sum(squares, axis=0, keepdims=True)
    stats_ref[7:8] = extra


def prepare(genotypes, phenotype, fold_ids, parts=8):
    people, width = genotypes.shape
    return pl.pallas_call(
        prepare_kernel,
        in_specs=whole(2) + [pl.BlockSpec(memory_space=pl.ANY)],
        out_specs=whole(2),
        out_shape=[
            jax.ShapeDtypeStruct((people, width), jnp.bfloat16),
            jax.ShapeDtypeStruct((8, width), jnp.float32),
        ],
        scratch_shapes=[
            pltpu.VMEM((people, width), jnp.int32),
            pltpu.VMEM((32, people), jnp.bfloat16),
            pltpu.VMEM((32, width), jnp.float32),
            pltpu.SemaphoreType.DMA((parts,)),
        ],
        compiler_params=params(),
    )(phenotype.reshape(1, people), fold_ids.reshape(1, people), genotypes)


def base_rows(rows):
    row = lax.broadcasted_iota(jnp.int32, (rows, 1), 0)
    cutoff = step_size * (lambda_base * jnp.exp((row // FOLDS).astype(jnp.float32) * math.log(lambda_ratio)))
    return row, row % FOLDS, cutoff


def spread(table, fold_of):
    out = jnp.broadcast_to(table[FOLDS - 1 : FOLDS], (fold_of.shape[0], table.shape[1]))
    for fold in range(FOLDS - 1):
        out = jnp.where(fold_of == fold, table[fold : fold + 1], out)
    return out


def next_coeff(coeff, product, target, shrink, cutoff):
    gradient = (1.0 - shrink) * product + shrink * coeff - target
    return soft_threshold(coeff - step_size * gradient, cutoff)


def first_kernel(core_ref, stats_ref, dose_ref, kept_ref, sent_ref, table_ref, both_ref, total_ref):
    stats = stats_ref[...]
    mean = stats[5:6] / PEOPLE
    scales = jnp.sqrt(stats[6:7] / PEOPLE - mean * mean + epsilon)
    inverse = 1.0 / scales
    lane = lax.broadcasted_iota(jnp.int32, (1, stats.shape[1]), 1)
    pick = lambda place: jnp.sum(jnp.where(lane == place, stats[7:8], 0.0), axis=1, keepdims=True)
    counts = [pick(fold) for fold in range(FOLDS)]
    sums = [pick(FOLDS + fold) for fold in range(FOLDS)]
    every = sums[0] + sums[1] + sums[2] + sums[3] + sums[4]
    geno_pheno = jnp.sum(stats[0:FOLDS], axis=0, keepdims=True)
    row, fold_of, cutoff = base_rows(ROWS0)
    target = jnp.zeros((ROWS0, stats.shape[1]), jnp.float32)
    for fold in range(FOLDS):
        train = geno_pheno - stats[fold : fold + 1]
        zscore = (train - (every - sums[fold]) * mean) / (scales * jnp.sqrt(PEOPLE - counts[fold]))
        table_ref[fold : fold + 1] = zscore
        table_ref[8 + fold : 9 + fold] = stats[fold : fold + 1] - mean * sums[fold]
        target = jnp.where(fold_of == fold, zscore, target)
    table_ref[5:6] = mean
    table_ref[6:7] = scales
    table_ref[7:8] = inverse
    table_ref[13:16] = jnp.zeros((3, stats.shape[1]), jnp.float32)
    coeff = soft_threshold(step_size * target, cutoff)
    scaled = jnp.where(row < BASE, coeff * inverse, 0.0)
    high, low = split2(scaled)
    both_ref[...] = jnp.zeros_like(both_ref)
    both_ref[0:ROWS0] = high
    both_ref[128 : 128 + ROWS0] = low
    line = lax.broadcasted_iota(jnp.int32, (16, 1), 0)
    mean_high, mean_mid, mean_low = parts3(mean)
    means = jnp.where(line == 0, mean_high, jnp.where(line == 1, mean_mid, jnp.where(line == 2, mean_low, 0.0)))
    offset = jnp.sum(matmul(means.astype(jnp.bfloat16), both_ref[...], NT), axis=0, keepdims=True)
    offset = offset[:, :128] + offset[:, 128:]
    total_ref[...] = jnp.zeros_like(total_ref)

    def body(step, carry):
        dose = dose_ref[pl.ds(pl.multiple_of(step * TILE, TILE), TILE)]
        scores = matmul(dose, both_ref[...], NT)
        scores = scores[:, :128] + scores[:, 128:] - carry
        pair = jnp.concatenate(split2(scores), axis=1)
        total_ref[...] += matmul(pair, dose, TN)
        return carry

    lax.fori_loop(0, dose_ref.shape[0] // TILE, body, offset)
    half = ROWS0 // 2
    first = total_ref[0:half] + total_ref[128 : 128 + half]
    second = total_ref[half:ROWS0] + total_ref[128 + half : 128 + ROWS0]
    is_first = core_ref[0] == 0
    kept_ref[...] = jnp.where(is_first, first, second)
    sent_ref[...] = jnp.where(is_first, second, first)


def first_product(core, stats, dose):
    width = dose.shape[1]
    half = jax.ShapeDtypeStruct((ROWS0 // 2, width), jnp.float32)
    return pl.pallas_call(
        first_kernel,
        in_specs=[pl.BlockSpec(memory_space=pltpu.SMEM)] + whole(2),
        out_specs=whole(3),
        out_shape=[half, half, jax.ShapeDtypeStruct((16, width), jnp.float32)],
        scratch_shapes=[pltpu.VMEM((256, width), jnp.bfloat16), pltpu.VMEM((256, width), jnp.float32)],
        compiler_params=params(),
    )(core, stats, dose)


def second_kernel(
    core_ref, table_ref, own_ref, other_ref, dose_ref, out_ref, product_ref, coeff_ref, both_ref, *, mine
):
    rows = 2 * ROWS1
    half = ROWS0 // 2
    table = table_ref[...]
    row, fold_of, cutoff = base_rows(ROWS1)
    target = spread(table[:FOLDS], fold_of)
    coeff = soft_threshold(step_size * target, cutoff)
    is_first = core_ref[0] == 0
    product_ref[0:half] = jnp.where(is_first, own_ref[...], other_ref[...])
    product_ref[half:] = jnp.where(is_first, other_ref[...], own_ref[...])
    product = product_ref[0:ROWS1] * (table[7:8] / PEOPLE)
    side = core_ref[0] if mine else 1 - core_ref[0]
    for group in range(2):
        shrink = shrink_unit * (2 * side + group + 1).astype(jnp.float32)
        new = next_coeff(coeff, product, target, shrink, cutoff)
        coeff_ref[group * ROWS1 : (group + 1) * ROWS1] = jnp.where(row < BASE, new, 0.0)
    scaled = coeff_ref[...] * table[7:8]
    offset = jnp.sum(scaled * table[5:6], axis=1, keepdims=True)
    high, low = split2(scaled)
    both_ref[0:rows] = high
    both_ref[rows:] = low
    out_ref[...] = jnp.zeros_like(out_ref)

    def body(step, carry):
        dose = dose_ref[pl.ds(pl.multiple_of(step * TILE, TILE), TILE)]
        scores = matmul(both_ref[...], dose, NT)
        scores = scores[:rows] + scores[rows:] - carry
        pair = jnp.concatenate(split2(scores), axis=0)
        sums = matmul(pair, dose, NN)
        out_ref[...] += sums[:rows] + sums[rows:]
        return carry

    lax.fori_loop(0, dose_ref.shape[0] // TILE, body, offset)


def second_product(core, table, own, other, dose, mine):
    people, width = dose.shape
    rows = 2 * ROWS1
    return pl.pallas_call(
        functools.partial(second_kernel, mine=mine),
        in_specs=[pl.BlockSpec(memory_space=pltpu.SMEM)] + whole(4),
        out_specs=pl.BlockSpec(memory_space=pltpu.VMEM),
        out_shape=jax.ShapeDtypeStruct((rows, width), jnp.float32),
        scratch_shapes=[
            pltpu.VMEM((ROWS0, width), jnp.float32),
            pltpu.VMEM((rows, width), jnp.float32),
            pltpu.VMEM((2 * rows, width), jnp.bfloat16),
        ],
        compiler_params=params(),
        cost_estimate=pl.CostEstimate(
            flops=8 * people * width * rows, bytes_accessed=2 * people * width, transcendentals=0
        ),
    )(core, table, own, other, dose)


def predict_kernel(
    core_ref, own_ref, other_ref, table_ref, fold_ref, dose_ref,
    coeff_out, number_out, score_out, coeff_ref, wide_ref, weight_ref, offset_ref,
):
    half, width = own_ref.shape

    def place(first_ref, second_ref):
        for lane in range(width // 128):
            lanes = slice(lane * 128, (lane + 1) * 128)
            coeff_ref[lane, 0:half] = first_ref[:, lanes]
            coeff_ref[lane, half:] = second_ref[:, lanes]
        for group in range(SHRINKS):
            ref = first_ref if group < 2 else second_ref
            start = group % 2 * ROWS1
            coeff_out[group * BASE : (group + 1) * BASE] = ref[start : start + BASE]

    @pl.when(core_ref[0] == 0)
    def _():
        place(own_ref, other_ref)

    @pl.when(core_ref[0] != 0)
    def _():
        place(other_ref, own_ref)

    for lane in range(width // 128):
        lanes = slice(lane * 128, (lane + 1) * 128)
        for fold in range(FOLDS):
            for group in range(SHRINKS):
                first = fold * LEVELS + group * LAMBDAS
                rows = pl.ds(group * ROWS1 + fold, LAMBDAS, FOLDS)
                wide_ref[first : first + LAMBDAS, lanes] = coeff_ref[lane, rows]
    table = table_ref[...]
    for fold in range(FOLDS):
        span = slice(fold * LEVELS, (fold + 1) * LEVELS)
        weighted = (wide_ref[span] / table[6:7]).astype(jnp.bfloat16)
        weight_ref[span] = weighted
        wide = weighted.astype(jnp.float32)
        offset_ref[span] = jnp.sum(wide * table[5:6], axis=1, keepdims=True)
        number_out[span] = jnp.sum(wide * table[8 + fold : 9 + fold], axis=1, keepdims=True)

    parts, _, tile = score_out.shape

    def body(part, carry):
        start = pl.multiple_of(part * tile, tile)
        scores = matmul(weight_ref[...], dose_ref[pl.ds(start, tile)], NT) - offset_ref[...]
        folds = fold_ref[:, pl.ds(start, tile)]
        out = scores[0:LEVELS]
        for fold in range(1, FOLDS):
            out = jnp.where(folds == fold, scores[fold * LEVELS : (fold + 1) * LEVELS], out)
        score_out[part] = out
        return carry

    lax.fori_loop(0, parts, body, 0)


def predict(core, own, other, table, fold_ids, dose, parts):
    people, width = dose.shape
    half = own.shape[0]
    return pl.pallas_call(
        predict_kernel,
        in_specs=[pl.BlockSpec(memory_space=pltpu.SMEM)] + whole(5),
        out_specs=whole(3),
        out_shape=[
            jax.ShapeDtypeStruct((GRID, width), jnp.float32),
            jax.ShapeDtypeStruct((GRID, 1), jnp.float32),
            jax.ShapeDtypeStruct((parts, LEVELS, people // parts), jnp.float32),
        ],
        scratch_shapes=[
            pltpu.VMEM((width // 128, 2 * half, 128), jnp.float32),
            pltpu.VMEM((GRID, width), jnp.float32),
            pltpu.VMEM((GRID, width), jnp.bfloat16),
            pltpu.VMEM((GRID, 1), jnp.float32),
        ],
        compiler_params=params(),
    )(core, own, other, table, fold_ids.reshape(1, people), dose)


def local(genotypes, phenotype, fold_ids):
    num_rows, block_width = genotypes.shape
    samp, blk = lax.axis_index("samp"), lax.axis_index("blk")
    core, place = samp & 1, (samp >> 1) & 3

    dose, stats = prepare(genotypes, phenotype, fold_ids)
    stats = all_sum(stats, SAMP_BITS)
    fold_count = stats[7, :FOLDS][:, None]

    kept, sent, table = first_product(core[None], stats, dose)
    piece = scatter_chips(kept + swap(sent, "samp", 1), place)
    own_product = gather_chips(piece, place)
    other_product = swap(own_product, "samp", 1)

    sent = second_product(core[None], table, own_product, other_product, dose, False)
    sent = swap(sent, "samp", 1)
    kept = second_product(core[None], table, own_product, other_product, dose, True)
    piece = scatter_chips(kept + sent, place)
    width = block_width // 4
    here = lambda a: lax.dynamic_slice_in_dim(a, place * width, width, 1)
    row, fold_of, cutoff = base_rows(ROWS1)
    table_here = here(table)
    target = spread(table_here[:FOLDS], fold_of)
    coeff = soft_threshold(step_size * target, cutoff)
    scale_here = table_here[7:8] / PEOPLE
    first = core == 0
    own, other = here(own_product), here(other_product)
    old = jnp.concatenate([jnp.where(first, own, other), jnp.where(first, other, own)], axis=0)
    old = old[:ROWS1] * scale_here
    final = []
    for group in range(2):
        shrink = shrink_unit * (2 * core + group + 1).astype(jnp.float32)
        new = next_coeff(coeff, old, target, shrink, cutoff)
        latest = piece[group * ROWS1 : (group + 1) * ROWS1] * scale_here
        final.append(next_coeff(new, latest, target, shrink, cutoff))
    own = gather_chips(jnp.concatenate(final, axis=0), place)
    other = swap(own, "samp", 1)

    blocks = lax.axis_size("blk")
    coeff_all, numerator, scores = predict(core[None], own, other, table, fold_ids, dose, blocks)
    scores = jnp.sum(lax.all_to_all(scores, "blk", 0, 0, tiled=True), axis=0)
    people = num_rows // blocks
    folds_here = lax.dynamic_slice_in_dim(fold_ids, blk * people, people, 0)
    square = scores * scores
    denominator = jnp.stack(
        [jnp.sum(jnp.where((folds_here == fold)[None, :], square, 0.0), axis=1) for fold in range(FOLDS)]
    )
    sums = jnp.stack([numerator.reshape(FOLDS, LEVELS) / lax.axis_size("samp"), denominator])
    sums = all_sum(sums, ALL_BITS)
    sums = sums * jnp.array([1.0 / math.sqrt(SNPS), 1.0 / SNPS], jnp.float32)[:, None, None] / fold_count[None]
    fold_scores = sums.transpose(0, 2, 1).reshape(2, GRID)
    return (coeff_all.T, fold_scores)


def solution(mesh):
    return jax.shard_map(
        local,
        mesh=mesh,
        in_specs=(P("samp", "blk"), P("samp"), P("samp")),
        out_specs=(P("blk", None), P()),
        check_vma=False,
    )
```

time: 423 us -> 184 us (0.43)
  waiting for transfers between devices: 224 us -> 80.9 us
  blocking collectives: 108 us -> 0 us
  matrix products: 54 us -> 0 us
  starting transfers between devices: 0.3 us -> 50.6 us
  Pallas kernels: 0 us -> 35.5 us
  other arithmetic: 18.2 us -> 3.09 us
  between operations: 13.9 us -> 0.95 us
  local copies, waits for them, and re-layouts: 3.91 us -> 12.7 us
    psum x2 -> x0, waiting for transfers between devices: 172 us -> none  [the longest x1 90.3 us: local(): predicted = lax.psum(partial_value, 'blk') / root_snps]
    psum x2 -> x0, blocking collectives: 108 us -> none  [the longest x1 71.7 us: local(): lax.psum((gram_local, local_sum, local_sq, local_geno_pheno, local_pheno_...]
    ppermute x0 -> x33, waiting for transfers between devices: none -> 69.5 us  [swap(): return lax.ppermute(values, axis, [(i, i ^ bit) for i in range(size)])]
    dot_general x6 -> x0, matrix products: 54 us -> none  [the longest x1 19 us: local(): jnp.dot(dosage_bf.T, dosage_bf, preferred_element_type=jnp.float32)]
    all_gather x1 -> x0, waiting for transfers between devices: 52.5 us -> none  [local(): coeff_all = lax.all_gather(coeffs, 'samp', axis=1, tiled=True)]
    ppermute x0 -> x33, starting transfers between devices: none -> 45.7 us  [swap(): return lax.ppermute(values, axis, [(i, i ^ bit) for i in range(size)])]
    pallas_call x0 -> x5, Pallas kernels: none -> 35.5 us  [the longest x2 15.4 us: second_product(): pl.pallas_call(functools.partial(second_kernel, mine=mine), in_specs=[pl....]
    all_to_all x0 -> x1, waiting for transfers between devices: none -> 11.5 us  [local(): scores = jnp.sum(lax.all_to_all(scores, 'blk', 0, 0, tiled=True), axis=0)]
  transfers between devices with their start and end apart: 3 -> 34, of which waited for: 3 -> 29; matrix products, arithmetic and copies ran while one was open for 4% -> 0% of each run, Pallas kernels for 0% -> 4%
where the time goes in v3:
time: 184 us
  waiting for transfers between devices  80.9 us (44%)
  starting transfers between devices  50.6 us (28%)
  Pallas kernels  35.5 us (19%)
  local copies, waits for them, and re-layouts  12.7 us (7%)
  other arithmetic  3.09 us (2%)
    ppermute x33, waiting for transfers between devices, swap(): return lax.ppermute(values, axis, [(i, i ^ bit) for i in range(size)])  69.5 us
    ppermute x33, starting transfers between devices, swap(): return lax.ppermute(values, axis, [(i, i ^ bit) for i in range(size)])  45.7 us
    pallas_call x2, Pallas kernels, second_product(): pl.pallas_call(functools.partial(second_kernel, mine=mine), in_specs=[pl....  15.4 us
    all_to_all x1, waiting for transfers between devices, local(): scores = jnp.sum(lax.all_to_all(scores, 'blk', 0, 0, tiled=True), axis=0)  11.5 us
    unnamed x20, local copies, waits for them, and re-layouts  10.7 us
    pallas_call x1, Pallas kernels, first_product(): pl.pallas_call(first_kernel, in_specs=[pl.BlockSpec(memory_space=pltpu.SM...  8.51 us
    pallas_call x1, Pallas kernels, predict(): pl.pallas_call(predict_kernel, in_specs=[pl.BlockSpec(memory_space=pltpu....  6.55 us
    pallas_call x1, Pallas kernels, prepare(): pl.pallas_call(prepare_kernel, in_specs=whole(2) + [pl.BlockSpec(memory_s...  5.06 us
  transfers between devices with their start and end apart: 34, of which 29 were waited for; matrix products, arithmetic and copies ran while one was open for 0% of the time, Pallas kernels for 4%

profile of v3, /device:TPU:0, one launch (start us, length us, event | category | flops | bytes accessed | tf_op | source)
XLA Modules:
  0.0 183.8 jit_solution(16997779317599748478)
XLA Ops:
  2.0 5.1 %shard_map.59 = (bf16[2048,1536]{1,0:T(8,128)(2,1)S(1)}, f32[8,1536]{1,0:T(8,128)S(1)}) custom-call(f32[1,2048]{1,0:T(1,128)S(1)} %bitcast.18, s32[1,2048]{1,0:T(1,128)S(1)} %bitcast.16, s32[2048,1536]{1,0:T(8,128)} %geno_ref.1), custom_call_target="tpu_custom_call" | custom-call | tf_op jit(solution)/shard_map/pallas_call | solution.py:144
  7.1 2.6 %copy-done = bf16[2048,1536]{1,0:T(8,128)(2,1)} copy-done((bf16[2048,1536]{1,0:T(8,128)(2,1)}, bf16[2048,1536]{1,0:T(8,128)(2,1)S(1)}, u32[]{:S(2)}) %copy-start) | copy-done | bytes 6291480
  11.0 4.0 %collective-permute-start.1 = (f32[8,1536]{1,0:T(8,128)S(1)}, f32[8,1536]{1,0:T(8,128)S(1)}, u32[]{:S(2)}, u32[]{:S(2)}) collective-permute-start(f32[8,1536]{1,0:T(8,128)S(1)} %add.154), channel_id=1, source_target_pairs={{0,64},{8,72},{16,80},{24,88},{32,96},{40,104},{48,112},{56,120},{... | collective-permute-start | bytes 147464 | tf_op jit(solution)/shard_map/ppermute | solution.py:45
  17.1 2.8 %collective-permute-start.4 = (f32[8,1536]{1,0:T(8,128)S(1)}, f32[8,1536]{1,0:T(8,128)S(1)}, u32[]{:S(2)}, u32[]{:S(2)}) collective-permute-start(f32[8,1536]{1,0:T(8,128)S(1)} %add.155), channel_id=1, source_target_pairs={{0,48},{8,56},{16,32},{24,40},{32,16},{40,24},{48,0},{56,8},{64,11... | collective-permute-start | bytes 147464 | tf_op jit(solution)/shard_map/ppermute | solution.py:45
  22.5 3.1 %collective-permute-done.3 = f32[8,1536]{1,0:T(8,128)S(1)} collective-permute-done((f32[8,1536]{1,0:T(8,128)S(1)}, f32[8,1536]{1,0:T(8,128)S(1)}, u32[]{:S(2)}, u32[]{:S(2)}) %collective-permute-start.3) | collective-permute-done | bytes 49184 | tf_op jit(solution)/shard_map/ppermute | solution.py:45
  25.6 2.8 %copy-done.1 = bf16[2048,1536]{1,0:T(8,128)(2,1)S(1)} copy-done((bf16[2048,1536]{1,0:T(8,128)(2,1)S(1)}, bf16[2048,1536]{1,0:T(8,128)(2,1)}, u32[]{:S(2)}) %copy-start.1) | copy-done | bytes 6291480
  28.3 8.5 %shard_map.60 = (f32[56,1536]{1,0:T(8,128)S(1)}, f32[56,1536]{1,0:T(8,128)S(1)}, f32[16,1536]{1,0:T(8,128)S(1)}) custom-call(s32[1]{0:T(128)} %bitcast.core_ref, f32[8,1536]{1,0:T(8,128)S(1)} %add_add_fusion.2.stats_ref, bf16[2048,1536]{1,0:T(8,128)(2,1)S(1)} %copy-done.1), custom_call_target="tpu_custom_call" | custom-call | tf_op jit(solution)/shard_map/pallas_call | solution.py:236
  39.0 2.4 %collective-permute-start.8 = (f32[56,384]{1,0:T(8,128)S(1)}, f32[56,384]{1,0:T(8,128)S(1)}, u32[]{:S(2)}, u32[]{:S(2)}) collective-permute-start(f32[56,384]{1,0:T(8,128)S(1)} %get-tuple-element.43), channel_id=1, source_target_pairs={{0,48},{8,56},{16,32},{24,40},{32,16},{40,24},{48,0},{56,8},{64,11... | collective-permute-start | bytes 258056 | tf_op jit(solution)/shard_map/ppermute | solution.py:45
  45.1 2.2 %collective-permute-done.7 = f32[56,384]{1,0:T(8,128)S(1)} collective-permute-done((f32[56,384]{1,0:T(8,128)S(1)}, f32[56,384]{1,0:T(8,128)S(1)}, u32[]{:S(2)}, u32[]{:S(2)}) %collective-permute-start.7) | collective-permute-done | bytes 86048 | tf_op jit(solution)/shard_map/ppermute | solution.py:45
  47.4 3.6 %collective-permute-start.9 = (f32[56,384]{1,0:T(8,128)S(1)}, f32[56,384]{1,0:T(8,128)S(1)}, u32[]{:S(2)}, u32[]{:S(2)}) collective-permute-start(f32[56,384]{1,0:T(8,128)S(1)} %add_add_fusion.1), channel_id=1, source_target_pairs={{0,64},{8,72},{16,80},{24,88},{32,96},{40,104},{48,112},{56,120},{... | collective-permute-start | bytes 258056 | tf_op jit(solution)/shard_map/ppermute | solution.py:45
  51.0 2.5 %collective-permute-done.9 = f32[56,384]{1,0:T(8,128)S(1)} collective-permute-done((f32[56,384]{1,0:T(8,128)S(1)}, f32[56,384]{1,0:T(8,128)S(1)}, u32[]{:S(2)}, u32[]{:S(2)}) %collective-permute-start.9) | collective-permute-done | bytes 86048 | tf_op jit(solution)/shard_map/ppermute | solution.py:45
  53.7 2.7 %collective-permute-start.11 = (f32[56,384]{1,0:T(8,128)S(1)}, f32[56,384]{1,0:T(8,128)S(1)}, u32[]{:S(2)}, u32[]{:S(2)}) collective-permute-start(f32[56,384]{1,0:T(8,128)S(1)} %add.168), channel_id=1, source_target_pairs={{0,32},{8,40},{16,48},{24,56},{32,0},{40,8},{48,16},{56,24},{64,96... | collective-permute-start | bytes 258056 | tf_op jit(solution)/shard_map/ppermute | solution.py:45
  59.8 2.3 %collective-permute-done.10 = f32[56,384]{1,0:T(8,128)S(1)} collective-permute-done((f32[56,384]{1,0:T(8,128)S(1)}, f32[56,384]{1,0:T(8,128)S(1)}, u32[]{:S(2)}, u32[]{:S(2)}) %collective-permute-start.10) | collective-permute-done | bytes 86048 | tf_op jit(solution)/shard_map/ppermute | solution.py:45
  64.0 2.8 %copy-done.2 = bf16[2048,1536]{1,0:T(8,128)(2,1)S(1)} copy-done((bf16[2048,1536]{1,0:T(8,128)(2,1)S(1)}, bf16[2048,1536]{1,0:T(8,128)(2,1)}, u32[]{:S(2)}) %copy-start.2) | copy-done | bytes 6291480
  66.8 7.7 %shard_map.62 = f32[208,1536]{1,0:T(8,128)S(1)} custom-call(s32[1]{0:T(128)} %bitcast.core_ref, f32[16,1536]{1,0:T(8,128)S(1)} %get-tuple-element.12.table_ref, f32[56,1536]{1,0:T(8,128)S(1)} %pad_maximum_fusion.1.own_ref, f32[56,1536]{1,0:T(8,128)S(1)} %collective-permute-done.13.other_ref, bf16[2048,1536]{1,0:T(8,128)(2,1)S(1)} %copy-done.2), custom_call_target="tpu_custom_call" | custom-call | flops 5234491392 | bytes 6291456 | tf_op jit(solution)/shard_map/pallas_call | solution.py:286
  74.9 7.7 %shard_map.61 = f32[208,1536]{1,0:T(8,128)S(1)} custom-call(s32[1]{0:T(128)} %bitcast.core_ref, f32[16,1536]{1,0:T(8,128)S(1)} %get-tuple-element.12.table_ref, f32[56,1536]{1,0:T(8,128)S(1)} %pad_maximum_fusion.1.own_ref, f32[56,1536]{1,0:T(8,128)S(1)} %collective-permute-done.13.other_ref, bf16[2048,1536]{1,0:T(8,128)(2,1)S(1)} %copy-done.2), custom_call_target="tpu_custom_call" | custom-call | flops 5234491392 | bytes 6291456 | tf_op jit(solution)/shard_map/pallas_call | solution.py:286
  86.6 2.3 %collective-permute-start.16 = (f32[208,384]{1,0:T(8,128)}, f32[208,384]{1,0:T(8,128)}, u32[]{:S(2)}, u32[]{:S(2)}) collective-permute-start(f32[208,384]{1,0:T(8,128)} %get-tuple-element.35), channel_id=1, source_target_pairs={{0,32},{8,40},{16,48},{24,56},{32,0},{40,8},{48,16},{56,24},{64,96... | collective-permute-start | bytes 958472 | tf_op jit(solution)/shard_map/ppermute | solution.py:45
  88.9 6.5 %collective-permute-done.15 = f32[208,384]{1,0:T(8,128)S(1)} collective-permute-done((f32[208,384]{1,0:T(8,128)}, f32[208,384]{1,0:T(8,128)S(1)}, u32[]{:S(2)}, u32[]{:S(2)}) %collective-permute-start.15) | collective-permute-done | bytes 319520 | tf_op jit(solution)/shard_map/ppermute | solution.py:45
  95.4 5.7 %collective-permute-done.17 = f32[208,384]{1,0:T(8,128)} collective-permute-done((f32[208,384]{1,0:T(8,128)}, f32[208,384]{1,0:T(8,128)}, u32[]{:S(2)}, u32[]{:S(2)}) %collective-permute-start.17) | collective-permute-done | bytes 319520 | tf_op jit(solution)/shard_map/ppermute | solution.py:45
  104.2 3.6 %collective-permute-start.18 = (f32[208,384]{1,0:T(8,128)S(1)}, f32[208,384]{1,0:T(8,128)S(1)}, u32[]{:S(2)}, u32[]{:S(2)}) collective-permute-start(f32[208,384]{1,0:T(8,128)S(1)} %add_add_fusion), channel_id=1, source_target_pairs={{0,64},{8,72},{16,80},{24,88},{32,96},{40,104},{48,112},{56,120},{... | collective-permute-start | bytes 958472 | tf_op jit(solution)/shard_map/ppermute | solution.py:45
  108.0 7.0 %collective-permute-done.18 = f32[208,384]{1,0:T(8,128)S(1)} collective-permute-done((f32[208,384]{1,0:T(8,128)S(1)}, f32[208,384]{1,0:T(8,128)S(1)}, u32[]{:S(2)}, u32[]{:S(2)}) %collective-permute-start.18) | collective-permute-done | bytes 319520 | tf_op jit(solution)/shard_map/ppermute | solution.py:45
  115.7 3.0 %collective-permute-start.20 = (f32[208,384]{1,0:T(8,128)S(1)}, f32[208,384]{1,0:T(8,128)S(1)}, u32[]{:S(2)}, u32[]{:S(2)}) collective-permute-start(f32[208,384]{1,0:T(8,128)S(1)} %pad_maximum_fusion.2), channel_id=1, source_target_pairs={{0,32},{8,40},{16,48},{24,56},{32,0},{40,8},{48,16},{56,24},{64,96... | collective-permute-start | bytes 958472 | tf_op jit(solution)/shard_map/ppermute | solution.py:45
  120.4 5.8 %collective-permute-done.21 = f32[208,384]{1,0:T(8,128)S(1)} collective-permute-done((f32[208,384]{1,0:T(8,128)S(1)}, f32[208,384]{1,0:T(8,128)S(1)}, u32[]{:S(2)}, u32[]{:S(2)}) %collective-permute-start.21) | collective-permute-done | bytes 319520 | tf_op jit(solution)/shard_map/ppermute | solution.py:45
  126.2 5.6 %collective-permute-done.20 = f32[208,384]{1,0:T(8,128)S(1)} collective-permute-done((f32[208,384]{1,0:T(8,128)S(1)}, f32[208,384]{1,0:T(8,128)S(1)}, u32[]{:S(2)}, u32[]{:S(2)}) %collective-permute-start.20) | collective-permute-done | bytes 319520 | tf_op jit(solution)/shard_map/ppermute | solution.py:45
  131.8 2.6 %collective-permute-done.19 = f32[208,384]{1,0:T(8,128)S(1)} collective-permute-done((f32[208,384]{1,0:T(8,128)S(1)}, f32[208,384]{1,0:T(8,128)S(1)}, u32[]{:S(2)}, u32[]{:S(2)}) %collective-permute-start.19) | collective-permute-done | bytes 319520 | tf_op jit(solution)/shard_map/ppermute | solution.py:45
  134.7 3.0 %collective-permute-done.22.other_ref = f32[208,1536]{1,0:T(8,128)S(1)} collective-permute-done((f32[208,1536]{1,0:T(8,128)S(1)}, f32[208,1536]{1,0:T(8,128)S(1)}, u32[]{:S(2)}, u32[]{:S(2)}) %collective-permute-start.22) | collective-permute-done | bytes 1277984 | tf_op jit(solution)/shard_map/ppermute | solution.py:45
  137.7 6.6 %shard_map.63 = (f32[400,1536]{1,0:T(8,128)}, f32[400,1]{1,0:T(8,128)S(1)}, f32[8,80,256]{2,1,0:T(8,128)}) custom-call(s32[1]{0:T(128)} %bitcast.core_ref, f32[208,1536]{1,0:T(8,128)S(1)} %pad_maximum_fusion.own_ref, f32[208,1536]{1,0:T(8,128)S(1)} %collective-permute-done.22.other_ref, f32[16,1536]{1,0:T(8,128)S(1)} %get-tuple-element.12.table_ref, ...), custom_call_target="tpu_custom_call" | custom-call | tf_op jit(solution)/shard_map/pallas_call | solution.py:361
  144.3 5.0 %all-to-all-start = ((f32[8,80,256]{2,1,0:T(8,128)}), f32[8,80,256]{2,1,0:T(8,128)S(1)}, u32[]{:S(2)}, u32[]{:S(2)}) async-start(f32[8,80,256]{2,1,0:T(8,128)} %get-tuple-element.17), calls=%async_computation | async-start | bytes 1310720 | tf_op jit(solution)/shard_map/all_to_all | solution.py:420
  149.5 11.5 %all-to-all-done = f32[8,80,256]{2,1,0:T(8,128)S(1)} async-done(((f32[8,80,256]{2,1,0:T(8,128)}), f32[8,80,256]{2,1,0:T(8,128)S(1)}, u32[]{:S(2)}, u32[]{:S(2)}) %all-to-all-start) | async-done | bytes 655392 | tf_op jit(solution)/shard_map/all_to_all | solution.py:420
  168.9 2.3 %collective-permute-start.28 = (f32[2,5,80]{2,1,0:T(8,128)S(1)}, f32[2,5,80]{2,1,0:T(8,128)S(1)}, u32[]{:S(2)}, u32[]{:S(2)}) collective-permute-start(f32[2,5,80]{2,1,0:T(8,128)S(1)} %add_add_fusion.4), channel_id=1, source_target_pairs={{0,2},{1,3},{2,0},{3,1},{4,6},{5,7},{6,4},{7,5},{8,10},{9,11},{10,... | collective-permute-start | bytes 9608 | tf_op jit(solution)/shard_map/ppermute | solution.py:45
  174.9 2.8 %collective-permute-start.32 = (f32[2,5,80]{2,1,0:T(8,128)S(1)}, f32[2,5,80]{2,1,0:T(8,128)S(1)}, u32[]{:S(2)}, u32[]{:S(2)}) collective-permute-start(f32[2,5,80]{2,1,0:T(8,128)S(1)} %add_add_fusion.3), channel_id=1, source_target_pairs={{0,68},{1,69},{2,70},{3,71},{4,64},{5,65},{6,66},{7,67},{8,76},{9,... | collective-permute-start | bytes 9608 | tf_op jit(solution)/shard_map/ppermute | solution.py:45
  179.8 3.1 %collective-permute-done.31 = f32[2,5,80]{2,1,0:T(8,128)S(1)} collective-permute-done((f32[2,5,80]{2,1,0:T(8,128)S(1)}, f32[2,5,80]{2,1,0:T(8,128)S(1)}, u32[]{:S(2)}, u32[]{:S(2)}) %collective-permute-start.31) | collective-permute-done | bytes 3232 | tf_op jit(solution)/shard_map/ppermute | solution.py:45
  (99 shorter events, 43.9 us)
Async XLA Ops:
  11.0 6.1 %collective-permute-start.1 = (f32[8,1536]{1,0:T(8,128)S(1)}, f32[8,1536]{1,0:T(8,128)S(1)}, u32[]{:S(2)}, u32[]{:S(2)}) collective-permute-start(f32[8,1536]{1,0:T(8,128)S(1)} %add.154), channel_id=1, source_target_pairs={{0,64},{8,72},{16,80},{24,88},{32,96},{40,104},{48,112},{56,120},{... | collective-permute-start | bytes 147464 | tf_op jit(solution)/shard_map/ppermute | solution.py:45
  17.1 5.4 %collective-permute-start.4 = (f32[8,1536]{1,0:T(8,128)S(1)}, f32[8,1536]{1,0:T(8,128)S(1)}, u32[]{:S(2)}, u32[]{:S(2)}) collective-permute-start(f32[8,1536]{1,0:T(8,128)S(1)} %add.155), channel_id=1, source_target_pairs={{0,48},{8,56},{16,32},{24,40},{32,16},{40,24},{48,0},{56,8},{64,11... | collective-permute-start | bytes 147464 | tf_op jit(solution)/shard_map/ppermute | solution.py:45
  19.9 5.6 %collective-permute-start.3 = (f32[8,1536]{1,0:T(8,128)S(1)}, f32[8,1536]{1,0:T(8,128)S(1)}, u32[]{:S(2)}, u32[]{:S(2)}) collective-permute-start(f32[8,1536]{1,0:T(8,128)S(1)} %add.155), channel_id=1, source_target_pairs={{0,32},{8,40},{16,48},{24,56},{32,0},{40,8},{48,16},{56,24},{64,96... | collective-permute-start | bytes 147464 | tf_op jit(solution)/shard_map/ppermute | solution.py:45
  20.7 4.8 %collective-permute-start.2 = (f32[8,1536]{1,0:T(8,128)S(1)}, f32[8,1536]{1,0:T(8,128)S(1)}, u32[]{:S(2)}, u32[]{:S(2)}) collective-permute-start(f32[8,1536]{1,0:T(8,128)S(1)} %add.155), channel_id=1, source_target_pairs={{0,16},{8,24},{16,0},{24,8},{32,48},{40,56},{48,32},{56,40},{64,80... | collective-permute-start | bytes 147464 | tf_op jit(solution)/shard_map/ppermute | solution.py:45
  36.9 1.7 collective-permute-start.5
  38.7 4.7 %collective-permute-start.6 = (f32[56,384]{1,0:T(8,128)S(1)}, f32[56,384]{1,0:T(8,128)S(1)}, u32[]{:S(2)}, u32[]{:S(2)}) collective-permute-start(f32[56,384]{1,0:T(8,128)S(1)} %get-tuple-element.42), channel_id=1, source_target_pairs={{0,16},{8,24},{16,0},{24,8},{32,48},{40,56},{48,32},{56,40},{64,80... | collective-permute-start | bytes 258056 | tf_op jit(solution)/shard_map/ppermute | solution.py:45
  39.0 6.2 %collective-permute-start.8 = (f32[56,384]{1,0:T(8,128)S(1)}, f32[56,384]{1,0:T(8,128)S(1)}, u32[]{:S(2)}, u32[]{:S(2)}) collective-permute-start(f32[56,384]{1,0:T(8,128)S(1)} %get-tuple-element.43), channel_id=1, source_target_pairs={{0,48},{8,56},{16,32},{24,40},{32,16},{40,24},{48,0},{56,8},{64,11... | collective-permute-start | bytes 258056 | tf_op jit(solution)/shard_map/ppermute | solution.py:45
  41.3 6.0 %collective-permute-start.7 = (f32[56,384]{1,0:T(8,128)S(1)}, f32[56,384]{1,0:T(8,128)S(1)}, u32[]{:S(2)}, u32[]{:S(2)}) collective-permute-start(f32[56,384]{1,0:T(8,128)S(1)} %get-tuple-element.44), channel_id=1, source_target_pairs={{0,32},{8,40},{16,48},{24,56},{32,0},{40,8},{48,16},{56,24},{64,96... | collective-permute-start | bytes 258056 | tf_op jit(solution)/shard_map/ppermute | solution.py:45
  47.4 6.1 %collective-permute-start.9 = (f32[56,384]{1,0:T(8,128)S(1)}, f32[56,384]{1,0:T(8,128)S(1)}, u32[]{:S(2)}, u32[]{:S(2)}) collective-permute-start(f32[56,384]{1,0:T(8,128)S(1)} %add_add_fusion.1), channel_id=1, source_target_pairs={{0,64},{8,72},{16,80},{24,88},{32,96},{40,104},{48,112},{56,120},{... | collective-permute-start | bytes 258056 | tf_op jit(solution)/shard_map/ppermute | solution.py:45
  53.4 4.8 %collective-permute-start.12 = (f32[56,384]{1,0:T(8,128)S(1)}, f32[56,384]{1,0:T(8,128)S(1)}, u32[]{:S(2)}, u32[]{:S(2)}) collective-permute-start(f32[56,384]{1,0:T(8,128)S(1)} %add.168), channel_id=1, source_target_pairs={{0,16},{8,24},{16,0},{24,8},{32,48},{40,56},{48,32},{56,40},{64,80... | collective-permute-start | bytes 258056 | tf_op jit(solution)/shard_map/ppermute | solution.py:45
  53.7 6.1 %collective-permute-start.11 = (f32[56,384]{1,0:T(8,128)S(1)}, f32[56,384]{1,0:T(8,128)S(1)}, u32[]{:S(2)}, u32[]{:S(2)}) collective-permute-start(f32[56,384]{1,0:T(8,128)S(1)} %add.168), channel_id=1, source_target_pairs={{0,32},{8,40},{16,48},{24,56},{32,0},{40,8},{48,16},{56,24},{64,96... | collective-permute-start | bytes 258056 | tf_op jit(solution)/shard_map/ppermute | solution.py:45
  56.5 5.7 %collective-permute-start.10 = (f32[56,384]{1,0:T(8,128)S(1)}, f32[56,384]{1,0:T(8,128)S(1)}, u32[]{:S(2)}, u32[]{:S(2)}) collective-permute-start(f32[56,384]{1,0:T(8,128)S(1)} %add.168), channel_id=1, source_target_pairs={{0,48},{8,56},{16,32},{24,40},{32,16},{40,24},{48,0},{56,8},{64,11... | collective-permute-start | bytes 258056 | tf_op jit(solution)/shard_map/ppermute | solution.py:45
  62.2 1.7 collective-permute-start.13
  74.5 8.1 %collective-permute-start.14 = (f32[208,1536]{1,0:T(8,128)S(1)}, f32[208,1536]{1,0:T(8,128)S(1)}, u32[]{:S(2)}, u32[]{:S(2)}) collective-permute-start(f32[208,1536]{1,0:T(8,128)S(1)} %shard_map.62), channel_id=1, source_target_pairs={{0,8},{8,0},{16,24},{24,16},{32,40},{40,32},{48,56},{56,48},{64,72... | collective-permute-start | bytes 3833864 | tf_op jit(solution)/shard_map/ppermute | solution.py:45
  84.8 10.6 %collective-permute-start.15 = (f32[208,384]{1,0:T(8,128)}, f32[208,384]{1,0:T(8,128)S(1)}, u32[]{:S(2)}, u32[]{:S(2)}) collective-permute-start(f32[208,384]{1,0:T(8,128)} %get-tuple-element.33), channel_id=1, source_target_pairs={{0,16},{8,24},{16,0},{24,8},{32,48},{40,56},{48,32},{56,40},{64,80... | collective-permute-start | bytes 958472 | tf_op jit(solution)/shard_map/ppermute | solution.py:45
  84.8 16.3 %collective-permute-start.17 = (f32[208,384]{1,0:T(8,128)}, f32[208,384]{1,0:T(8,128)}, u32[]{:S(2)}, u32[]{:S(2)}) collective-permute-start(f32[208,384]{1,0:T(8,128)} %get-tuple-element.34), channel_id=1, source_target_pairs={{0,48},{8,56},{16,32},{24,40},{32,16},{40,24},{48,0},{56,8},{64,11... | collective-permute-start | bytes 958472 | tf_op jit(solution)/shard_map/ppermute | solution.py:45
  86.6 16.4 %collective-permute-start.16 = (f32[208,384]{1,0:T(8,128)}, f32[208,384]{1,0:T(8,128)}, u32[]{:S(2)}, u32[]{:S(2)}) collective-permute-start(f32[208,384]{1,0:T(8,128)} %get-tuple-element.35), channel_id=1, source_target_pairs={{0,32},{8,40},{16,48},{24,56},{32,0},{40,8},{48,16},{56,24},{64,96... | collective-permute-start | bytes 958472 | tf_op jit(solution)/shard_map/ppermute | solution.py:45
  104.2 10.8 %collective-permute-start.18 = (f32[208,384]{1,0:T(8,128)S(1)}, f32[208,384]{1,0:T(8,128)S(1)}, u32[]{:S(2)}, u32[]{:S(2)}) collective-permute-start(f32[208,384]{1,0:T(8,128)S(1)} %add_add_fusion), channel_id=1, source_target_pairs={{0,64},{8,72},{16,80},{24,88},{32,96},{40,104},{48,112},{56,120},{... | collective-permute-start | bytes 958472 | tf_op jit(solution)/shard_map/ppermute | solution.py:45
  115.6 10.6 %collective-permute-start.21 = (f32[208,384]{1,0:T(8,128)S(1)}, f32[208,384]{1,0:T(8,128)S(1)}, u32[]{:S(2)}, u32[]{:S(2)}) collective-permute-start(f32[208,384]{1,0:T(8,128)S(1)} %pad_maximum_fusion.2), channel_id=1, source_target_pairs={{0,16},{8,24},{16,0},{24,8},{32,48},{40,56},{48,32},{56,40},{64,80... | collective-permute-start | bytes 958472 | tf_op jit(solution)/shard_map/ppermute | solution.py:45
  115.7 16.0 %collective-permute-start.20 = (f32[208,384]{1,0:T(8,128)S(1)}, f32[208,384]{1,0:T(8,128)S(1)}, u32[]{:S(2)}, u32[]{:S(2)}) collective-permute-start(f32[208,384]{1,0:T(8,128)S(1)} %pad_maximum_fusion.2), channel_id=1, source_target_pairs={{0,32},{8,40},{16,48},{24,56},{32,0},{40,8},{48,16},{56,24},{64,96... | collective-permute-start | bytes 958472 | tf_op jit(solution)/shard_map/ppermute | solution.py:45
  118.7 15.6 %collective-permute-start.19 = (f32[208,384]{1,0:T(8,128)S(1)}, f32[208,384]{1,0:T(8,128)S(1)}, u32[]{:S(2)}, u32[]{:S(2)}) collective-permute-start(f32[208,384]{1,0:T(8,128)S(1)} %pad_maximum_fusion.2), channel_id=1, source_target_pairs={{0,48},{8,56},{16,32},{24,40},{32,16},{40,24},{48,0},{56,8},{64,11... | collective-permute-start | bytes 958472 | tf_op jit(solution)/shard_map/ppermute | solution.py:45
  134.6 3.1 %collective-permute-start.22 = (f32[208,1536]{1,0:T(8,128)S(1)}, f32[208,1536]{1,0:T(8,128)S(1)}, u32[]{:S(2)}, u32[]{:S(2)}) collective-permute-start(f32[208,1536]{1,0:T(8,128)S(1)} %pad_maximum_fusion.own_ref), channel_id=1, source_target_pairs={{0,8},{8,0},{16,24},{24,16},{32,40},{40,32},{48,56},{56,48},{64,72... | collective-permute-start | bytes 3833864 | tf_op jit(solution)/shard_map/ppermute | solution.py:45
  144.3 16.8 %all-to-all-start = ((f32[8,80,256]{2,1,0:T(8,128)}), f32[8,80,256]{2,1,0:T(8,128)S(1)}, u32[]{:S(2)}, u32[]{:S(2)}) async-start(f32[8,80,256]{2,1,0:T(8,128)} %get-tuple-element.17), calls=%async_computation | async-start | bytes 1310720 | tf_op jit(solution)/shard_map/all_to_all | solution.py:420
  162.6 5.2 %collective-permute-start.25 = (f32[2,5,80]{2,1,0:T(8,128)S(1)}, f32[2,5,80]{2,1,0:T(8,128)S(1)}, u32[]{:S(2)}, u32[]{:S(2)}) collective-permute-start(f32[2,5,80]{2,1,0:T(8,128)S(1)} %fusion.18), channel_id=1, source_target_pairs={{0,32},{8,40},{16,48},{24,56},{32,0},{40,8},{48,16},{56,24},{64,96... | collective-permute-start | bytes 9608 | tf_op jit(solution)/shard_map/ppermute | solution.py:45
  162.6 5.1 %collective-permute-start.26 = (f32[2,5,80]{2,1,0:T(8,128)S(1)}, f32[2,5,80]{2,1,0:T(8,128)S(1)}, u32[]{:S(2)}, u32[]{:S(2)}) collective-permute-start(f32[2,5,80]{2,1,0:T(8,128)S(1)} %fusion.18), channel_id=1, source_target_pairs={{0,48},{8,56},{16,32},{24,40},{32,16},{40,24},{48,0},{56,8},{64,11... | collective-permute-start | bytes 9608 | tf_op jit(solution)/shard_map/ppermute | solution.py:45
  164.7 3.7 %collective-permute-start.24 = (f32[2,5,80]{2,1,0:T(8,128)S(1)}, f32[2,5,80]{2,1,0:T(8,128)S(1)}, u32[]{:S(2)}, u32[]{:S(2)}) collective-permute-start(f32[2,5,80]{2,1,0:T(8,128)S(1)} %fusion.18), channel_id=1, source_target_pairs={{0,16},{8,24},{16,0},{24,8},{32,48},{40,56},{48,32},{56,40},{64,80... | collective-permute-start | bytes 9608 | tf_op jit(solution)/shard_map/ppermute | solution.py:45
  168.3 4.9 %collective-permute-start.29 = (f32[2,5,80]{2,1,0:T(8,128)S(1)}, f32[2,5,80]{2,1,0:T(8,128)S(1)}, u32[]{:S(2)}, u32[]{:S(2)}) collective-permute-start(f32[2,5,80]{2,1,0:T(8,128)S(1)} %add_add_fusion.4), channel_id=1, source_target_pairs={{0,3},{1,2},{2,1},{3,0},{4,7},{5,6},{6,5},{7,4},{8,11},{9,10},{10,... | collective-permute-start | bytes 9608 | tf_op jit(solution)/shard_map/ppermute | solution.py:45
  168.9 5.2 %collective-permute-start.28 = (f32[2,5,80]{2,1,0:T(8,128)S(1)}, f32[2,5,80]{2,1,0:T(8,128)S(1)}, u32[]{:S(2)}, u32[]{:S(2)}) collective-permute-start(f32[2,5,80]{2,1,0:T(8,128)S(1)} %add_add_fusion.4), channel_id=1, source_target_pairs={{0,2},{1,3},{2,0},{3,1},{4,6},{5,7},{6,4},{7,5},{8,10},{9,11},{10,... | collective-permute-start | bytes 9608 | tf_op jit(solution)/shard_map/ppermute | solution.py:45
  171.3 3.7 %collective-permute-start.27 = (f32[2,5,80]{2,1,0:T(8,128)S(1)}, f32[2,5,80]{2,1,0:T(8,128)S(1)}, u32[]{:S(2)}, u32[]{:S(2)}) collective-permute-start(f32[2,5,80]{2,1,0:T(8,128)S(1)} %add_add_fusion.4), channel_id=1, source_target_pairs={{0,1},{1,0},{2,3},{3,2},{4,5},{5,4},{6,7},{7,6},{8,9},{9,8},{10,11... | collective-permute-start | bytes 9608 | tf_op jit(solution)/shard_map/ppermute | solution.py:45
  174.9 4.9 %collective-permute-start.32 = (f32[2,5,80]{2,1,0:T(8,128)S(1)}, f32[2,5,80]{2,1,0:T(8,128)S(1)}, u32[]{:S(2)}, u32[]{:S(2)}) collective-permute-start(f32[2,5,80]{2,1,0:T(8,128)S(1)} %add_add_fusion.3), channel_id=1, source_target_pairs={{0,68},{1,69},{2,70},{3,71},{4,64},{5,65},{6,66},{7,67},{8,76},{9,... | collective-permute-start | bytes 9608 | tf_op jit(solution)/shard_map/ppermute | solution.py:45
  177.7 5.2 %collective-permute-start.31 = (f32[2,5,80]{2,1,0:T(8,128)S(1)}, f32[2,5,80]{2,1,0:T(8,128)S(1)}, u32[]{:S(2)}, u32[]{:S(2)}) collective-permute-start(f32[2,5,80]{2,1,0:T(8,128)S(1)} %add_add_fusion.3), channel_id=1, source_target_pairs={{0,64},{1,65},{2,66},{3,67},{4,68},{5,69},{6,70},{7,71},{8,72},{9,... | collective-permute-start | bytes 9608 | tf_op jit(solution)/shard_map/ppermute | solution.py:45
  178.6 4.3 %collective-permute-start.30 = (f32[2,5,80]{2,1,0:T(8,128)S(1)}, f32[2,5,80]{2,1,0:T(8,128)S(1)}, u32[]{:S(2)}, u32[]{:S(2)}) collective-permute-start(f32[2,5,80]{2,1,0:T(8,128)S(1)} %add_add_fusion.3), channel_id=1, source_target_pairs={{0,4},{1,5},{2,6},{3,7},{4,0},{5,1},{6,2},{7,3},{8,12},{9,13},{10,... | collective-permute-start | bytes 9608 | tf_op jit(solution)/shard_map/ppermute | solution.py:45
  (12 other events, 139.8 us)

commit v4 on v3

--- a/solution.py
+++ b/solution.py
@@ -50,13 +50,6 @@
     return high, (values - high.astype(jnp.float32)).astype(jnp.bfloat16)
 
 
-def order4(parts, place):
-    low, high = (place & 1) == 1, (place & 2) == 2
-    a, b, c, d = parts
-    a, b, c, d = (jnp.where(low, b, a), jnp.where(low, a, b), jnp.where(low, d, c), jnp.where(low, c, d))
-    return jnp.where(high, c, a), jnp.where(high, d, b), jnp.where(high, a, c), jnp.where(high, b, d)
-
-
 def all_sum(values, bits):
     for axis, group in bits:
         got = [swap(values, axis, bit) for bit in group]
@@ -69,19 +62,39 @@
 ALL_BITS = (("samp", (1,)), ("samp", (2, 4, 6)), ("blk", (1, 2, 3)), (BOTH, (4, 64, 68)))
 
 
-def scatter_chips(kept, place):
-    width = kept.shape[1] // 4
-    got = [
-        swap(lax.dynamic_slice_in_dim(kept, (place ^ k) * width, width, 1), "samp", 2 * k) for k in (1, 2, 3)
-    ]
-    mine = lax.dynamic_slice_in_dim(kept, place * width, width, 1)
-    mine = (mine + got[0]) + (got[1] + got[2])
-    return mine + swap(mine, "samp", 8)
-
-
-def gather_chips(piece, place):
-    parts = [piece] + [swap(piece, "samp", 2 * k) for k in (1, 2, 3)]
-    return jnp.concatenate(order4(parts, place), axis=1)
+def here():
+    samp = lax.axis_index("samp")
+    return samp & 1, (samp >> 1) & 3
+
+
+def split_kernel(kept_ref, got_ref, *out_refs):
+    width = out_refs[0].shape[1]
+    place = here()[1]
+    for k, out_ref in enumerate(out_refs):
+        lanes = pl.ds(pl.multiple_of((place ^ k) * width, 128), width)
+        out_ref[...] = kept_ref[:, lanes] + got_ref[:, lanes]
+
+
+def scatter_chips(kept, got):
+    rows, width = kept.shape
+    mine, *sent = pl.pallas_call(
+        split_kernel,
+        in_specs=whole(2),
+        out_specs=whole(4),
+        out_shape=[jax.ShapeDtypeStruct((rows, width // 4), jnp.float32)] * 4,
+        compiler_params=params(),
+    )(kept, got)
+    got = [swap(part, "samp", 2 * k) for k, part in zip((1, 2, 3), sent)]
+    return (mine + got[0]) + (got[1] + got[2])
+
+
+def gather_chips(piece):
+    own = jnp.stack([piece] + [swap(piece, "samp", 2 * k) for k in (1, 2, 3)])
+    return own, swap(own, "samp", 1)
+
+
+def lanes_of(place, k, width):
+    return pl.ds(pl.multiple_of((place ^ k) * width, 128), width)
 
 
 def whole(count):
@@ -177,7 +190,7 @@
     return soft_threshold(coeff - step_size * gradient, cutoff)
 
 
-def first_kernel(core_ref, stats_ref, dose_ref, kept_ref, sent_ref, table_ref, both_ref, total_ref):
+def first_kernel(stats_ref, dose_ref, kept_ref, sent_ref, table_ref, both_ref, total_ref):
     stats = stats_ref[...]
     mean = stats[5:6] / PEOPLE
     scales = jnp.sqrt(stats[6:7] / PEOPLE - mean * mean + epsilon)
@@ -225,26 +238,26 @@
     half = ROWS0 // 2
     first = total_ref[0:half] + total_ref[128 : 128 + half]
     second = total_ref[half:ROWS0] + total_ref[128 + half : 128 + ROWS0]
-    is_first = core_ref[0] == 0
+    is_first = here()[0] == 0
     kept_ref[...] = jnp.where(is_first, first, second)
     sent_ref[...] = jnp.where(is_first, second, first)
 
 
-def first_product(core, stats, dose):
+def first_product(stats, dose):
     width = dose.shape[1]
     half = jax.ShapeDtypeStruct((ROWS0 // 2, width), jnp.float32)
     return pl.pallas_call(
         first_kernel,
-        in_specs=[pl.BlockSpec(memory_space=pltpu.SMEM)] + whole(2),
+        in_specs=whole(2),
         out_specs=whole(3),
         out_shape=[half, half, jax.ShapeDtypeStruct((16, width), jnp.float32)],
         scratch_shapes=[pltpu.VMEM((256, width), jnp.bfloat16), pltpu.VMEM((256, width), jnp.float32)],
         compiler_params=params(),
-    )(core, stats, dose)
+    )(stats, dose)
 
 
 def second_kernel(
-    core_ref, table_ref, own_ref, other_ref, dose_ref, out_ref, product_ref, coeff_ref, both_ref, *, mine
+    table_ref, own_ref, other_ref, dose_ref, out_ref, product_ref, coeff_ref, both_ref, *, mine
 ):
     rows = 2 * ROWS1
     half = ROWS0 // 2
@@ -252,11 +265,13 @@
     row, fold_of, cutoff = base_rows(ROWS1)
     target = spread(table[:FOLDS], fold_of)
     coeff = soft_threshold(step_size * target, cutoff)
-    is_first = core_ref[0] == 0
-    product_ref[0:half] = jnp.where(is_first, own_ref[...], other_ref[...])
-    product_ref[half:] = jnp.where(is_first, other_ref[...], own_ref[...])
+    core, place = here()
+    for k in range(4):
+        lanes = lanes_of(place, k, own_ref.shape[2])
+        product_ref[0:half, lanes] = jnp.where(core == 0, own_ref[k], other_ref[k])
+        product_ref[half:, lanes] = jnp.where(core == 0, other_ref[k], own_ref[k])
     product = product_ref[0:ROWS1] * (table[7:8] / PEOPLE)
-    side = core_ref[0] if mine else 1 - core_ref[0]
+    side = core if mine else 1 - core
     for group in range(2):
         shrink = shrink_unit * (2 * side + group + 1).astype(jnp.float32)
         new = next_coeff(coeff, product, target, shrink, cutoff)
@@ -280,12 +295,12 @@
     lax.fori_loop(0, dose_ref.shape[0] // TILE, body, offset)
 
 
-def second_product(core, table, own, other, dose, mine):
+def second_product(table, own, other, dose, mine):
     people, width = dose.shape
     rows = 2 * ROWS1
     return pl.pallas_call(
         functools.partial(second_kernel, mine=mine),
-        in_specs=[pl.BlockSpec(memory_space=pltpu.SMEM)] + whole(4),
+        in_specs=whole(4),
         out_specs=pl.BlockSpec(memory_space=pltpu.VMEM),
         out_shape=jax.ShapeDtypeStruct((rows, width), jnp.float32),
         scratch_shapes=[
@@ -297,32 +312,65 @@
         cost_estimate=pl.CostEstimate(
             flops=8 * people * width * rows, bytes_accessed=2 * people * width, transcendentals=0
         ),
-    )(core, table, own, other, dose)
+    )(table, own, other, dose)
+
+
+def finish_kernel(table_ref, own_ref, other_ref, mine_ref, got_ref, out_ref):
+    core, place = here()
+    half, width = own_ref.shape
+    table = table_ref[:, lanes_of(place, 0, width)]
+    row, fold_of, cutoff = base_rows(ROWS1)
+    target = spread(table[:FOLDS], fold_of)
+    coeff = soft_threshold(step_size * target, cutoff)
+    scale = table[7:8] / PEOPLE
+    low = jnp.where(core == 0, own_ref[...], other_ref[...])
+    high = jnp.where(core == 0, other_ref[...], own_ref[...])
+    old = jnp.concatenate([low, high], axis=0)[:ROWS1] * scale
+    for group in range(2):
+        shrink = shrink_unit * (2 * core + group + 1).astype(jnp.float32)
+        new = next_coeff(coeff, old, target, shrink, cutoff)
+        span = slice(group * ROWS1, (group + 1) * ROWS1)
+        out_ref[span] = next_coeff(new, (mine_ref[span] + got_ref[span]) * scale, target, shrink, cutoff)
+
+
+def finish(table, own, other, mine, got):
+    return pl.pallas_call(
+        finish_kernel,
+        in_specs=whole(5),
+        out_specs=pl.BlockSpec(memory_space=pltpu.VMEM),
+        out_shape=jax.ShapeDtypeStruct(mine.shape, jnp.float32),
+        compiler_params=params(),
+    )(table, own, other, mine, got)
 
 
 def predict_kernel(
-    core_ref, own_ref, other_ref, table_ref, fold_ref, dose_ref,
+    own_ref, other_ref, table_ref, fold_ref, dose_ref,
     coeff_out, number_out, score_out, coeff_ref, wide_ref, weight_ref, offset_ref,
 ):
-    half, width = own_ref.shape
-
-    def place(first_ref, second_ref):
-        for lane in range(width // 128):
-            lanes = slice(lane * 128, (lane + 1) * 128)
-            coeff_ref[lane, 0:half] = first_ref[:, lanes]
-            coeff_ref[lane, half:] = second_ref[:, lanes]
-        for group in range(SHRINKS):
-            ref = first_ref if group < 2 else second_ref
-            start = group % 2 * ROWS1
-            coeff_out[group * BASE : (group + 1) * BASE] = ref[start : start + BASE]
-
-    @pl.when(core_ref[0] == 0)
+    core, place = here()
+    _, half, quarter = own_ref.shape
+    width = dose_ref.shape[1]
+
+    def order(first_ref, second_ref):
+        for k in range(4):
+            lanes = lanes_of(place, k, quarter)
+            for part in range(quarter // 128):
+                span = slice(part * 128, (part + 1) * 128)
+                lane = (place ^ k) * (quarter // 128) + part
+                coeff_ref[lane, 0:half] = first_ref[k, :, span]
+                coeff_ref[lane, half:] = second_ref[k, :, span]
+            for group in range(SHRINKS):
+                ref = first_ref if group < 2 else second_ref
+                start = group % 2 * ROWS1
+                coeff_out[group * BASE : (group + 1) * BASE, lanes] = ref[k, start : start + BASE]
+
+    @pl.when(core == 0)
     def _():
-        place(own_ref, other_ref)
-
-    @pl.when(core_ref[0] != 0)
+        order(own_ref, other_ref)
+
+    @pl.when(core != 0)
     def _():
-        place(other_ref, own_ref)
+        order(other_ref, own_ref)
 
     for lane in range(width // 128):
         lanes = slice(lane * 128, (lane + 1) * 128)
@@ -334,7 +382,7 @@
     table = table_ref[...]
     for fold in range(FOLDS):
         span = slice(fold * LEVELS, (fold + 1) * LEVELS)
-        weighted = (wide_ref[span] / table[6:7]).astype(jnp.bfloat16)
+        weighted = (wide_ref[span] * table[7:8]).astype(jnp.bfloat16)
         weight_ref[span] = weighted
         wide = weighted.astype(jnp.float32)
         offset_ref[span] = jnp.sum(wide * table[5:6], axis=1, keepdims=True)
@@ -355,12 +403,12 @@
     lax.fori_loop(0, parts, body, 0)
 
 
-def predict(core, own, other, table, fold_ids, dose, parts):
+def predict(own, other, table, fold_ids, dose, parts):
     people, width = dose.shape
-    half = own.shape[0]
+    half = own.shape[1]
     return pl.pallas_call(
         predict_kernel,
-        in_specs=[pl.BlockSpec(memory_space=pltpu.SMEM)] + whole(5),
+        in_specs=whole(5),
         out_specs=whole(3),
         out_shape=[
             jax.ShapeDtypeStruct((GRID, width), jnp.float32),
@@ -374,60 +422,60 @@
             pltpu.VMEM((GRID, 1), jnp.float32),
         ],
         compiler_params=params(),
-    )(core, own, other, table, fold_ids.reshape(1, people), dose)
+    )(own, other, table, fold_ids.reshape(1, people), dose)
+
+
+def score_kernel(scores_ref, fold_ref, number_ref, out_ref):
+    blocks, rows, people = scores_ref.shape
+    start = pl.multiple_of(lax.axis_index("blk") * people, 128)
+    folds = fold_ref[:, pl.ds(start, people)]
+    scores = scores_ref[0]
+    for block in range(1, blocks):
+        scores = scores + scores_ref[block]
+    square = scores * scores
+    lane = lax.broadcasted_iota(jnp.int32, out_ref.shape, 1)
+    out = jnp.zeros(out_ref.shape, jnp.float32)
+    for fold in range(FOLDS):
+        sums = jnp.sum(jnp.where(folds == fold, square, 0.0), axis=1, keepdims=True)
+        out = jnp.where(lane == FOLDS + fold, sums, out)
+        number = number_ref[fold * LEVELS : (fold + 1) * LEVELS] * (1.0 / lax.axis_size("samp"))
+        out = jnp.where(lane == fold, number, out)
+    out_ref[...] = out
+
+
+def score_sums(scores, fold_ids, number):
+    return pl.pallas_call(
+        score_kernel,
+        in_specs=whole(3),
+        out_specs=pl.BlockSpec(memory_space=pltpu.VMEM),
+        out_shape=jax.ShapeDtypeStruct((LEVELS, 128), jnp.float32),
+        compiler_params=params(),
+    )(scores, fold_ids.reshape(1, -1), number)
 
 
 def local(genotypes, phenotype, fold_ids):
-    num_rows, block_width = genotypes.shape
-    samp, blk = lax.axis_index("samp"), lax.axis_index("blk")
-    core, place = samp & 1, (samp >> 1) & 3
-
     dose, stats = prepare(genotypes, phenotype, fold_ids)
     stats = all_sum(stats, SAMP_BITS)
-    fold_count = stats[7, :FOLDS][:, None]
-
-    kept, sent, table = first_product(core[None], stats, dose)
-    piece = scatter_chips(kept + swap(sent, "samp", 1), place)
-    own_product = gather_chips(piece, place)
-    other_product = swap(own_product, "samp", 1)
-
-    sent = second_product(core[None], table, own_product, other_product, dose, False)
+
+    kept, sent, table = first_product(stats, dose)
+    piece = scatter_chips(kept, swap(sent, "samp", 1))
+    own_product, other_product = gather_chips(piece + swap(piece, "samp", 8))
+
+    sent = second_product(table, own_product, other_product, dose, False)
     sent = swap(sent, "samp", 1)
-    kept = second_product(core[None], table, own_product, other_product, dose, True)
-    piece = scatter_chips(kept + sent, place)
-    width = block_width // 4
-    here = lambda a: lax.dynamic_slice_in_dim(a, place * width, width, 1)
-    row, fold_of, cutoff = base_rows(ROWS1)
-    table_here = here(table)
-    target = spread(table_here[:FOLDS], fold_of)
-    coeff = soft_threshold(step_size * target, cutoff)
-    scale_here = table_here[7:8] / PEOPLE
-    first = core == 0
-    own, other = here(own_product), here(other_product)
-    old = jnp.concatenate([jnp.where(first, own, other), jnp.where(first, other, own)], axis=0)
-    old = old[:ROWS1] * scale_here
-    final = []
-    for group in range(2):
-        shrink = shrink_unit * (2 * core + group + 1).astype(jnp.float32)
-        new = next_coeff(coeff, old, target, shrink, cutoff)
-        latest = piece[group * ROWS1 : (group + 1) * ROWS1] * scale_here
-        final.append(next_coeff(new, latest, target, shrink, cutoff))
-    own = gather_chips(jnp.concatenate(final, axis=0), place)
-    other = swap(own, "samp", 1)
+    kept = second_product(table, own_product, other_product, dose, True)
+    piece = scatter_chips(kept, sent)
+    piece = finish(table, own_product[0], other_product[0], piece, swap(piece, "samp", 8))
+    own, other = gather_chips(piece)
 
     blocks = lax.axis_size("blk")
-    coeff_all, numerator, scores = predict(core[None], own, other, table, fold_ids, dose, blocks)
-    scores = jnp.sum(lax.all_to_all(scores, "blk", 0, 0, tiled=True), axis=0)
-    people = num_rows // blocks
-    folds_here = lax.dynamic_slice_in_dim(fold_ids, blk * people, people, 0)
-    square = scores * scores
-    denominator = jnp.stack(
-        [jnp.sum(jnp.where((folds_here == fold)[None, :], square, 0.0), axis=1) for fold in range(FOLDS)]
-    )
-    sums = jnp.stack([numerator.reshape(FOLDS, LEVELS) / lax.axis_size("samp"), denominator])
-    sums = all_sum(sums, ALL_BITS)
-    sums = sums * jnp.array([1.0 / math.sqrt(SNPS), 1.0 / SNPS], jnp.float32)[:, None, None] / fold_count[None]
-    fold_scores = sums.transpose(0, 2, 1).reshape(2, GRID)
+    coeff_all, numerator, scores = predict(own, other, table, fold_ids, dose, blocks)
+    scores = lax.all_to_all(scores, "blk", 0, 0, tiled=True)
+    sums = all_sum(score_sums(scores, fold_ids, numerator), ALL_BITS)
+    counts = stats[7, :FOLDS]
+    numerator = sums[:, :FOLDS] / (math.sqrt(SNPS) * counts)
+    denominator = sums[:, FOLDS : 2 * FOLDS] / (SNPS * counts)
+    fold_scores = jnp.stack([numerator.reshape(GRID), denominator.reshape(GRID)])
     return (coeff_all.T, fold_scores)
 
 

time: 184 us -> 173 us (0.940)
  blocking collectives: 0 us -> 16.5 us
  local copies, waits for them, and re-layouts: 12.7 us -> 1.71 us
  waiting for transfers between devices: 80.9 us -> 70.1 us
  starting transfers between devices: 50.6 us -> 46.6 us
  other arithmetic: 3.09 us -> 0.99 us
    all_to_all x0 -> x1, blocking collectives: none -> 16.5 us  [local(): scores = lax.all_to_all(scores, 'blk', 0, 0, tiled=True)]
    all_to_all x1 -> x0, waiting for transfers between devices: 11.5 us -> none  [local(): scores = jnp.sum(lax.all_to_all(scores, 'blk', 0, 0, tiled=True), axis=0)]
    unnamed x20 -> x4, local copies, waits for them, and re-layouts: 10.7 us -> 1.39 us
    all_to_all x1 -> x0, starting transfers between devices: 4.99 us -> none  [local(): scores = jnp.sum(lax.all_to_all(scores, 'blk', 0, 0, tiled=True), axis=0)]
    pallas_call x4 -> x8, Pallas kernels: 30.5 us -> 31.1 us  [the longest x2 15.5 us: second_product(): pl.pallas_call(functools.partial(second_kernel, mine=mine), in_specs=whol...]
  transfers between devices with their start and end apart: 34 -> 33, of which waited for: 29 -> 27; matrix products, arithmetic and copies ran while one was open for 0% -> 0% of each run, Pallas kernels for 4% -> 4%
where the time goes in v4:
time: 173 us
  waiting for transfers between devices  70.1 us (41%)
  starting transfers between devices  46.6 us (27%)
  Pallas kernels  36.1 us (21%)
  blocking collectives  16.5 us (10%)
    ppermute x33, waiting for transfers between devices, swap(): return lax.ppermute(values, axis, [(i, i ^ bit) for i in range(size)])  70.1 us
    ppermute x33, starting transfers between devices, swap(): return lax.ppermute(values, axis, [(i, i ^ bit) for i in range(size)])  46.6 us
    all_to_all x1, blocking collectives, local(): scores = lax.all_to_all(scores, 'blk', 0, 0, tiled=True)  16.5 us
    pallas_call x2, Pallas kernels, second_product(): pl.pallas_call(functools.partial(second_kernel, mine=mine), in_specs=whol...  15.5 us
    pallas_call x1, Pallas kernels, first_product(): pl.pallas_call(first_kernel, in_specs=whole(2), out_specs=whole(3), out_s...  8.52 us
    pallas_call x1, Pallas kernels, predict(): pl.pallas_call(predict_kernel, in_specs=whole(5), out_specs=whole(3), out...  6.37 us
    pallas_call x1, Pallas kernels, prepare(): pl.pallas_call(prepare_kernel, in_specs=whole(2) + [pl.BlockSpec(memory_s...  5.06 us
  transfers between devices with their start and end apart: 33, of which 27 were waited for; matrix products, arithmetic and copies ran while one was open for 0% of the time, Pallas kernels for 4%

profile of v4, /device:TPU:0, one launch (start us, length us, event | category | flops | bytes accessed | tf_op | source)
XLA Modules:
  0.0 172.9 jit_solution(12557698785444495914)
XLA Ops:
  2.0 5.1 %shard_map.50 = (bf16[2048,1536]{1,0:T(8,128)(2,1)S(1)}, f32[8,1536]{1,0:T(8,128)S(1)}) custom-call(f32[1,2048]{1,0:T(1,128)S(1)} %bitcast.22, s32[1,2048]{1,0:T(1,128)S(1)} %bitcast.19, s32[2048,1536]{1,0:T(8,128)} %geno_ref.1), custom_call_target="tpu_custom_call" | custom-call | tf_op jit(solution)/shard_map/pallas_call | solution.py:157
  8.4 4.0 %collective-permute-start.1 = (f32[8,1536]{1,0:T(8,128)S(1)}, f32[8,1536]{1,0:T(8,128)S(1)}, u32[]{:S(2)}, u32[]{:S(2)}) collective-permute-start(f32[8,1536]{1,0:T(8,128)S(1)} %add.66), channel_id=1, source_target_pairs={{0,64},{8,72},{16,80},{24,88},{32,96},{40,104},{48,112},{56,120},{... | collective-permute-start | bytes 147464 | tf_op jit(solution)/shard_map/ppermute | solution.py:45
  12.4 2.1 %collective-permute-done.1 = f32[8,1536]{1,0:T(8,128)S(1)} collective-permute-done((f32[8,1536]{1,0:T(8,128)S(1)}, f32[8,1536]{1,0:T(8,128)S(1)}, u32[]{:S(2)}, u32[]{:S(2)}) %collective-permute-start.1) | collective-permute-done | bytes 49184 | tf_op jit(solution)/shard_map/ppermute | solution.py:45
  14.5 2.8 %collective-permute-start.4 = (f32[8,1536]{1,0:T(8,128)S(1)}, f32[8,1536]{1,0:T(8,128)S(1)}, u32[]{:S(2)}, u32[]{:S(2)}) collective-permute-start(f32[8,1536]{1,0:T(8,128)S(1)} %add.67), channel_id=1, source_target_pairs={{0,48},{8,56},{16,32},{24,40},{32,16},{40,24},{48,0},{56,8},{64,11... | collective-permute-start | bytes 147464 | tf_op jit(solution)/shard_map/ppermute | solution.py:45
  19.9 3.1 %collective-permute-done.3 = f32[8,1536]{1,0:T(8,128)S(1)} collective-permute-done((f32[8,1536]{1,0:T(8,128)S(1)}, f32[8,1536]{1,0:T(8,128)S(1)}, u32[]{:S(2)}, u32[]{:S(2)}) %collective-permute-start.3) | collective-permute-done | bytes 49184 | tf_op jit(solution)/shard_map/ppermute | solution.py:45
  23.0 8.5 %shard_map.51 = (f32[56,1536]{1,0:T(8,128)S(1)}, f32[56,1536]{1,0:T(8,128)S(1)}, f32[16,1536]{1,0:T(8,128)S(1)}) custom-call(f32[8,1536]{1,0:T(8,128)S(1)} %add_add_fusion.2.stats_ref, bf16[2048,1536]{1,0:T(8,128)(2,1)S(1)} %get-tuple-element.19.dose_ref), custom_call_target="tpu_custom_call" | custom-call | tf_op jit(solution)/shard_map/pallas_call | solution.py:249
  33.6 2.6 %collective-permute-start.7 = (f32[56,384]{1,0:T(8,128)S(1)}, f32[56,384]{1,0:T(8,128)S(1)}, u32[]{:S(2)}, u32[]{:S(2)}) collective-permute-start(f32[56,384]{1,0:T(8,128)S(1)} %get-tuple-element.25), channel_id=1, source_target_pairs={{0,32},{8,40},{16,48},{24,56},{32,0},{40,8},{48,16},{56,24},{64,96... | collective-permute-start | bytes 258056 | tf_op jit(solution)/shard_map/ppermute | solution.py:45
  36.2 1.8 %collective-permute-start.8 = (f32[56,384]{1,0:T(8,128)S(1)}, f32[56,384]{1,0:T(8,128)S(1)}, u32[]{:S(2)}, u32[]{:S(2)}) collective-permute-start(f32[56,384]{1,0:T(8,128)S(1)} %get-tuple-element.26), channel_id=1, source_target_pairs={{0,48},{8,56},{16,32},{24,40},{32,16},{40,24},{48,0},{56,8},{64,11... | collective-permute-start | bytes 258056 | tf_op jit(solution)/shard_map/ppermute | solution.py:45
  38.6 2.1 %collective-permute-done.7 = f32[56,384]{1,0:T(8,128)S(1)} collective-permute-done((f32[56,384]{1,0:T(8,128)S(1)}, f32[56,384]{1,0:T(8,128)S(1)}, u32[]{:S(2)}, u32[]{:S(2)}) %collective-permute-start.7) | collective-permute-done | bytes 86048 | tf_op jit(solution)/shard_map/ppermute | solution.py:45
  42.5 3.6 %collective-permute-start.9 = (f32[56,384]{1,0:T(8,128)S(1)}, f32[56,384]{1,0:T(8,128)S(1)}, u32[]{:S(2)}, u32[]{:S(2)}) collective-permute-start(f32[56,384]{1,0:T(8,128)S(1)} %add_add_fusion.1), channel_id=1, source_target_pairs={{0,64},{8,72},{16,80},{24,88},{32,96},{40,104},{48,112},{56,120},{... | collective-permute-start | bytes 258056 | tf_op jit(solution)/shard_map/ppermute | solution.py:45
  46.1 2.5 %collective-permute-done.9 = f32[56,384]{1,0:T(8,128)S(1)} collective-permute-done((f32[56,384]{1,0:T(8,128)S(1)}, f32[56,384]{1,0:T(8,128)S(1)}, u32[]{:S(2)}, u32[]{:S(2)}) %collective-permute-start.9) | collective-permute-done | bytes 86048 | tf_op jit(solution)/shard_map/ppermute | solution.py:45
  48.5 1.9 %collective-permute-start.12 = (f32[56,384]{1,0:T(8,128)S(1)}, f32[56,384]{1,0:T(8,128)S(1)}, u32[]{:S(2)}, u32[]{:S(2)}) collective-permute-start(f32[56,384]{1,0:T(8,128)S(1)} %add.74.own_ref), channel_id=1, source_target_pairs={{0,48},{8,56},{16,32},{24,40},{32,16},{40,24},{48,0},{56,8},{64,11... | collective-permute-start | bytes 258056 | tf_op jit(solution)/shard_map/ppermute | solution.py:45
  50.9 1.8 %collective-permute-start.10 = (f32[56,384]{1,0:T(8,128)S(1)}, f32[56,384]{1,0:T(8,128)S(1)}, u32[]{:S(2)}, u32[]{:S(2)}) collective-permute-start(f32[56,384]{1,0:T(8,128)S(1)} %add.74.own_ref), channel_id=1, source_target_pairs={{0,16},{8,24},{16,0},{24,8},{32,48},{40,56},{48,32},{56,40},{64,80... | collective-permute-start | bytes 258056 | tf_op jit(solution)/shard_map/ppermute | solution.py:45
  52.7 2.2 %collective-permute-done.12 = f32[56,384]{1,0:T(8,128)S(1)} collective-permute-done((f32[56,384]{1,0:T(8,128)S(1)}, f32[56,384]{1,0:T(8,128)S(1)}, u32[]{:S(2)}, u32[]{:S(2)}) %collective-permute-start.12) | collective-permute-done | bytes 86048 | tf_op jit(solution)/shard_map/ppermute | solution.py:45
  58.2 7.7 %shard_map.54 = f32[208,1536]{1,0:T(8,128)S(1)} custom-call(f32[16,1536]{1,0:T(8,128)S(1)} %get-tuple-element.20.table_ref, f32[4,56,384]{2,1,0:T(8,128)S(1)} %pad_maximum_fusion.1.own_ref, f32[4,56,384]{2,1,0:T(8,128)S(1)} %collective-permute-done.13.other_ref, bf16[2048,1536]{1,0:T(8,128)(2,1)S(1)} %get-tuple-element.19.dose_ref), custom_call_target="tpu_custom_call" | custom-call | flops 5234491392 | bytes 6291456 | tf_op jit(solution)/shard_map/pallas_call | solution.py:301
  66.4 7.7 %shard_map.53.kept_ref = f32[208,1536]{1,0:T(8,128)S(1)} custom-call(f32[16,1536]{1,0:T(8,128)S(1)} %get-tuple-element.20.table_ref, f32[4,56,384]{2,1,0:T(8,128)S(1)} %pad_maximum_fusion.1.own_ref, f32[4,56,384]{2,1,0:T(8,128)S(1)} %collective-permute-done.13.other_ref, bf16[2048,1536]{1,0:T(8,128)(2,1)S(1)} %get-tuple-element.19.dose_ref), custom_call_target="tpu_custom_call" | custom-call | flops 5234491392 | bytes 6291456 | tf_op jit(solution)/shard_map/pallas_call | solution.py:301
  75.1 2.2 %collective-permute-start.16 = (f32[208,384]{1,0:T(8,128)S(1)}, f32[208,384]{1,0:T(8,128)S(1)}, u32[]{:S(2)}, u32[]{:S(2)}) collective-permute-start(f32[208,384]{1,0:T(8,128)S(1)} %get-tuple-element.29), channel_id=1, source_target_pairs={{0,32},{8,40},{16,48},{24,56},{32,0},{40,8},{48,16},{56,24},{64,96... | collective-permute-start | bytes 958472 | tf_op jit(solution)/shard_map/ppermute | solution.py:45
  79.1 5.7 %collective-permute-done.15 = f32[208,384]{1,0:T(8,128)S(1)} collective-permute-done((f32[208,384]{1,0:T(8,128)S(1)}, f32[208,384]{1,0:T(8,128)S(1)}, u32[]{:S(2)}, u32[]{:S(2)}) %collective-permute-start.15) | collective-permute-done | bytes 319520 | tf_op jit(solution)/shard_map/ppermute | solution.py:45
  84.7 7.3 %collective-permute-done.16 = f32[208,384]{1,0:T(8,128)S(1)} collective-permute-done((f32[208,384]{1,0:T(8,128)S(1)}, f32[208,384]{1,0:T(8,128)S(1)}, u32[]{:S(2)}, u32[]{:S(2)}) %collective-permute-start.16) | collective-permute-done | bytes 319520 | tf_op jit(solution)/shard_map/ppermute | solution.py:45
  92.0 2.6 %collective-permute-done.17 = f32[208,384]{1,0:T(8,128)S(1)} collective-permute-done((f32[208,384]{1,0:T(8,128)S(1)}, f32[208,384]{1,0:T(8,128)S(1)}, u32[]{:S(2)}, u32[]{:S(2)}) %collective-permute-start.17) | collective-permute-done | bytes 319520 | tf_op jit(solution)/shard_map/ppermute | solution.py:45
  94.7 3.6 %collective-permute-start.18 = (f32[208,384]{1,0:T(8,128)S(1)}, f32[208,384]{1,0:T(8,128)S(1)}, u32[]{:S(2)}, u32[]{:S(2)}) collective-permute-start(f32[208,384]{1,0:T(8,128)S(1)} %add_add_fusion.mine_ref), channel_id=1, source_target_pairs={{0,64},{8,72},{16,80},{24,88},{32,96},{40,104},{48,112},{56,120},{... | collective-permute-start | bytes 958472 | tf_op jit(solution)/shard_map/ppermute | solution.py:45
  98.3 6.6 %collective-permute-done.18.got_ref = f32[208,384]{1,0:T(8,128)S(1)} collective-permute-done((f32[208,384]{1,0:T(8,128)S(1)}, f32[208,384]{1,0:T(8,128)S(1)}, u32[]{:S(2)}, u32[]{:S(2)}) %collective-permute-start.18) | collective-permute-done | bytes 319520 | tf_op jit(solution)/shard_map/ppermute | solution.py:45
  105.2 1.8 %collective-permute-start.21 = (f32[208,384]{1,0:T(8,128)S(1)}, f32[208,384]{1,0:T(8,128)S(1)}, u32[]{:S(2)}, u32[]{:S(2)}) collective-permute-start(f32[208,384]{1,0:T(8,128)S(1)} %shard_map.56), channel_id=1, source_target_pairs={{0,48},{8,56},{16,32},{24,40},{32,16},{40,24},{48,0},{56,8},{64,11... | collective-permute-start | bytes 958472 | tf_op jit(solution)/shard_map/ppermute | solution.py:45
  107.1 2.3 %collective-permute-start.19 = (f32[208,384]{1,0:T(8,128)S(1)}, f32[208,384]{1,0:T(8,128)S(1)}, u32[]{:S(2)}, u32[]{:S(2)}) collective-permute-start(f32[208,384]{1,0:T(8,128)S(1)} %shard_map.56), channel_id=1, source_target_pairs={{0,16},{8,24},{16,0},{24,8},{32,48},{40,56},{48,32},{56,40},{64,80... | collective-permute-start | bytes 958472 | tf_op jit(solution)/shard_map/ppermute | solution.py:45
  109.4 11.7 %collective-permute-done.21 = f32[208,384]{1,0:T(8,128)S(1)} collective-permute-done((f32[208,384]{1,0:T(8,128)S(1)}, f32[208,384]{1,0:T(8,128)S(1)}, u32[]{:S(2)}, u32[]{:S(2)}) %collective-permute-start.21) | collective-permute-done | bytes 319520 | tf_op jit(solution)/shard_map/ppermute | solution.py:45
  121.9 3.0 %collective-permute-done.22.other_ref = f32[4,208,384]{2,1,0:T(8,128)S(1)} collective-permute-done((f32[4,208,384]{2,1,0:T(8,128)S(1)}, f32[4,208,384]{2,1,0:T(8,128)S(1)}, u32[]{:S(2)}, u32[]{:S(2)}) %collective-permute-start.22) | collective-permute-done | bytes 1277984 | tf_op jit(solution)/shard_map/ppermute | solution.py:45
  124.9 6.4 %shard_map.57 = (f32[400,1536]{1,0:T(8,128)}, f32[400,1]{1,0:T(8,128)S(1)}, f32[8,80,256]{2,1,0:T(8,128)S(1)}) custom-call(f32[4,208,384]{2,1,0:T(8,128)S(1)} %pad_maximum_fusion.own_ref, f32[4,208,384]{2,1,0:T(8,128)S(1)} %collective-permute-done.22.other_ref, f32[16,1536]{1,0:T(8,128)S(1)} %get-tuple-element.20.table_ref, s32[1,2048]{1,0:T(1,128)S(1)} %bitcast.20, ...), custom_call_target="tpu_custom_call" | custom-call | tf_op jit(solution)/shard_map/pallas_call | solution.py:409
  131.2 16.5 %all_to_all.5.scores_ref = f32[8,80,256]{2,1,0:T(8,128)S(1)} all-to-all(f32[8,80,256]{2,1,0:T(8,128)S(1)} %get-tuple-element.32), channel_id=1, replica_groups=mesh['samp'=16,'blk'=8] {'blk'}, dimensions={0} | all-to-all | bytes 1310720 | tf_op jit(solution)/shard_map/all_to_all | solution.py:473
  151.3 2.1 %collective-permute-start.24 = (f32[80,128]{1,0:T(8,128)S(1)}, f32[80,128]{1,0:T(8,128)S(1)}, u32[]{:S(2)}, u32[]{:S(2)}) collective-permute-start(f32[80,128]{1,0:T(8,128)S(1)} %add.78), channel_id=1, source_target_pairs={{0,16},{8,24},{16,0},{24,8},{32,48},{40,56},{48,32},{56,40},{64,80... | collective-permute-start | bytes 122888 | tf_op jit(solution)/shard_map/ppermute | solution.py:45
  154.5 2.1 %collective-permute-done.25 = f32[80,128]{1,0:T(8,128)S(1)} collective-permute-done((f32[80,128]{1,0:T(8,128)S(1)}, f32[80,128]{1,0:T(8,128)S(1)}, u32[]{:S(2)}, u32[]{:S(2)}) %collective-permute-start.25) | collective-permute-done | bytes 40992 | tf_op jit(solution)/shard_map/ppermute | solution.py:45
  163.6 2.8 %collective-permute-start.32 = (f32[80,128]{1,0:T(8,128)S(1)}, f32[80,128]{1,0:T(8,128)S(1)}, u32[]{:S(2)}, u32[]{:S(2)}) collective-permute-start(f32[80,128]{1,0:T(8,128)S(1)} %add_add_fusion.4), channel_id=1, source_target_pairs={{0,68},{1,69},{2,70},{3,71},{4,64},{5,65},{6,66},{7,67},{8,76},{9,... | collective-permute-start | bytes 122888 | tf_op jit(solution)/shard_map/ppermute | solution.py:45
  168.9 3.0 %collective-permute-done.31 = f32[80,128]{1,0:T(8,128)S(1)} collective-permute-done((f32[80,128]{1,0:T(8,128)S(1)}, f32[80,128]{1,0:T(8,128)S(1)}, u32[]{:S(2)}, u32[]{:S(2)}) %collective-permute-start.31) | collective-permute-done | bytes 40992 | tf_op jit(solution)/shard_map/ppermute | solution.py:45
  (66 shorter events, 33.0 us)
Async XLA Ops:
  7.1 1.3 collective-permute-start
  8.4 6.1 %collective-permute-start.1 = (f32[8,1536]{1,0:T(8,128)S(1)}, f32[8,1536]{1,0:T(8,128)S(1)}, u32[]{:S(2)}, u32[]{:S(2)}) collective-permute-start(f32[8,1536]{1,0:T(8,128)S(1)} %add.66), channel_id=1, source_target_pairs={{0,64},{8,72},{16,80},{24,88},{32,96},{40,104},{48,112},{56,120},{... | collective-permute-start | bytes 147464 | tf_op jit(solution)/shard_map/ppermute | solution.py:45
  14.5 5.4 %collective-permute-start.4 = (f32[8,1536]{1,0:T(8,128)S(1)}, f32[8,1536]{1,0:T(8,128)S(1)}, u32[]{:S(2)}, u32[]{:S(2)}) collective-permute-start(f32[8,1536]{1,0:T(8,128)S(1)} %add.67), channel_id=1, source_target_pairs={{0,48},{8,56},{16,32},{24,40},{32,16},{40,24},{48,0},{56,8},{64,11... | collective-permute-start | bytes 147464 | tf_op jit(solution)/shard_map/ppermute | solution.py:45
  17.4 5.6 %collective-permute-start.3 = (f32[8,1536]{1,0:T(8,128)S(1)}, f32[8,1536]{1,0:T(8,128)S(1)}, u32[]{:S(2)}, u32[]{:S(2)}) collective-permute-start(f32[8,1536]{1,0:T(8,128)S(1)} %add.67), channel_id=1, source_target_pairs={{0,32},{8,40},{16,48},{24,56},{32,0},{40,8},{48,16},{56,24},{64,96... | collective-permute-start | bytes 147464 | tf_op jit(solution)/shard_map/ppermute | solution.py:45
  18.2 4.8 %collective-permute-start.2 = (f32[8,1536]{1,0:T(8,128)S(1)}, f32[8,1536]{1,0:T(8,128)S(1)}, u32[]{:S(2)}, u32[]{:S(2)}) collective-permute-start(f32[8,1536]{1,0:T(8,128)S(1)} %add.67), channel_id=1, source_target_pairs={{0,16},{8,24},{16,0},{24,8},{32,48},{40,56},{48,32},{56,40},{64,80... | collective-permute-start | bytes 147464 | tf_op jit(solution)/shard_map/ppermute | solution.py:45
  31.5 1.7 %collective-permute-start.5 = (f32[56,1536]{1,0:T(8,128)S(1)}, f32[56,1536]{1,0:T(8,128)S(1)}, u32[]{:S(2)}, u32[]{:S(2)}) collective-permute-start(f32[56,1536]{1,0:T(8,128)S(1)} %get-tuple-element.22), channel_id=1, source_target_pairs={{0,8},{8,0},{16,24},{24,16},{32,40},{40,32},{48,56},{56,48},{64,72... | collective-permute-start | bytes 1032200 | tf_op jit(solution)/shard_map/ppermute | solution.py:45
  33.3 5.4 %collective-permute-start.6 = (f32[56,384]{1,0:T(8,128)S(1)}, f32[56,384]{1,0:T(8,128)S(1)}, u32[]{:S(2)}, u32[]{:S(2)}) collective-permute-start(f32[56,384]{1,0:T(8,128)S(1)} %get-tuple-element.24), channel_id=1, source_target_pairs={{0,16},{8,24},{16,0},{24,8},{32,48},{40,56},{48,32},{56,40},{64,80... | collective-permute-start | bytes 258056 | tf_op jit(solution)/shard_map/ppermute | solution.py:45
  33.6 7.1 %collective-permute-start.7 = (f32[56,384]{1,0:T(8,128)S(1)}, f32[56,384]{1,0:T(8,128)S(1)}, u32[]{:S(2)}, u32[]{:S(2)}) collective-permute-start(f32[56,384]{1,0:T(8,128)S(1)} %get-tuple-element.25), channel_id=1, source_target_pairs={{0,32},{8,40},{16,48},{24,56},{32,0},{40,8},{48,16},{56,24},{64,96... | collective-permute-start | bytes 258056 | tf_op jit(solution)/shard_map/ppermute | solution.py:45
  36.2 6.2 %collective-permute-start.8 = (f32[56,384]{1,0:T(8,128)S(1)}, f32[56,384]{1,0:T(8,128)S(1)}, u32[]{:S(2)}, u32[]{:S(2)}) collective-permute-start(f32[56,384]{1,0:T(8,128)S(1)} %get-tuple-element.26), channel_id=1, source_target_pairs={{0,48},{8,56},{16,32},{24,40},{32,16},{40,24},{48,0},{56,8},{64,11... | collective-permute-start | bytes 258056 | tf_op jit(solution)/shard_map/ppermute | solution.py:45
  42.5 6.1 %collective-permute-start.9 = (f32[56,384]{1,0:T(8,128)S(1)}, f32[56,384]{1,0:T(8,128)S(1)}, u32[]{:S(2)}, u32[]{:S(2)}) collective-permute-start(f32[56,384]{1,0:T(8,128)S(1)} %add_add_fusion.1), channel_id=1, source_target_pairs={{0,64},{8,72},{16,80},{24,88},{32,96},{40,104},{48,112},{56,120},{... | collective-permute-start | bytes 258056 | tf_op jit(solution)/shard_map/ppermute | solution.py:45
  48.5 6.4 %collective-permute-start.12 = (f32[56,384]{1,0:T(8,128)S(1)}, f32[56,384]{1,0:T(8,128)S(1)}, u32[]{:S(2)}, u32[]{:S(2)}) collective-permute-start(f32[56,384]{1,0:T(8,128)S(1)} %add.74.own_ref), channel_id=1, source_target_pairs={{0,48},{8,56},{16,32},{24,40},{32,16},{40,24},{48,0},{56,8},{64,11... | collective-permute-start | bytes 258056 | tf_op jit(solution)/shard_map/ppermute | solution.py:45
  50.5 6.0 %collective-permute-start.11 = (f32[56,384]{1,0:T(8,128)S(1)}, f32[56,384]{1,0:T(8,128)S(1)}, u32[]{:S(2)}, u32[]{:S(2)}) collective-permute-start(f32[56,384]{1,0:T(8,128)S(1)} %add.74.own_ref), channel_id=1, source_target_pairs={{0,32},{8,40},{16,48},{24,56},{32,0},{40,8},{48,16},{56,24},{64,96... | collective-permute-start | bytes 258056 | tf_op jit(solution)/shard_map/ppermute | solution.py:45
  50.9 5.6 %collective-permute-start.10 = (f32[56,384]{1,0:T(8,128)S(1)}, f32[56,384]{1,0:T(8,128)S(1)}, u32[]{:S(2)}, u32[]{:S(2)}) collective-permute-start(f32[56,384]{1,0:T(8,128)S(1)} %add.74.own_ref), channel_id=1, source_target_pairs={{0,16},{8,24},{16,0},{24,8},{32,48},{40,56},{48,32},{56,40},{64,80... | collective-permute-start | bytes 258056 | tf_op jit(solution)/shard_map/ppermute | solution.py:45
  56.5 1.7 %collective-permute-start.13 = (f32[4,56,384]{2,1,0:T(8,128)S(1)}, f32[4,56,384]{2,1,0:T(8,128)S(1)}, u32[]{:S(2)}, u32[]{:S(2)}) collective-permute-start(f32[4,56,384]{2,1,0:T(8,128)S(1)} %pad_maximum_fusion.1.own_ref), channel_id=1, source_target_pairs={{0,8},{8,0},{16,24},{24,16},{32,40},{40,32},{48,56},{56,48},{64,72... | collective-permute-start | bytes 1032200 | tf_op jit(solution)/shard_map/ppermute | solution.py:45
  66.0 8.1 %collective-permute-start.14 = (f32[208,1536]{1,0:T(8,128)S(1)}, f32[208,1536]{1,0:T(8,128)S(1)}, u32[]{:S(2)}, u32[]{:S(2)}) collective-permute-start(f32[208,1536]{1,0:T(8,128)S(1)} %shard_map.54), channel_id=1, source_target_pairs={{0,8},{8,0},{16,24},{24,16},{32,40},{40,32},{48,56},{56,48},{64,72... | collective-permute-start | bytes 3833864 | tf_op jit(solution)/shard_map/ppermute | solution.py:45
  74.3 10.4 %collective-permute-start.15 = (f32[208,384]{1,0:T(8,128)S(1)}, f32[208,384]{1,0:T(8,128)S(1)}, u32[]{:S(2)}, u32[]{:S(2)}) collective-permute-start(f32[208,384]{1,0:T(8,128)S(1)} %get-tuple-element.28), channel_id=1, source_target_pairs={{0,16},{8,24},{16,0},{24,8},{32,48},{40,56},{48,32},{56,40},{64,80... | collective-permute-start | bytes 958472 | tf_op jit(solution)/shard_map/ppermute | solution.py:45
  75.1 16.9 %collective-permute-start.16 = (f32[208,384]{1,0:T(8,128)S(1)}, f32[208,384]{1,0:T(8,128)S(1)}, u32[]{:S(2)}, u32[]{:S(2)}) collective-permute-start(f32[208,384]{1,0:T(8,128)S(1)} %get-tuple-element.29), channel_id=1, source_target_pairs={{0,32},{8,40},{16,48},{24,56},{32,0},{40,8},{48,16},{56,24},{64,96... | collective-permute-start | bytes 958472 | tf_op jit(solution)/shard_map/ppermute | solution.py:45
  77.3 17.3 %collective-permute-start.17 = (f32[208,384]{1,0:T(8,128)S(1)}, f32[208,384]{1,0:T(8,128)S(1)}, u32[]{:S(2)}, u32[]{:S(2)}) collective-permute-start(f32[208,384]{1,0:T(8,128)S(1)} %get-tuple-element.30), channel_id=1, source_target_pairs={{0,48},{8,56},{16,32},{24,40},{32,16},{40,24},{48,0},{56,8},{64,11... | collective-permute-start | bytes 958472 | tf_op jit(solution)/shard_map/ppermute | solution.py:45
  94.7 10.2 %collective-permute-start.18 = (f32[208,384]{1,0:T(8,128)S(1)}, f32[208,384]{1,0:T(8,128)S(1)}, u32[]{:S(2)}, u32[]{:S(2)}) collective-permute-start(f32[208,384]{1,0:T(8,128)S(1)} %add_add_fusion.mine_ref), channel_id=1, source_target_pairs={{0,64},{8,72},{16,80},{24,88},{32,96},{40,104},{48,112},{56,120},{... | collective-permute-start | bytes 958472 | tf_op jit(solution)/shard_map/ppermute | solution.py:45
  105.2 15.9 %collective-permute-start.21 = (f32[208,384]{1,0:T(8,128)S(1)}, f32[208,384]{1,0:T(8,128)S(1)}, u32[]{:S(2)}, u32[]{:S(2)}) collective-permute-start(f32[208,384]{1,0:T(8,128)S(1)} %shard_map.56), channel_id=1, source_target_pairs={{0,48},{8,56},{16,32},{24,40},{32,16},{40,24},{48,0},{56,8},{64,11... | collective-permute-start | bytes 958472 | tf_op jit(solution)/shard_map/ppermute | solution.py:45
  107.1 14.0 %collective-permute-start.20 = (f32[208,384]{1,0:T(8,128)S(1)}, f32[208,384]{1,0:T(8,128)S(1)}, u32[]{:S(2)}, u32[]{:S(2)}) collective-permute-start(f32[208,384]{1,0:T(8,128)S(1)} %shard_map.56), channel_id=1, source_target_pairs={{0,32},{8,40},{16,48},{24,56},{32,0},{40,8},{48,16},{56,24},{64,96... | collective-permute-start | bytes 958472 | tf_op jit(solution)/shard_map/ppermute | solution.py:45
  107.1 14.7 %collective-permute-start.19 = (f32[208,384]{1,0:T(8,128)S(1)}, f32[208,384]{1,0:T(8,128)S(1)}, u32[]{:S(2)}, u32[]{:S(2)}) collective-permute-start(f32[208,384]{1,0:T(8,128)S(1)} %shard_map.56), channel_id=1, source_target_pairs={{0,16},{8,24},{16,0},{24,8},{32,48},{40,56},{48,32},{56,40},{64,80... | collective-permute-start | bytes 958472 | tf_op jit(solution)/shard_map/ppermute | solution.py:45
  121.8 3.1 %collective-permute-start.22 = (f32[4,208,384]{2,1,0:T(8,128)S(1)}, f32[4,208,384]{2,1,0:T(8,128)S(1)}, u32[]{:S(2)}, u32[]{:S(2)}) collective-permute-start(f32[4,208,384]{2,1,0:T(8,128)S(1)} %pad_maximum_fusion.own_ref), channel_id=1, source_target_pairs={{0,8},{8,0},{16,24},{24,16},{32,40},{40,32},{48,56},{56,48},{64,72... | collective-permute-start | bytes 3833864 | tf_op jit(solution)/shard_map/ppermute | solution.py:45
  149.3 5.2 %collective-permute-start.26 = (f32[80,128]{1,0:T(8,128)S(1)}, f32[80,128]{1,0:T(8,128)S(1)}, u32[]{:S(2)}, u32[]{:S(2)}) collective-permute-start(f32[80,128]{1,0:T(8,128)S(1)} %add.78), channel_id=1, source_target_pairs={{0,48},{8,56},{16,32},{24,40},{32,16},{40,24},{48,0},{56,8},{64,11... | collective-permute-start | bytes 122888 | tf_op jit(solution)/shard_map/ppermute | solution.py:45
  151.0 5.5 %collective-permute-start.25 = (f32[80,128]{1,0:T(8,128)S(1)}, f32[80,128]{1,0:T(8,128)S(1)}, u32[]{:S(2)}, u32[]{:S(2)}) collective-permute-start(f32[80,128]{1,0:T(8,128)S(1)} %add.78), channel_id=1, source_target_pairs={{0,32},{8,40},{16,48},{24,56},{32,0},{40,8},{48,16},{56,24},{64,96... | collective-permute-start | bytes 122888 | tf_op jit(solution)/shard_map/ppermute | solution.py:45
  151.3 5.2 %collective-permute-start.24 = (f32[80,128]{1,0:T(8,128)S(1)}, f32[80,128]{1,0:T(8,128)S(1)}, u32[]{:S(2)}, u32[]{:S(2)}) collective-permute-start(f32[80,128]{1,0:T(8,128)S(1)} %add.78), channel_id=1, source_target_pairs={{0,16},{8,24},{16,0},{24,8},{32,48},{40,56},{48,32},{56,40},{64,80... | collective-permute-start | bytes 122888 | tf_op jit(solution)/shard_map/ppermute | solution.py:45
  156.6 5.3 %collective-permute-start.29 = (f32[80,128]{1,0:T(8,128)S(1)}, f32[80,128]{1,0:T(8,128)S(1)}, u32[]{:S(2)}, u32[]{:S(2)}) collective-permute-start(f32[80,128]{1,0:T(8,128)S(1)} %add_add_fusion.5), channel_id=1, source_target_pairs={{0,3},{1,2},{2,1},{3,0},{4,7},{5,6},{6,5},{7,4},{8,11},{9,10},{10,... | collective-permute-start | bytes 122888 | tf_op jit(solution)/shard_map/ppermute | solution.py:45
  157.9 5.5 %collective-permute-start.28 = (f32[80,128]{1,0:T(8,128)S(1)}, f32[80,128]{1,0:T(8,128)S(1)}, u32[]{:S(2)}, u32[]{:S(2)}) collective-permute-start(f32[80,128]{1,0:T(8,128)S(1)} %add_add_fusion.5), channel_id=1, source_target_pairs={{0,2},{1,3},{2,0},{3,1},{4,6},{5,7},{6,4},{7,5},{8,10},{9,11},{10,... | collective-permute-start | bytes 122888 | tf_op jit(solution)/shard_map/ppermute | solution.py:45
  159.6 4.0 %collective-permute-start.27 = (f32[80,128]{1,0:T(8,128)S(1)}, f32[80,128]{1,0:T(8,128)S(1)}, u32[]{:S(2)}, u32[]{:S(2)}) collective-permute-start(f32[80,128]{1,0:T(8,128)S(1)} %add_add_fusion.5), channel_id=1, source_target_pairs={{0,1},{1,0},{2,3},{3,2},{4,5},{5,4},{6,7},{7,6},{8,9},{9,8},{10,11... | collective-permute-start | bytes 122888 | tf_op jit(solution)/shard_map/ppermute | solution.py:45
  163.6 5.3 %collective-permute-start.32 = (f32[80,128]{1,0:T(8,128)S(1)}, f32[80,128]{1,0:T(8,128)S(1)}, u32[]{:S(2)}, u32[]{:S(2)}) collective-permute-start(f32[80,128]{1,0:T(8,128)S(1)} %add_add_fusion.4), channel_id=1, source_target_pairs={{0,68},{1,69},{2,70},{3,71},{4,64},{5,65},{6,66},{7,67},{8,76},{9,... | collective-permute-start | bytes 122888 | tf_op jit(solution)/shard_map/ppermute | solution.py:45
  166.4 5.5 %collective-permute-start.31 = (f32[80,128]{1,0:T(8,128)S(1)}, f32[80,128]{1,0:T(8,128)S(1)}, u32[]{:S(2)}, u32[]{:S(2)}) collective-permute-start(f32[80,128]{1,0:T(8,128)S(1)} %add_add_fusion.4), channel_id=1, source_target_pairs={{0,64},{1,65},{2,66},{3,67},{4,68},{5,69},{6,70},{7,71},{8,72},{9,... | collective-permute-start | bytes 122888 | tf_op jit(solution)/shard_map/ppermute | solution.py:45
  167.3 4.6 %collective-permute-start.30 = (f32[80,128]{1,0:T(8,128)S(1)}, f32[80,128]{1,0:T(8,128)S(1)}, u32[]{:S(2)}, u32[]{:S(2)}) collective-permute-start(f32[80,128]{1,0:T(8,128)S(1)} %add_add_fusion.4), channel_id=1, source_target_pairs={{0,4},{1,5},{2,6},{3,7},{4,0},{5,1},{6,2},{7,3},{8,12},{9,13},{10,... | collective-permute-start | bytes 122888 | tf_op jit(solution)/shard_map/ppermute | solution.py:45
  (3 other events, 2.7 us)

commit v5 on v4

--- a/solution.py
+++ b/solution.py
@@ -18,7 +18,6 @@
 ROWS1 = 104
 PEOPLE = 32768
 SNPS = 12288
-VMEM = 36 * 1024 * 1024
 TILE = 512
 
 step_size = 0.6
@@ -101,8 +100,8 @@
     return [pl.BlockSpec(memory_space=pltpu.VMEM)] * count
 
 
-def params():
-    return pltpu.CompilerParams(vmem_limit_bytes=VMEM)
+def params(mebibytes=20):
+    return pltpu.CompilerParams(vmem_limit_bytes=mebibytes * 1024 * 1024)
 
 
 def parts3(values):
@@ -168,7 +167,7 @@
             pltpu.VMEM((32, width), jnp.float32),
             pltpu.SemaphoreType.DMA((parts,)),
         ],
-        compiler_params=params(),
+        compiler_params=params(36),
     )(phenotype.reshape(1, people), fold_ids.reshape(1, people), genotypes)
 
 
@@ -256,63 +255,87 @@
     )(stats, dose)
 
 
+def gram_kernel(dose_ref, *out_refs, mine):
+    core, place = here()
+    side = core if mine else 1 - core
+    rows, width = out_refs[0].shape
+    step = 256
+    for block in range(rows // step):
+        left = dose_ref[:, pl.ds(pl.multiple_of(side * rows + block * step, 128), step)].T
+        for k, out_ref in enumerate(out_refs):
+            right = dose_ref[:, lanes_of(place, k, width)]
+            out_ref[block * step : (block + 1) * step] = matmul(left, right, NN)
+
+
+def gram_parts(dose, mine):
+    people, width = dose.shape
+    part = jax.ShapeDtypeStruct((width // 2, width // 4), jnp.float32)
+    return pl.pallas_call(
+        functools.partial(gram_kernel, mine=mine),
+        in_specs=whole(1),
+        out_specs=whole(4),
+        out_shape=[part] * 4,
+        compiler_params=params(16),
+        cost_estimate=pl.CostEstimate(
+            flops=people * width * width, bytes_accessed=2 * people * width, transcendentals=0
+        ),
+    )(dose)
+
+
 def second_kernel(
-    table_ref, own_ref, other_ref, dose_ref, out_ref, product_ref, coeff_ref, both_ref, *, mine
+    table_ref, own_ref, other_ref, g0_ref, g1_ref, g2_ref, g3_ref,
+    kept_ref, sent_ref, product_ref, coeff_ref, both_ref, gram_ref,
 ):
-    rows = 2 * ROWS1
-    half = ROWS0 // 2
-    table = table_ref[...]
+    core, place = here()
+    half, width = own_ref.shape[1:]
+    rows = coeff_ref.shape[0]
+    for part in range(2):
+        k = place ^ (2 * core + part)
+        lanes = slice(part * width, (part + 1) * width)
+        own, other = own_ref[k], other_ref[k]
+        product_ref[0:half, lanes] = jnp.where(core == 0, own, other)
+        product_ref[half:, lanes] = jnp.where(core == 0, other, own)
+    table = table_ref[:, pl.ds(pl.multiple_of(core * 2 * width, 128), 2 * width)]
     row, fold_of, cutoff = base_rows(ROWS1)
     target = spread(table[:FOLDS], fold_of)
     coeff = soft_threshold(step_size * target, cutoff)
-    core, place = here()
-    for k in range(4):
-        lanes = lanes_of(place, k, own_ref.shape[2])
-        product_ref[0:half, lanes] = jnp.where(core == 0, own_ref[k], other_ref[k])
-        product_ref[half:, lanes] = jnp.where(core == 0, other_ref[k], own_ref[k])
     product = product_ref[0:ROWS1] * (table[7:8] / PEOPLE)
-    side = core if mine else 1 - core
-    for group in range(2):
-        shrink = shrink_unit * (2 * side + group + 1).astype(jnp.float32)
-        new = next_coeff(coeff, product, target, shrink, cutoff)
+    for group in range(SHRINKS):
+        new = next_coeff(coeff, product, target, shrink_unit * (group + 1), cutoff)
         coeff_ref[group * ROWS1 : (group + 1) * ROWS1] = jnp.where(row < BASE, new, 0.0)
-    scaled = coeff_ref[...] * table[7:8]
-    offset = jnp.sum(scaled * table[5:6], axis=1, keepdims=True)
-    high, low = split2(scaled)
+    high, low = split2(coeff_ref[...] * table[7:8])
     both_ref[0:rows] = high
     both_ref[rows:] = low
-    out_ref[...] = jnp.zeros_like(out_ref)
-
-    def body(step, carry):
-        dose = dose_ref[pl.ds(pl.multiple_of(step * TILE, TILE), TILE)]
-        scores = matmul(both_ref[...], dose, NT)
-        scores = scores[:rows] + scores[rows:] - carry
-        pair = jnp.concatenate(split2(scores), axis=0)
-        sums = matmul(pair, dose, NN)
-        out_ref[...] += sums[:rows] + sums[rows:]
-        return carry
-
-    lax.fori_loop(0, dose_ref.shape[0] // TILE, body, offset)
-
-
-def second_product(table, own, other, dose, mine):
-    people, width = dose.shape
-    rows = 2 * ROWS1
-    return pl.pallas_call(
-        functools.partial(second_kernel, mine=mine),
-        in_specs=whole(4),
-        out_specs=pl.BlockSpec(memory_space=pltpu.VMEM),
-        out_shape=jax.ShapeDtypeStruct((rows, width), jnp.float32),
+    scaled = high.astype(jnp.float32) + low.astype(jnp.float32)
+    offset = jnp.sum(scaled * table[5:6], axis=1, keepdims=True)
+    gram = (g0_ref[...] + g1_ref[...]) + (g2_ref[...] + g3_ref[...])
+    high, low = split2(gram)
+    gram_ref[:, :width] = high
+    gram_ref[:, width:] = low
+    sums = matmul(both_ref[...], gram_ref[...], NN)
+    sums = sums[:rows] + sums[rows:]
+    mean = table_ref[5:6, lanes_of(place, 0, width)]
+    sums = sums[:, :width] + sums[:, width:] - (0.5 * PEOPLE) * offset * mean
+    kept_ref[...] = jnp.where(core == 0, sums[: rows // 2], sums[rows // 2 :])
+    sent_ref[...] = jnp.where(core == 0, sums[rows // 2 :], sums[: rows // 2])
+
+
+def second_product(table, own, other, panels):
+    depth, width = panels[0].shape
+    half = jax.ShapeDtypeStruct((2 * ROWS1, width), jnp.float32)
+    return pl.pallas_call(
+        second_kernel,
+        in_specs=whole(7),
+        out_specs=whole(2),
+        out_shape=[half, half],
         scratch_shapes=[
-            pltpu.VMEM((ROWS0, width), jnp.float32),
-            pltpu.VMEM((rows, width), jnp.float32),
-            pltpu.VMEM((2 * rows, width), jnp.bfloat16),
+            pltpu.VMEM((ROWS0, depth), jnp.float32),
+            pltpu.VMEM((4 * ROWS1, depth), jnp.float32),
+            pltpu.VMEM((8 * ROWS1, depth), jnp.bfloat16),
+            pltpu.VMEM((depth, 2 * width), jnp.bfloat16),
         ],
-        compiler_params=params(),
-        cost_estimate=pl.CostEstimate(
-            flops=8 * people * width * rows, bytes_accessed=2 * people * width, transcendentals=0
-        ),
-    )(table, own, other, dose)
+        compiler_params=params(28),
+    )(table, own, other, *panels)
 
 
 def finish_kernel(table_ref, own_ref, other_ref, mine_ref, got_ref, out_ref):
@@ -421,7 +444,7 @@
             pltpu.VMEM((GRID, width), jnp.bfloat16),
             pltpu.VMEM((GRID, 1), jnp.float32),
         ],
-        compiler_params=params(),
+        compiler_params=params(28),
     )(own, other, table, fold_ids.reshape(1, people), dose)
 
 
@@ -457,14 +480,16 @@
     dose, stats = prepare(genotypes, phenotype, fold_ids)
     stats = all_sum(stats, SAMP_BITS)
 
+    got = [swap(part, "samp", 1) for part in gram_parts(dose, False)]
+    parts = [a + b for a, b in zip(gram_parts(dose, True), got)]
+    panels = [parts[0]] + [swap(parts[k], "samp", 2 * k) for k in (1, 2, 3)]
+
     kept, sent, table = first_product(stats, dose)
     piece = scatter_chips(kept, swap(sent, "samp", 1))
     own_product, other_product = gather_chips(piece + swap(piece, "samp", 8))
 
-    sent = second_product(table, own_product, other_product, dose, False)
-    sent = swap(sent, "samp", 1)
-    kept = second_product(table, own_product, other_product, dose, True)
-    piece = scatter_chips(kept, sent)
+    kept, sent = second_product(table, own_product, other_product, panels)
+    piece = kept + swap(sent, "samp", 1)
     piece = finish(table, own_product[0], other_product[0], piece, swap(piece, "samp", 8))
     own, other = gather_chips(piece)
 

time: 173 us -> 217 us (1.25)
  waiting for transfers between devices: 70.1 us -> 114 us
    ppermute x33 -> x37, waiting for transfers between devices: 70.1 us -> 114 us  [swap(): return lax.ppermute(values, axis, [(i, i ^ bit) for i in range(size)])]
    ppermute x33 -> x37, starting transfers between devices: 46.6 us -> 46.7 us  [swap(): return lax.ppermute(values, axis, [(i, i ^ bit) for i in range(size)])]
    pallas_call x2 -> x3, Pallas kernels: 15.5 us -> 15.5 us  [the longest x2 13.6 us: gram_parts(): pl.pallas_call(functools.partial(gram_kernel, mine=mine), in_specs=whole(...]
  transfers between devices with their start and end apart: 33 -> 37, of which waited for: 27 -> 21; matrix products, arithmetic and copies ran while one was open for 0% -> 0% of each run, Pallas kernels for 4% -> 10%
where the time goes in v5:
time: 217 us
  waiting for transfers between devices  114 us (53%)
  starting transfers between devices  46.7 us (22%)
  Pallas kernels  36 us (17%)
  blocking collectives  16.5 us (8%)
    ppermute x37, waiting for transfers between devices, swap(): return lax.ppermute(values, axis, [(i, i ^ bit) for i in range(size)])  114 us
    ppermute x37, starting transfers between devices, swap(): return lax.ppermute(values, axis, [(i, i ^ bit) for i in range(size)])  46.7 us
    all_to_all x1, blocking collectives, local(): scores = lax.all_to_all(scores, 'blk', 0, 0, tiled=True)  16.5 us
    pallas_call x2, Pallas kernels, gram_parts(): pl.pallas_call(functools.partial(gram_kernel, mine=mine), in_specs=whole(...  13.6 us
    pallas_call x1, Pallas kernels, first_product(): pl.pallas_call(first_kernel, in_specs=whole(2), out_specs=whole(3), out_s...  8.52 us
    pallas_call x1, Pallas kernels, predict(): pl.pallas_call(predict_kernel, in_specs=whole(5), out_specs=whole(3), out...  6.36 us
    pallas_call x1, Pallas kernels, prepare(): pl.pallas_call(prepare_kernel, in_specs=whole(2) + [pl.BlockSpec(memory_s...  5.06 us
  transfers between devices with their start and end apart: 37, of which 21 were waited for; matrix products, arithmetic and copies ran while one was open for 0% of the time, Pallas kernels for 10%

profile of v5, /device:TPU:0, one launch (start us, length us, event | category | flops | bytes accessed | tf_op | source)
XLA Modules:
  0.0 217.2 jit_solution(2116239401517666837)
XLA Ops:
  2.0 5.1 %shard_map.50 = (bf16[2048,1536]{1,0:T(8,128)(2,1)S(1)}, f32[8,1536]{1,0:T(8,128)S(1)}) custom-call(f32[1,2048]{1,0:T(1,128)S(1)} %bitcast.22, s32[1,2048]{1,0:T(1,128)S(1)} %bitcast.19, s32[2048,1536]{1,0:T(8,128)} %geno_ref.1), custom_call_target="tpu_custom_call" | custom-call | tf_op jit(solution)/shard_map/pallas_call | solution.py:156
  8.4 4.0 %collective-permute-start.1 = (f32[8,1536]{1,0:T(8,128)S(1)}, f32[8,1536]{1,0:T(8,128)S(1)}, u32[]{:S(2)}, u32[]{:S(2)}) collective-permute-start(f32[8,1536]{1,0:T(8,128)S(1)} %add.72), channel_id=1, source_target_pairs={{0,64},{8,72},{16,80},{24,88},{32,96},{40,104},{48,112},{56,120},{... | collective-permute-start | bytes 147464 | tf_op jit(solution)/shard_map/ppermute | solution.py:44
  12.4 2.1 collective-permute-done.1
  16.1 2.7 %collective-permute-start.3 = (f32[8,1536]{1,0:T(8,128)S(1)}, f32[8,1536]{1,0:T(8,128)S(1)}, u32[]{:S(2)}, u32[]{:S(2)}) collective-permute-start(f32[8,1536]{1,0:T(8,128)S(1)} %add.73), channel_id=1, source_target_pairs={{0,32},{8,40},{16,48},{24,56},{32,0},{40,8},{48,16},{56,24},{64,96... | collective-permute-start | bytes 147464 | tf_op jit(solution)/shard_map/ppermute | solution.py:44
  19.3 6.8 %shard_map.54 = (f32[768,384]{1,0:T(8,128)S(1)}, f32[768,384]{1,0:T(8,128)S(1)}, f32[768,384]{1,0:T(8,128)S(1)}, f32[768,384]{1,0:T(8,128)S(1)}) custom-call(bf16[2048,1536]{1,0:T(8,128)(2,1)S(1)} %get-tuple-element.25.dose_ref), custom_call_target="tpu_custom_call" | custom-call | flops 4831838208 | bytes 6291456 | tf_op jit(solution)/shard_map/pallas_call | solution.py:273
  26.8 8.5 %shard_map.51 = (f32[56,1536]{1,0:T(8,128)S(1)}, f32[56,1536]{1,0:T(8,128)S(1)}, f32[16,1536]{1,0:T(8,128)S(1)}) custom-call(f32[8,1536]{1,0:T(8,128)S(1)} %add_add_fusion.1.stats_ref, bf16[2048,1536]{1,0:T(8,128)(2,1)S(1)} %get-tuple-element.25.dose_ref), custom_call_target="tpu_custom_call" | custom-call | tf_op jit(solution)/shard_map/pallas_call | solution.py:248
  37.5 3.9 %collective-permute-start.7 = (f32[56,384]{1,0:T(8,128)S(1)}, f32[56,384]{1,0:T(8,128)S(1)}, u32[]{:S(2)}, u32[]{:S(2)}) collective-permute-start(f32[56,384]{1,0:T(8,128)S(1)} %get-tuple-element.31), channel_id=1, source_target_pairs={{0,32},{8,40},{16,48},{24,56},{32,0},{40,8},{48,16},{56,24},{64,96... | collective-permute-start | bytes 258056 | tf_op jit(solution)/shard_map/ppermute | solution.py:44
  41.5 6.8 %shard_map.53 = (f32[768,384]{1,0:T(8,128)S(1)}, f32[768,384]{1,0:T(8,128)S(1)}, f32[768,384]{1,0:T(8,128)S(1)}, f32[768,384]{1,0:T(8,128)S(1)}) custom-call(bf16[2048,1536]{1,0:T(8,128)(2,1)S(1)} %get-tuple-element.25.dose_ref), custom_call_target="tpu_custom_call" | custom-call | flops 4831838208 | bytes 6291456 | tf_op jit(solution)/shard_map/pallas_call | solution.py:273
  48.9 2.3 %collective-permute-start.20 = (f32[768,384]{1,0:T(8,128)S(1)}, f32[768,384]{1,0:T(8,128)S(1)}, u32[]{:S(2)}, u32[]{:S(2)}) collective-permute-start(f32[768,384]{1,0:T(8,128)S(1)} %add.84), channel_id=1, source_target_pairs={{0,48},{8,56},{16,32},{24,40},{32,16},{40,24},{48,0},{56,8},{64,11... | collective-permute-start | bytes 3538952 | tf_op jit(solution)/shard_map/ppermute | solution.py:44
  53.2 52.4 %collective-permute-done.8 = f32[56,384]{1,0:T(8,128)S(1)} collective-permute-done((f32[56,384]{1,0:T(8,128)S(1)}, f32[56,384]{1,0:T(8,128)S(1)}, u32[]{:S(2)}, u32[]{:S(2)}) %collective-permute-start.8) | collective-permute-done | bytes 86048 | tf_op jit(solution)/shard_map/ppermute | solution.py:44
  105.6 3.6 %collective-permute-start.9 = (f32[56,384]{1,0:T(8,128)S(1)}, f32[56,384]{1,0:T(8,128)S(1)}, u32[]{:S(2)}, u32[]{:S(2)}) collective-permute-start(f32[56,384]{1,0:T(8,128)S(1)} %add_add_fusion), channel_id=1, source_target_pairs={{0,64},{8,72},{16,80},{24,88},{32,96},{40,104},{48,112},{56,120},{... | collective-permute-start | bytes 258056 | tf_op jit(solution)/shard_map/ppermute | solution.py:44
  109.2 2.7 %collective-permute-done.9 = f32[56,384]{1,0:T(8,128)S(1)} collective-permute-done((f32[56,384]{1,0:T(8,128)S(1)}, f32[56,384]{1,0:T(8,128)S(1)}, u32[]{:S(2)}, u32[]{:S(2)}) %collective-permute-start.9) | collective-permute-done | bytes 86048 | tf_op jit(solution)/shard_map/ppermute | solution.py:44
  112.0 4.5 %collective-permute-done.10 = f32[56,384]{1,0:T(8,128)S(1)} collective-permute-done((f32[56,384]{1,0:T(8,128)S(1)}, f32[56,384]{1,0:T(8,128)S(1)}, u32[]{:S(2)}, u32[]{:S(2)}) %collective-permute-start.10) | collective-permute-done | bytes 86048 | tf_op jit(solution)/shard_map/ppermute | solution.py:44
  116.9 5.6 %collective-permute-done.11 = f32[56,384]{1,0:T(8,128)S(1)} collective-permute-done((f32[56,384]{1,0:T(8,128)S(1)}, f32[56,384]{1,0:T(8,128)S(1)}, u32[]{:S(2)}, u32[]{:S(2)}) %collective-permute-start.11) | collective-permute-done | bytes 86048 | tf_op jit(solution)/shard_map/ppermute | solution.py:44
  123.0 5.2 %collective-permute-done.12 = f32[56,384]{1,0:T(8,128)S(1)} collective-permute-done((f32[56,384]{1,0:T(8,128)S(1)}, f32[56,384]{1,0:T(8,128)S(1)}, u32[]{:S(2)}, u32[]{:S(2)}) %collective-permute-start.12) | collective-permute-done | bytes 86048 | tf_op jit(solution)/shard_map/ppermute | solution.py:44
  130.0 1.9 shard_map.55
  133.6 3.8 %collective-permute-start.22 = (f32[208,384]{1,0:T(8,128)S(1)}, f32[208,384]{1,0:T(8,128)S(1)}, u32[]{:S(2)}, u32[]{:S(2)}) collective-permute-start(f32[208,384]{1,0:T(8,128)S(1)} %add.85.mine_ref), channel_id=1, source_target_pairs={{0,64},{8,72},{16,80},{24,88},{32,96},{40,104},{48,112},{56,120},{... | collective-permute-start | bytes 958472 | tf_op jit(solution)/shard_map/ppermute | solution.py:44
  137.4 7.8 %collective-permute-done.22.got_ref = f32[208,384]{1,0:T(8,128)S(1)} collective-permute-done((f32[208,384]{1,0:T(8,128)S(1)}, f32[208,384]{1,0:T(8,128)S(1)}, u32[]{:S(2)}, u32[]{:S(2)}) %collective-permute-start.22) | collective-permute-done | bytes 319520 | tf_op jit(solution)/shard_map/ppermute | solution.py:44
  145.7 4.6 %collective-permute-start.24 = (f32[208,384]{1,0:T(8,128)S(1)}, f32[208,384]{1,0:T(8,128)S(1)}, u32[]{:S(2)}, u32[]{:S(2)}) collective-permute-start(f32[208,384]{1,0:T(8,128)S(1)} %shard_map.56), channel_id=1, source_target_pairs={{0,32},{8,40},{16,48},{24,56},{32,0},{40,8},{48,16},{56,24},{64,96... | collective-permute-start | bytes 958472 | tf_op jit(solution)/shard_map/ppermute | solution.py:44
  150.3 6.1 %collective-permute-done.25 = f32[208,384]{1,0:T(8,128)S(1)} collective-permute-done((f32[208,384]{1,0:T(8,128)S(1)}, f32[208,384]{1,0:T(8,128)S(1)}, u32[]{:S(2)}, u32[]{:S(2)}) %collective-permute-start.25) | collective-permute-done | bytes 319520 | tf_op jit(solution)/shard_map/ppermute | solution.py:44
  156.4 7.5 %collective-permute-done.24 = f32[208,384]{1,0:T(8,128)S(1)} collective-permute-done((f32[208,384]{1,0:T(8,128)S(1)}, f32[208,384]{1,0:T(8,128)S(1)}, u32[]{:S(2)}, u32[]{:S(2)}) %collective-permute-start.24) | collective-permute-done | bytes 319520 | tf_op jit(solution)/shard_map/ppermute | solution.py:44
  164.1 3.0 %collective-permute-done.26.other_ref = f32[4,208,384]{2,1,0:T(8,128)S(1)} collective-permute-done((f32[4,208,384]{2,1,0:T(8,128)S(1)}, f32[4,208,384]{2,1,0:T(8,128)S(1)}, u32[]{:S(2)}, u32[]{:S(2)}) %collective-permute-start.26) | collective-permute-done | bytes 1277984 | tf_op jit(solution)/shard_map/ppermute | solution.py:44
  167.1 6.4 %shard_map.57 = (f32[400,1536]{1,0:T(8,128)}, f32[400,1]{1,0:T(8,128)S(1)}, f32[8,80,256]{2,1,0:T(8,128)S(1)}) custom-call(f32[4,208,384]{2,1,0:T(8,128)S(1)} %pad_maximum_fusion.own_ref, f32[4,208,384]{2,1,0:T(8,128)S(1)} %collective-permute-done.26.other_ref, f32[16,1536]{1,0:T(8,128)S(1)} %get-tuple-element.26.table_ref, s32[1,2048]{1,0:T(1,128)S(1)} %bitcast.20, ...), custom_call_target="tpu_custom_call" | custom-call | tf_op jit(solution)/shard_map/pallas_call | solution.py:432
  173.4 16.5 %all_to_all.5.scores_ref = f32[8,80,256]{2,1,0:T(8,128)S(1)} all-to-all(f32[8,80,256]{2,1,0:T(8,128)S(1)} %get-tuple-element.44), channel_id=1, replica_groups=mesh['samp'=16,'blk'=8] {'blk'}, dimensions={0} | all-to-all | bytes 1310720 | tf_op jit(solution)/shard_map/all_to_all | solution.py:498
  191.4 1.8 collective-permute-start.29
  193.3 2.9 %collective-permute-start.30 = (f32[80,128]{1,0:T(8,128)S(1)}, f32[80,128]{1,0:T(8,128)S(1)}, u32[]{:S(2)}, u32[]{:S(2)}) collective-permute-start(f32[80,128]{1,0:T(8,128)S(1)} %add.86), channel_id=1, source_target_pairs={{0,48},{8,56},{16,32},{24,40},{32,16},{40,24},{48,0},{56,8},{64,11... | collective-permute-start | bytes 122888 | tf_op jit(solution)/shard_map/ppermute | solution.py:44
  199.4 1.9 collective-permute-start.32
  201.3 2.0 collective-permute-start.33
  203.3 1.7 collective-permute-done.32
  207.4 3.6 %collective-permute-start.35 = (f32[80,128]{1,0:T(8,128)S(1)}, f32[80,128]{1,0:T(8,128)S(1)}, u32[]{:S(2)}, u32[]{:S(2)}) collective-permute-start(f32[80,128]{1,0:T(8,128)S(1)} %add_add_fusion.3), channel_id=1, source_target_pairs={{0,64},{1,65},{2,66},{3,67},{4,68},{5,69},{6,70},{7,71},{8,72},{9,... | collective-permute-start | bytes 122888 | tf_op jit(solution)/shard_map/ppermute | solution.py:44
  211.3 2.0 collective-permute-done.35
  213.4 2.8 %collective-permute-done.36 = f32[80,128]{1,0:T(8,128)S(1)} collective-permute-done((f32[80,128]{1,0:T(8,128)S(1)}, f32[80,128]{1,0:T(8,128)S(1)}, u32[]{:S(2)}, u32[]{:S(2)}) %collective-permute-start.36) | collective-permute-done | bytes 40992 | tf_op jit(solution)/shard_map/ppermute | solution.py:44
  (78 shorter events, 24.0 us)
Async XLA Ops:
  8.4 6.1 %collective-permute-start.1 = (f32[8,1536]{1,0:T(8,128)S(1)}, f32[8,1536]{1,0:T(8,128)S(1)}, u32[]{:S(2)}, u32[]{:S(2)}) collective-permute-start(f32[8,1536]{1,0:T(8,128)S(1)} %add.72), channel_id=1, source_target_pairs={{0,64},{8,72},{16,80},{24,88},{32,96},{40,104},{48,112},{56,120},{... | collective-permute-start | bytes 147464 | tf_op jit(solution)/shard_map/ppermute | solution.py:44
  14.5 12.2 %collective-permute-start.2 = (f32[8,1536]{1,0:T(8,128)S(1)}, f32[8,1536]{1,0:T(8,128)S(1)}, u32[]{:S(2)}, u32[]{:S(2)}) collective-permute-start(f32[8,1536]{1,0:T(8,128)S(1)} %add.73), channel_id=1, source_target_pairs={{0,16},{8,24},{16,0},{24,8},{32,48},{40,56},{48,32},{56,40},{64,80... | collective-permute-start | bytes 147464 | tf_op jit(solution)/shard_map/ppermute | solution.py:44
  16.1 10.7 %collective-permute-start.3 = (f32[8,1536]{1,0:T(8,128)S(1)}, f32[8,1536]{1,0:T(8,128)S(1)}, u32[]{:S(2)}, u32[]{:S(2)}) collective-permute-start(f32[8,1536]{1,0:T(8,128)S(1)} %add.73), channel_id=1, source_target_pairs={{0,32},{8,40},{16,48},{24,56},{32,0},{40,8},{48,16},{56,24},{64,96... | collective-permute-start | bytes 147464 | tf_op jit(solution)/shard_map/ppermute | solution.py:44
  18.8 8.0 %collective-permute-start.4 = (f32[8,1536]{1,0:T(8,128)S(1)}, f32[8,1536]{1,0:T(8,128)S(1)}, u32[]{:S(2)}, u32[]{:S(2)}) collective-permute-start(f32[8,1536]{1,0:T(8,128)S(1)} %add.73), channel_id=1, source_target_pairs={{0,48},{8,56},{16,32},{24,40},{32,16},{40,24},{48,0},{56,8},{64,11... | collective-permute-start | bytes 147464 | tf_op jit(solution)/shard_map/ppermute | solution.py:44
  26.1 22.2 %collective-permute-start.17 = (f32[768,384]{1,0:T(8,128)S(1)}, f32[768,384]{1,0:T(8,128)S(1)}, u32[]{:S(2)}, u32[]{:S(2)}) collective-permute-start(f32[768,384]{1,0:T(8,128)S(1)} %get-tuple-element.38), channel_id=1, source_target_pairs={{0,8},{8,0},{16,24},{24,16},{32,40},{40,32},{48,56},{56,48},{64,72... | collective-permute-start | bytes 3538952 | tf_op jit(solution)/shard_map/ppermute | solution.py:44
  26.2 22.3 %collective-permute-start.19 = (f32[768,384]{1,0:T(8,128)S(1)}, f32[768,384]{1,0:T(8,128)S(1)}, u32[]{:S(2)}, u32[]{:S(2)}) collective-permute-start(f32[768,384]{1,0:T(8,128)S(1)} %get-tuple-element.40), channel_id=1, source_target_pairs={{0,8},{8,0},{16,24},{24,16},{32,40},{40,32},{48,56},{56,48},{64,72... | collective-permute-start | bytes 3538952 | tf_op jit(solution)/shard_map/ppermute | solution.py:44
  26.7 22.1 %collective-permute-start.15 = (f32[768,384]{1,0:T(8,128)S(1)}, f32[768,384]{1,0:T(8,128)S(1)}, u32[]{:S(2)}, u32[]{:S(2)}) collective-permute-start(f32[768,384]{1,0:T(8,128)S(1)} %get-tuple-element.36), channel_id=1, source_target_pairs={{0,8},{8,0},{16,24},{24,16},{32,40},{40,32},{48,56},{56,48},{64,72... | collective-permute-start | bytes 3538952 | tf_op jit(solution)/shard_map/ppermute | solution.py:44
  37.2 14.1 %collective-permute-start.6 = (f32[56,384]{1,0:T(8,128)S(1)}, f32[56,384]{1,0:T(8,128)S(1)}, u32[]{:S(2)}, u32[]{:S(2)}) collective-permute-start(f32[56,384]{1,0:T(8,128)S(1)} %get-tuple-element.30), channel_id=1, source_target_pairs={{0,16},{8,24},{16,0},{24,8},{32,48},{40,56},{48,32},{56,40},{64,80... | collective-permute-start | bytes 258056 | tf_op jit(solution)/shard_map/ppermute | solution.py:44
  37.5 15.1 %collective-permute-start.7 = (f32[56,384]{1,0:T(8,128)S(1)}, f32[56,384]{1,0:T(8,128)S(1)}, u32[]{:S(2)}, u32[]{:S(2)}) collective-permute-start(f32[56,384]{1,0:T(8,128)S(1)} %get-tuple-element.31), channel_id=1, source_target_pairs={{0,32},{8,40},{16,48},{24,56},{32,0},{40,8},{48,16},{56,24},{64,96... | collective-permute-start | bytes 258056 | tf_op jit(solution)/shard_map/ppermute | solution.py:44
  48.3 80.0 %collective-permute-start.14 = (f32[768,384]{1,0:T(8,128)S(1)}, f32[768,384]{1,0:T(8,128)S(1)}, u32[]{:S(2)}, u32[]{:S(2)}) collective-permute-start(f32[768,384]{1,0:T(8,128)S(1)} %get-tuple-element.34), channel_id=1, source_target_pairs={{0,8},{8,0},{16,24},{24,16},{32,40},{40,32},{48,56},{56,48},{64,72... | collective-permute-start | bytes 3538952 | tf_op jit(solution)/shard_map/ppermute | solution.py:44
  48.6 81.4 %collective-permute-start.18 = (f32[768,384]{1,0:T(8,128)S(1)}, f32[768,384]{1,0:T(8,128)S(1)}, u32[]{:S(2)}, u32[]{:S(2)}) collective-permute-start(f32[768,384]{1,0:T(8,128)S(1)} %add.83), channel_id=1, source_target_pairs={{0,32},{8,40},{16,48},{24,56},{32,0},{40,8},{48,16},{56,24},{64,96... | collective-permute-start | bytes 3538952 | tf_op jit(solution)/shard_map/ppermute | solution.py:44
  48.9 81.1 %collective-permute-start.20 = (f32[768,384]{1,0:T(8,128)S(1)}, f32[768,384]{1,0:T(8,128)S(1)}, u32[]{:S(2)}, u32[]{:S(2)}) collective-permute-start(f32[768,384]{1,0:T(8,128)S(1)} %add.84), channel_id=1, source_target_pairs={{0,48},{8,56},{16,32},{24,40},{32,16},{40,24},{48,0},{56,8},{64,11... | collective-permute-start | bytes 3538952 | tf_op jit(solution)/shard_map/ppermute | solution.py:44
  51.2 78.7 %collective-permute-start.16 = (f32[768,384]{1,0:T(8,128)S(1)}, f32[768,384]{1,0:T(8,128)S(1)}, u32[]{:S(2)}, u32[]{:S(2)}) collective-permute-start(f32[768,384]{1,0:T(8,128)S(1)} %add.82), channel_id=1, source_target_pairs={{0,16},{8,24},{16,0},{24,8},{32,48},{40,56},{48,32},{56,40},{64,80... | collective-permute-start | bytes 3538952 | tf_op jit(solution)/shard_map/ppermute | solution.py:44
  52.6 53.0 %collective-permute-start.8 = (f32[56,384]{1,0:T(8,128)S(1)}, f32[56,384]{1,0:T(8,128)S(1)}, u32[]{:S(2)}, u32[]{:S(2)}) collective-permute-start(f32[56,384]{1,0:T(8,128)S(1)} %get-tuple-element.32), channel_id=1, source_target_pairs={{0,48},{8,56},{16,32},{24,40},{32,16},{40,24},{48,0},{56,8},{64,11... | collective-permute-start | bytes 258056 | tf_op jit(solution)/shard_map/ppermute | solution.py:44
  105.6 6.3 %collective-permute-start.9 = (f32[56,384]{1,0:T(8,128)S(1)}, f32[56,384]{1,0:T(8,128)S(1)}, u32[]{:S(2)}, u32[]{:S(2)}) collective-permute-start(f32[56,384]{1,0:T(8,128)S(1)} %add_add_fusion), channel_id=1, source_target_pairs={{0,64},{8,72},{16,80},{24,88},{32,96},{40,104},{48,112},{56,120},{... | collective-permute-start | bytes 258056 | tf_op jit(solution)/shard_map/ppermute | solution.py:44
  111.9 4.6 %collective-permute-start.10 = (f32[56,384]{1,0:T(8,128)S(1)}, f32[56,384]{1,0:T(8,128)S(1)}, u32[]{:S(2)}, u32[]{:S(2)}) collective-permute-start(f32[56,384]{1,0:T(8,128)S(1)} %add.80.own_ref), channel_id=1, source_target_pairs={{0,16},{8,24},{16,0},{24,8},{32,48},{40,56},{48,32},{56,40},{64,80... | collective-permute-start | bytes 258056 | tf_op jit(solution)/shard_map/ppermute | solution.py:44
  116.5 6.0 %collective-permute-start.11 = (f32[56,384]{1,0:T(8,128)S(1)}, f32[56,384]{1,0:T(8,128)S(1)}, u32[]{:S(2)}, u32[]{:S(2)}) collective-permute-start(f32[56,384]{1,0:T(8,128)S(1)} %add.80.own_ref), channel_id=1, source_target_pairs={{0,32},{8,40},{16,48},{24,56},{32,0},{40,8},{48,16},{56,24},{64,96... | collective-permute-start | bytes 258056 | tf_op jit(solution)/shard_map/ppermute | solution.py:44
  122.5 5.7 %collective-permute-start.12 = (f32[56,384]{1,0:T(8,128)S(1)}, f32[56,384]{1,0:T(8,128)S(1)}, u32[]{:S(2)}, u32[]{:S(2)}) collective-permute-start(f32[56,384]{1,0:T(8,128)S(1)} %add.80.own_ref), channel_id=1, source_target_pairs={{0,48},{8,56},{16,32},{24,40},{32,16},{40,24},{48,0},{56,8},{64,11... | collective-permute-start | bytes 258056 | tf_op jit(solution)/shard_map/ppermute | solution.py:44
  133.6 11.6 %collective-permute-start.22 = (f32[208,384]{1,0:T(8,128)S(1)}, f32[208,384]{1,0:T(8,128)S(1)}, u32[]{:S(2)}, u32[]{:S(2)}) collective-permute-start(f32[208,384]{1,0:T(8,128)S(1)} %add.85.mine_ref), channel_id=1, source_target_pairs={{0,64},{8,72},{16,80},{24,88},{32,96},{40,104},{48,112},{56,120},{... | collective-permute-start | bytes 958472 | tf_op jit(solution)/shard_map/ppermute | solution.py:44
  145.5 10.9 %collective-permute-start.25 = (f32[208,384]{1,0:T(8,128)S(1)}, f32[208,384]{1,0:T(8,128)S(1)}, u32[]{:S(2)}, u32[]{:S(2)}) collective-permute-start(f32[208,384]{1,0:T(8,128)S(1)} %shard_map.56), channel_id=1, source_target_pairs={{0,48},{8,56},{16,32},{24,40},{32,16},{40,24},{48,0},{56,8},{64,11... | collective-permute-start | bytes 958472 | tf_op jit(solution)/shard_map/ppermute | solution.py:44
  145.7 10.7 %collective-permute-start.23 = (f32[208,384]{1,0:T(8,128)S(1)}, f32[208,384]{1,0:T(8,128)S(1)}, u32[]{:S(2)}, u32[]{:S(2)}) collective-permute-start(f32[208,384]{1,0:T(8,128)S(1)} %shard_map.56), channel_id=1, source_target_pairs={{0,16},{8,24},{16,0},{24,8},{32,48},{40,56},{48,32},{56,40},{64,80... | collective-permute-start | bytes 958472 | tf_op jit(solution)/shard_map/ppermute | solution.py:44
  145.7 18.2 %collective-permute-start.24 = (f32[208,384]{1,0:T(8,128)S(1)}, f32[208,384]{1,0:T(8,128)S(1)}, u32[]{:S(2)}, u32[]{:S(2)}) collective-permute-start(f32[208,384]{1,0:T(8,128)S(1)} %shard_map.56), channel_id=1, source_target_pairs={{0,32},{8,40},{16,48},{24,56},{32,0},{40,8},{48,16},{56,24},{64,96... | collective-permute-start | bytes 958472 | tf_op jit(solution)/shard_map/ppermute | solution.py:44
  164.0 3.1 %collective-permute-start.26 = (f32[4,208,384]{2,1,0:T(8,128)S(1)}, f32[4,208,384]{2,1,0:T(8,128)S(1)}, u32[]{:S(2)}, u32[]{:S(2)}) collective-permute-start(f32[4,208,384]{2,1,0:T(8,128)S(1)} %pad_maximum_fusion.own_ref), channel_id=1, source_target_pairs={{0,8},{8,0},{16,24},{24,16},{32,40},{40,32},{48,56},{56,48},{64,72... | collective-permute-start | bytes 3833864 | tf_op jit(solution)/shard_map/ppermute | solution.py:44
  191.4 4.7 %collective-permute-start.28 = (f32[80,128]{1,0:T(8,128)S(1)}, f32[80,128]{1,0:T(8,128)S(1)}, u32[]{:S(2)}, u32[]{:S(2)}) collective-permute-start(f32[80,128]{1,0:T(8,128)S(1)} %add.86), channel_id=1, source_target_pairs={{0,16},{8,24},{16,0},{24,8},{32,48},{40,56},{48,32},{56,40},{64,80... | collective-permute-start | bytes 122888 | tf_op jit(solution)/shard_map/ppermute | solution.py:44
  191.4 5.6 %collective-permute-start.29 = (f32[80,128]{1,0:T(8,128)S(1)}, f32[80,128]{1,0:T(8,128)S(1)}, u32[]{:S(2)}, u32[]{:S(2)}) collective-permute-start(f32[80,128]{1,0:T(8,128)S(1)} %add.86), channel_id=1, source_target_pairs={{0,32},{8,40},{16,48},{24,56},{32,0},{40,8},{48,16},{56,24},{64,96... | collective-permute-start | bytes 122888 | tf_op jit(solution)/shard_map/ppermute | solution.py:44
  193.3 5.2 %collective-permute-start.30 = (f32[80,128]{1,0:T(8,128)S(1)}, f32[80,128]{1,0:T(8,128)S(1)}, u32[]{:S(2)}, u32[]{:S(2)}) collective-permute-start(f32[80,128]{1,0:T(8,128)S(1)} %add.86), channel_id=1, source_target_pairs={{0,48},{8,56},{16,32},{24,40},{32,16},{40,24},{48,0},{56,8},{64,11... | collective-permute-start | bytes 122888 | tf_op jit(solution)/shard_map/ppermute | solution.py:44
  198.5 4.8 %collective-permute-start.31 = (f32[80,128]{1,0:T(8,128)S(1)}, f32[80,128]{1,0:T(8,128)S(1)}, u32[]{:S(2)}, u32[]{:S(2)}) collective-permute-start(f32[80,128]{1,0:T(8,128)S(1)} %add_add_fusion.4), channel_id=1, source_target_pairs={{0,1},{1,0},{2,3},{3,2},{4,5},{5,4},{6,7},{7,6},{8,9},{9,8},{10,11... | collective-permute-start | bytes 122888 | tf_op jit(solution)/shard_map/ppermute | solution.py:44
  199.4 5.5 %collective-permute-start.32 = (f32[80,128]{1,0:T(8,128)S(1)}, f32[80,128]{1,0:T(8,128)S(1)}, u32[]{:S(2)}, u32[]{:S(2)}) collective-permute-start(f32[80,128]{1,0:T(8,128)S(1)} %add_add_fusion.4), channel_id=1, source_target_pairs={{0,2},{1,3},{2,0},{3,1},{4,6},{5,7},{6,4},{7,5},{8,10},{9,11},{10,... | collective-permute-start | bytes 122888 | tf_op jit(solution)/shard_map/ppermute | solution.py:44
  201.3 5.2 %collective-permute-start.33 = (f32[80,128]{1,0:T(8,128)S(1)}, f32[80,128]{1,0:T(8,128)S(1)}, u32[]{:S(2)}, u32[]{:S(2)}) collective-permute-start(f32[80,128]{1,0:T(8,128)S(1)} %add_add_fusion.4), channel_id=1, source_target_pairs={{0,3},{1,2},{2,1},{3,0},{4,7},{5,6},{6,5},{7,4},{8,11},{9,10},{10,... | collective-permute-start | bytes 122888 | tf_op jit(solution)/shard_map/ppermute | solution.py:44
  206.6 4.8 %collective-permute-start.34 = (f32[80,128]{1,0:T(8,128)S(1)}, f32[80,128]{1,0:T(8,128)S(1)}, u32[]{:S(2)}, u32[]{:S(2)}) collective-permute-start(f32[80,128]{1,0:T(8,128)S(1)} %add_add_fusion.3), channel_id=1, source_target_pairs={{0,4},{1,5},{2,6},{3,7},{4,0},{5,1},{6,2},{7,3},{8,12},{9,13},{10,... | collective-permute-start | bytes 122888 | tf_op jit(solution)/shard_map/ppermute | solution.py:44
  207.4 6.0 %collective-permute-start.35 = (f32[80,128]{1,0:T(8,128)S(1)}, f32[80,128]{1,0:T(8,128)S(1)}, u32[]{:S(2)}, u32[]{:S(2)}) collective-permute-start(f32[80,128]{1,0:T(8,128)S(1)} %add_add_fusion.3), channel_id=1, source_target_pairs={{0,64},{1,65},{2,66},{3,67},{4,68},{5,69},{6,70},{7,71},{8,72},{9,... | collective-permute-start | bytes 122888 | tf_op jit(solution)/shard_map/ppermute | solution.py:44
  211.0 5.2 %collective-permute-start.36 = (f32[80,128]{1,0:T(8,128)S(1)}, f32[80,128]{1,0:T(8,128)S(1)}, u32[]{:S(2)}, u32[]{:S(2)}) collective-permute-start(f32[80,128]{1,0:T(8,128)S(1)} %add_add_fusion.3), channel_id=1, source_target_pairs={{0,68},{1,69},{2,70},{3,71},{4,64},{5,65},{6,66},{7,67},{8,76},{9,... | collective-permute-start | bytes 122888 | tf_op jit(solution)/shard_map/ppermute | solution.py:44
  (7 other events, 9.2 us)
